TPU v7x, 128 devices: a whole 4x4x4 slice. The times are simulated.
128 devices in a mesh: fx: 8 (over y, core), fy: 16 (over z, x).
Axes of the slice: x: 4, y: 4, z: 4, core: 2. Of those that a mesh axis runs over, the one named last changes fastest.
Arguments:
- tracers: float32 [64, 16, 32768], P(None, None, ('fx', 'fy')), may hold values from -6 to 6
- node_mass: float32 [16, 32768], P(None, ('fx', 'fy')), may hold values from 0.05 to 1
- point_order: int32 [2, 128, 4096], P(None, ('fx', 'fy')), may hold values from 0 to 4095, each once within a row
- offsets: int32 [2, 128, 10], P(None, ('fx', 'fy')), may hold values from 0 to 4096, as said below
- source: int32 [2, 524288], P(None, ('fx', 'fy')), may hold values from 0 to 255
- coords: int32 [2, 2, 524288], P(None, None, ('fx', 'fy')), may hold values from 0 to 1024
Outputs:
- transported: float32 [64, 16, 32768], P(None, None, ('fx', 'fy'))
Inputs may be any that keep to these rules, and one draw needn't show every extreme that they name: offsets[s, t, 0] = 0 and offsets[s, t, 9] = 4096, never falling; every run k other than 4 holds at least 32 and at most 128 positions, and on every tile in every substep some run holds exactly 128.
All inputs are finite; a program needn't handle non-finite values.
Results may differ from a plain program's by a relative error of at most 0.0003.
Values sent between devices are 32-bit elements; how exact they have to be, the bound alone decides.
No kernel may reach another device: no remote copies, remote signals or barrier semaphores. Data moves between devices by JAX's collectives and lax.ppermute only.
A program may use at most 128 MiB of HBM per device.

v0:
```python
import jax
import jax.numpy as jnp
from jax import lax
from jax.experimental import pallas as pl
from jax.experimental.pallas import tpu as pltpu
from jax.sharding import PartitionSpec as P

TX = 16
CAP = 128
QGRID = 1024
SUBSTEPS = 2
F = 64
E = 256
NODES = 16
POINTS = 4096
TILES = POINTS // 128
PIECES = (((0, 10), (10, 14), (14, 16)), ((0, 8), (8, 14), (14, 16)))
GLL_NODES = (-1.0, -0.4472135954999579, 0.4472135954999579, 1.0)
REMOTE = (0, 1, 2, 3, 5, 6, 7, 8)
BF16 = jnp.bfloat16
F32 = jnp.float32
VMEM_LIMIT = 40 * 2**20


def call(body, out_shape, name, hbm=(), count=0, after=0, scratch=()):
    specs = [
        pl.BlockSpec(memory_space=pltpu.HBM if i in hbm else pltpu.VMEM) for i in range(count)
    ] + [pl.BlockSpec(memory_space=pl.ANY)] * after

    def kernel(*refs):
        body(*refs[:count], *refs[count + after :])

    return pl.pallas_call(
        kernel,
        out_shape=out_shape,
        in_specs=specs,
        scratch_shapes=scratch,
        name=name,
        compiler_params=pltpu.CompilerParams(vmem_limit_bytes=VMEM_LIMIT),
    )


def in_hbm(array):
    return pltpu.with_memory_space_constraint(array, pltpu.HBM)


def shape(dims, dtype=F32):
    return jax.ShapeDtypeStruct(dims, dtype)


def swap_far(axis, block):
    size = lax.axis_size(axis)
    pairs = [(i, (((i + size - 1) % size ^ 1) + 1) % size) for i in range(size)]
    return lax.ppermute(block, axis, pairs)


def swap_near(axis, block):
    return lax.ppermute(block, axis, [(i, i ^ 1) for i in range(lax.axis_size(axis))])


def swap(axis, far, near):
    return swap_far(axis, far), swap_near(axis, near)


def to_swaps(axis, low, high):
    even = lax.axis_index(axis) % 2 == 0
    return jnp.where(even, low, high), jnp.where(even, high, low)


def from_swaps(axis, first, second):
    even = lax.axis_index(axis) % 2 == 0
    return jnp.where(even, first, second), jnp.where(even, second, first)


def lagrange(step):
    x = step * (2.0 / QGRID) - 1.0
    rows = []
    for a in range(4):
        factor = None
        for b in range(4):
            if b != a:
                term = (x - GLL_NODES[b]) * (1.0 / (GLL_NODES[a] - GLL_NODES[b]))
                factor = term if factor is None else factor * term
        rows.append(factor)
    return rows


def halves(block):
    high = block.astype(BF16)
    return high, (block - high.astype(F32)).astype(BF16)


def one_hot(index_rows, depth):
    rows = lax.broadcasted_iota(jnp.int32, (depth, 128), 0).astype(F32).astype(BF16)
    parts = [jnp.where(rows == r.astype(BF16), BF16(1), BF16(0)) for r in index_rows]
    return jnp.concatenate(parts, axis=1)


def lane_index(rows):
    return lax.broadcasted_iota(jnp.int32, (rows, 128), 1)


def eight(row):
    return jnp.broadcast_to(row, (8, row.shape[1]))


def pick_lanes(block, index):
    return jnp.take_along_axis(block, index, axis=1, mode="promise_in_bounds")


def faces(tile):
    rows = tile(0, 0).shape[0]
    lane = lane_index(rows)
    along_x = jnp.zeros((rows, 128), F32)
    for b in range(4):
        along_x = jnp.where(lane // 16 == b, pltpu.roll(tile(b, 0), b * 16, 1), along_x)
        shifted = pltpu.roll(tile(12 + b, 1), (b * 16 + 80) % 128, 1)
        along_x = jnp.where(lane // 16 == b + 4, shifted, along_x)
    along_y = jnp.zeros((rows, 128), F32)
    index = (lane % 8) * 16
    for a in range(4):
        for t in range(2):
            here = ((lane % 64) // 16 == a) & ((lane % 16) // 8 == t)
            first = pick_lanes(tile(4 * a, t), index)
            last = pick_lanes(tile(4 * a + 3, t), index + 15)
            along_y = jnp.where(here, jnp.where(lane < 64, first, last), along_y)
    return along_x, along_y


def summed_faces(own, low, high):
    lane = lane_index(own.shape[0])
    place = lane % 64
    behind = pltpu.roll(own, 128 - 48 + 1, 1)
    ahead = pltpu.roll(own, 48 - 1, 1)
    behind = jnp.where(lane == 0, low[:, 64:65], jnp.where(lane == 64, low[:, 127:128], behind))
    ahead = jnp.where(lane == 63, high[:, 0:1], jnp.where(lane == 127, high[:, 63:64], ahead))
    return own + jnp.where(place < 16, behind, jnp.where(place >= 48, ahead, 0.0))


def summed_nodes(nodes, low, high):
    rows = nodes[0].shape[0]
    lane = lane_index(rows)
    wide = lax.broadcasted_iota(jnp.int32, (rows, E), 1)
    nodes = list(nodes)
    for b in range(4):
        first, last = nodes[b], nodes[12 + b]
        behind = pltpu.roll(last, 16, 1)
        ahead = pltpu.roll(first, E - 16, 1)
        from_low = pltpu.roll(low, (128 - 64 - 16 * b) % 128, 1)
        from_high = pltpu.roll(high, 112 - 16 * b, 1)
        behind = jnp.concatenate(
            [jnp.where(lane < 16, from_low, behind[:, :128]), behind[:, 128:]], axis=1
        )
        ahead = jnp.concatenate(
            [ahead[:, :128], jnp.where(lane >= 112, from_high, ahead[:, 128:])], axis=1
        )
        nodes[b] = first + behind
        nodes[12 + b] = last + ahead
    for a in range(4):
        first, last = nodes[4 * a], nodes[4 * a + 3]
        behind = jnp.where(wide % 16 == 0, 0.0, pltpu.roll(last, 1, 1))
        ahead = jnp.where(wide % 16 == 15, 0.0, pltpu.roll(first, E - 1, 1))
        nodes[4 * a] = first + behind
        nodes[4 * a + 3] = last + ahead
    return nodes


def halo_of(low, high):
    lane = lane_index(low.shape[0])
    return pltpu.roll(jnp.where(lane >= 64, low, high), 64, 1)


def with_halo(n, node, halo):
    if n % 4 not in (0, 3):
        return node
    rows = node.shape[0]
    lane = lane_index(rows)
    wide = lax.broadcasted_iota(jnp.int32, (rows, E), 1)
    start = 16 * (n // 4) + (64 if n % 4 == 3 else 0)
    spread = [pick_lanes(halo, start + 8 * t + lane // 16) for t in range(2)]
    at = 15 if n % 4 == 3 else 0
    return node + jnp.where(wide % 16 == at, jnp.concatenate(spread, axis=1), 0.0)


def fetch(pairs, sems):
    copies = [pltpu.make_async_copy(*pair, sems.at[i]) for i, pair in enumerate(pairs)]
    for copy in copies:
        copy.start()
    for copy in copies:
        copy.wait()


def asks_body(
    offsets_in, source_in, coords_in, mass_in, first, second, mid, mass_faces,
    offsets, source, coords, mass, rows, message, sems,
):
    fetch(
        [(offsets_in, offsets), (source_in, source), (coords_in, coords), (mass_in, mass)], sems
    )
    for s in range(SUBSTEPS):
        rows[3 * s : 3 * s + 1, :] = source[s : s + 1, :].astype(F32)
        rows[3 * s + 1 : 3 * s + 3, :] = coords[s].astype(F32)
    rows[6:8, :] = jnp.zeros((2, POINTS), F32)
    early = lax.broadcasted_iota(jnp.int32, (8, 128), 0) < 3
    for k in REMOTE:
        parts = []
        for s in range(SUBSTEPS):
            start = offsets[s, 0, k]
            tile = jnp.minimum(start // 128, TILES - 1)
            after = jnp.minimum(tile + 1, TILES - 1)
            wide = jnp.concatenate(
                [rows[:, pl.ds(pl.multiple_of(t * 128, 128), 128)] for t in (tile, after)], axis=1
            )
            parts.append(pltpu.roll(wide, 256 - (start - tile * 128), 1)[:, 0:128])
        message[k * 8 : (k + 1) * 8, :] = jnp.where(early, parts[0], parts[1])
    along_x, along_y = faces(lambda n, t: eight(mass[n : n + 1, t * 128 : (t + 1) * 128]))
    for k in (1, 7):
        message[k * 8 + 6 : k * 8 + 7, :] = along_x[0:1]
    mass_faces[:, 0:128] = along_x
    mass_faces[:, 128:256] = along_y
    message[32:40, :] = jnp.zeros((8, 128), F32)
    first[...], second[...] = to_swaps("fx", message[0:24, :], message[48:72, :])
    mid[...] = message[24:48, :]


def order_body(
    s, offsets_in, order_in, source_in, coords_in, picks, factors, face_picks,
    offsets, order, source, coords, sems,
):
    fetch(
        [(offsets_in, offsets), (order_in, order), (source_in, source), (coords_in, coords)], sems
    )
    chunk = 1024
    total = None
    for c in range(POINTS // chunk):
        lanes = slice(c * chunk, (c + 1) * chunk)
        node = order[s, :, lanes]
        tile_of = (node // 128).astype(F32).astype(BF16)
        lane_of = (node % 128).astype(F32).astype(BF16)
        position = lax.broadcasted_iota(jnp.int32, (1, chunk), 1) + c * chunk
        run = jnp.zeros((1, chunk), jnp.int32)
        begin = jnp.zeros((1, chunk), jnp.int32) + offsets[s, 0, 0]
        for k in range(1, 9):
            passed = position >= offsets[s, 0, k]
            run = run + passed.astype(jnp.int32)
            begin = jnp.where(passed, offsets[s, 0, k], begin)
        own = run == 4
        kind = jnp.where(own, 8, jnp.where(run > 4, run - 1, run))
        pick = jnp.where(own, source[s : s + 1, lanes], position - begin)
        cx = coords[s, 0:1, lanes]
        cy = coords[s, 1:2, lanes]
        values = [pick, cx // 8, cx % 8, cy // 8, cy % 8, kind]
        tiles = lax.broadcasted_iota(jnp.int32, (TILES, chunk), 0).astype(F32).astype(BF16)
        here = tiles == tile_of
        left = jnp.concatenate(
            [jnp.where(here, v.astype(F32).astype(BF16), BF16(0)) for v in values], axis=0
        )
        spots = lax.broadcasted_iota(jnp.int32, (128, chunk), 0).astype(F32).astype(BF16)
        right = jnp.where(spots == lane_of, BF16(1), BF16(0))
        part = lax.dot_general(left, right, (((1,), (1,)), ((), ())), preferred_element_type=F32)
        total = part if total is None else total + part
    pick, xh, xl, yh, yl, kind = [total[q * TILES : (q + 1) * TILES] for q in range(6)]
    own = kind > 7.5
    picks[0] = jnp.where(own, pick, -1.0)
    picks[1] = jnp.where(own, -1.0, pick)
    mask = jnp.where(own, 1.0, 0.0)
    along_x = [row * mask for row in lagrange(xh * 8.0 + xl)]
    along_y = lagrange(yh * 8.0 + yl)
    for n in range(NODES):
        factors[n] = along_x[n // 4] * along_y[n % 4]
    for d in range(8):
        factors[NODES + d] = jnp.where(jnp.abs(kind - d) < 0.5, 1.0, 0.0)
    for q, rows in enumerate((picks[1], kind, picks[0], xh * 8.0 + xl, yh * 8.0 + yl)):
        along = faces(lambda n, t: eight(rows[2 * n + t : 2 * n + t + 1]))
        face_picks[q : q + 1, :] = jnp.concatenate(along, axis=1)[0:1]


def table_body(tracers_in, table, tracers, sems):
    fetch([(tracers_in, tracers)], sems)
    for q in range(0, F, 16):
        block = jnp.swapaxes(tracers[q : q + 16], 0, 1)
        for n in range(NODES):
            high, low = halves(block[n])
            table[n * F + q : n * F + q + 16, 0:E] = high
            table[n * F + q : n * F + q + 16, E : 2 * E] = low


def column_body(x_first, x_second, mid, mass_faces, first, second):
    low, high = from_swaps("fx", x_first[...], x_second[...])
    masses = summed_faces(mass_faces[:, 128:256], low[8:16], high[8:16])[6:7]
    rows = lax.broadcasted_iota(jnp.int32, (8, 128), 0)
    columns = []
    for k in (0, 2):
        block = slice(k * 8, (k + 1) * 8)
        center = jnp.where(rows == 6, masses, mid[block, :])
        columns.append(jnp.concatenate([high[block], center, low[block]], axis=0))
    first[...], second[...] = to_swaps("fy", *columns)


def row_body(y_first, y_second, own, far, near):
    low, high = from_swaps("fy", y_first[...], y_second[...])
    mine = own[...]
    ahead = jnp.concatenate([low[0:F], mine[0:F], high[0:F]], axis=0)
    behind = jnp.concatenate([low[2 * F :], mine[F:], high[2 * F :]], axis=0)
    far[...], near[...] = to_swaps("fx", behind, ahead)


def combine(products, weights):
    total = None
    for n, weight in enumerate(weights):
        term = products[n * F : (n + 1) * F] * weight
        total = term if total is None else total + term
    return total


def asked_blocks(x_first, x_second, y_first, y_second):
    x_low, x_high = from_swaps("fx", x_first[...], x_second[...])
    y_low, y_high = from_swaps("fy", y_first[...], y_second[...])
    by_direction = {(1, 0): x_low[8:16], (-1, 0): x_high[8:16]}
    for k in range(3):
        by_direction[(k - 1, 1)] = y_low[k * 8 : (k + 1) * 8]
        by_direction[(k - 1, -1)] = y_high[k * 8 : (k + 1) * 8]
    return [by_direction[(k // 3 - 1, k % 3 - 1)] for k in REMOTE]


def asked_rows(s, asked):
    return [
        jnp.concatenate([r[s * 3 + q : s * 3 + q + 1, :] for r in asked], axis=0) for q in range(3)
    ]


def weights_of(cx, cy):
    along_x = lagrange(cx)
    along_y = lagrange(cy)
    return [along_x[n // 4] * along_y[n % 4] for n in range(NODES)]


def answer(table, pick, weights, directions):
    values = {}
    for both in directions:
        hot = one_hot([pick[d : d + 1] for d in both], E)
        products = jnp.dot(
            table[...], jnp.concatenate([hot, hot], axis=0), preferred_element_type=F32
        )
        for h, d in enumerate(both):
            lanes = slice(h * 128, (h + 1) * 128)
            values[d] = combine(products[:, lanes], [w[d : d + 1] for w in weights])
    return values


BEHIND = (2, 4, 7)
AHEAD = (0, 3, 5)
SIDES = (1, 6)


def sides_first(rows):
    even = lax.axis_index("fy") % 2 == 0
    pairs = [(rows[b : b + 1], rows[a : a + 1]) for b, a in zip(BEHIND, AHEAD)]
    far = [jnp.where(even, behind, ahead) for behind, ahead in pairs]
    near = [jnp.where(even, ahead, behind) for behind, ahead in pairs]
    return jnp.concatenate(far + near + [rows[0:2]], axis=0)


def reply_y_body(table, x_first, x_second, y_first, y_second, far, near):
    rows = asked_rows(0, asked_blocks(x_first, x_second, y_first, y_second))
    pick, cx, cy = [sides_first(block) for block in rows]
    values = answer(table, pick, weights_of(cx, cy), ((0, 1), (2, 3), (4, 5)))
    for k in range(3):
        far[k * F : (k + 1) * F, :] = values[k]
        near[k * F : (k + 1) * F, :] = values[3 + k]


def reply_x_body(s, table, x_first, x_second, y_first, y_second, own):
    pick, cx, cy = asked_rows(s, asked_blocks(x_first, x_second, y_first, y_second))
    values = answer(table, pick, weights_of(cx, cy), (SIDES,))
    for k, d in enumerate(SIDES):
        own[k * F : (k + 1) * F, :] = values[d]


def early_body(s, table, x_first, x_second, y_first, y_second, values, lanes, shares):
    rows = asked_rows(s, asked_blocks(x_first, x_second, y_first, y_second))
    pick, cx, cy = [sides_first(block) for block in rows]
    weights = weights_of(cx, cy)
    found = answer(table, pick, weights, ((0, 1), (2, 3), (4, 5)))
    for d, value in found.items():
        values[d] = value
    element = pick.astype(jnp.int32)
    lanes[...] = element // 16 + jnp.where(element % 16 == 15, 64, 0)
    for a in range(4):
        share = jnp.where(element % 16 == 15, weights[4 * a + 3], 0.0)
        shares[a] = jnp.where(element % 16 == 0, weights[4 * a], share)


def late_body(values, lanes, shares, y_first, y_second, scale, far, near):
    halo = halo_of(*from_swaps("fy", y_first[...], y_second[...])) * scale[0:1, :]
    for d in range(6):
        index = jnp.broadcast_to(lanes[d : d + 1, :], (F, 128))
        value = values[d]
        for a in range(4):
            value = value + pick_lanes(halo, index + 16 * a) * shares[a, d : d + 1, :]
        (far if d < 3 else near)[d % 3 * F : (d % 3 + 1) * F, :] = value


def own_body(begin, table, picks, factors, result):
    def block(i, carry):
        at = 2 * (begin + i)
        hot = one_hot([picks[0, pl.ds(at + h, 1), :] for h in range(2)], E)
        products = jnp.dot(
            table[...], jnp.concatenate([hot, hot], axis=0), preferred_element_type=F32
        )
        weights = [
            jnp.concatenate([factors[n, pl.ds(at + h, 1), :] for h in range(2)], axis=1)
            for n in range(NODES)
        ]
        result[:, pl.ds(pl.multiple_of(i * E, E), E)] = combine(products, weights)
        return carry

    count = result.shape[1] // E
    lax.fori_loop(0, count, block, 0, unroll=5 if count == 10 else 4 if count == 8 else 3 if count == 6 else count)


def stacked(blocks):
    return jnp.concatenate([jnp.concatenate(halves(block), axis=1) for block in blocks], axis=0)


def three(ref):
    return [ref[k * F : (k + 1) * F, :] for k in range(3)]


def middles(y_first, y_second):
    return list(from_swaps("fy", y_first[F : 2 * F, :], y_second[F : 2 * F, :]))


def arrived(x_first, x_second, y_first, y_second):
    even = lax.axis_index("fx") % 2 == 0
    pairs = list(zip(three(x_first), three(x_second)))
    low = [jnp.where(even, far, near) for far, near in pairs]
    high = [jnp.where(even, near, far) for far, near in pairs]
    return stacked(low + middles(y_first, y_second) + high)


def placed(answers, slots, masks):
    hot = one_hot(slots, CAP)
    products = jnp.dot(answers, jnp.concatenate([hot, hot], axis=0), preferred_element_type=F32)
    return combine(products, masks)


def masks_of(kind, bases):
    return [jnp.where(jnp.abs(kind - base) < 0.5, 1.0, 0.0) for base in bases]


def kinds(even, near):
    start = jnp.where(even == near, 5.0, 0.0)
    return [start + k for k in range(3)]


def face_slots(face_picks):
    return [face_picks[0:1, h * 128 : (h + 1) * 128] for h in range(2)]


def own_faces_body(table, face_picks, result):
    hot = one_hot([face_picks[2:3, h * 128 : (h + 1) * 128] for h in range(2)], E)
    products = jnp.dot(table[...], jnp.concatenate([hot, hot], axis=0), preferred_element_type=F32)
    result[...] = combine(products, weights_of(face_picks[3:4, :], face_picks[4:5, :]))


def face_near_body(
    own, near, far, y_first, y_second, face_picks, mass_faces, partial, message
):
    even = lax.axis_index("fx") % 2 == 0
    masks = masks_of(face_picks[1:2, :], kinds(even, True) + [3.0, 4.0])
    answers = stacked(three(near) + middles(y_first, y_second))
    moved = own[...] + placed(answers, face_slots(face_picks), masks)
    moved = moved * mass_faces[0:1, :]
    partial[...] = moved
    message[0 : 3 * F, :] = far[...]
    message[3 * F : 4 * F, :] = moved[:, 0:128]
    message[4 * F : 4 * F + 8, :] = face_picks[:, 0:128]
    message[4 * F + 2 : 4 * F + 3, :] = mass_faces[0:1, 0:128]


def face_far_body(partial, far, sent, face_picks, mass_faces, along_x, along_y, other):
    even = lax.axis_index("fx") % 2 == 0
    masks = masks_of(face_picks[1:2, :], kinds(even, False))
    moved = placed(stacked(three(far)), face_slots(face_picks), masks) * mass_faces[0:1, :]
    result = partial[...] + moved
    along_x[...] = result[:, 0:128]
    along_y[...] = result[:, 128:256]
    slot, kind, weight = [far[4 * F + q : 4 * F + q + 1, :] for q in range(3)]
    moved = placed(stacked(three(sent)), [slot], masks_of(kind, kinds(even, True)))
    other[...] = far[3 * F : 4 * F, :] + moved * weight


def place_body(
    s, own_a, own_b, own_c, x_first, x_second, y_first, y_second, picks, factors, mass, result
):
    answers = arrived(x_first, x_second, y_first, y_second)
    for n in range(NODES):
        tiles = [slice(2 * n + h, 2 * n + h + 1) for h in range(2)]
        masks = [
            jnp.concatenate([factors[NODES + d, t, :] for t in tiles], axis=1) for d in range(8)
        ]
        moved = placed(answers, [picks[1, t, :] for t in tiles], masks)
        for ref, (begin, end) in zip((own_a, own_b, own_c), PIECES[s]):
            if begin <= n < end:
                own = ref[:, (n - begin) * E : (n - begin + 1) * E]
        result[:, n * E : (n + 1) * E] = (own + moved) * mass[n : n + 1, :]


def rim_body(along_y, x_first, x_second, first, second):
    low, high = from_swaps("fx", x_first[...], x_second[...])
    result = summed_faces(along_y[...], low, high)
    first[...] = result
    second[...] = result


def scale_body(mass, x_first, x_second, y_first, y_second, inverse, on_faces):
    x_low, x_high = from_swaps("fx", x_first[8:16, :], x_second[8:16, :])
    y_low, y_high = from_swaps("fy", y_first[8:16, :], y_second[8:16, :])
    low, high, halo = [
        eight(row[6:7]) for row in (x_low, x_high, halo_of(y_low, y_high))
    ]
    nodes = [eight(mass[n : n + 1, :]) for n in range(NODES)]
    nodes = summed_nodes(nodes, low, high)
    nodes = [1.0 / with_halo(n, node, halo) for n, node in enumerate(nodes)]
    for n in range(NODES):
        inverse[n : n + 1, :] = nodes[n][0:1]
    on_faces[...] = faces(lambda n, t: nodes[n][:, t * 128 : (t + 1) * 128])[1]


def sum_body(weighted, x_first, x_second, inverse, result, table=None):
    low, high = from_swaps("fx", x_first[...], x_second[...])
    nodes = summed_nodes([weighted[:, n * E : (n + 1) * E] for n in range(NODES)], low, high)
    for n in range(NODES):
        node = nodes[n] * inverse[n : n + 1, :]
        result[:, n * E : (n + 1) * E] = node
        if table is not None:
            high_part, low_part = halves(node)
            table[n * F : (n + 1) * F, 0:E] = high_part
            table[n * F : (n + 1) * F, E : 2 * E] = low_part


def finish_body(summed, y_first, y_second, scale, table):
    halo = halo_of(*from_swaps("fy", y_first[...], y_second[...])) * scale[0:1, :]
    for n in range(NODES):
        node = with_halo(n, summed[:, n * E : (n + 1) * E], halo)
        high, low = halves(node)
        table[n * F : (n + 1) * F, 0:E] = high
        table[n * F : (n + 1) * F, E : 2 * E] = low


def last_body(summed, y_first, y_second, scale, result, block, sems):
    halo = halo_of(*from_swaps("fy", y_first[...], y_second[...])) * scale[0:1, :]
    copies = []
    for i in range(F // 8):
        rows = slice(i * 8, (i + 1) * 8)
        nodes = [
            with_halo(n, summed[rows, n * E : (n + 1) * E], halo[rows]) for n in range(NODES)
        ]
        block[rows] = jnp.swapaxes(jnp.stack(nodes), 0, 1)
        copy = pltpu.make_async_copy(block.at[rows], result.at[rows], sems.at[i])
        copy.start()
        copies.append(copy)
    for copy in copies:
        copy.wait()


def per_device(tracers, node_mass, point_order, offsets, source, coords):
    ask = shape((24, 128))
    answers = shape((3 * F, 128))
    face = shape((F, 128))
    table_shape = shape((NODES * F, 2 * E), BF16)
    lists = [
        pltpu.SMEM(offsets.shape, jnp.int32),
        pltpu.VMEM(source.shape, jnp.int32),
        pltpu.VMEM(coords.shape, jnp.int32),
    ]
    first, second, mid, mass_faces = call(
        asks_body,
        [ask, ask, ask, shape((8, 256))],
        "asks",
        hbm=(0, 1, 2, 3),
        count=4,
        scratch=lists
        + [
            pltpu.VMEM(node_mass.shape, F32),
            pltpu.VMEM((8, POINTS), F32),
            pltpu.VMEM((72, 128), F32),
            pltpu.SemaphoreType.DMA((4,)),
        ],
    )(*[in_hbm(a) for a in (offsets, source, coords, node_mass)])
    asked = swap("fx", first, second)
    lists_in = [in_hbm(a) for a in (offsets, point_order, source, coords)]

    def requests(s, after=0):
        return call(
            lambda *refs: order_body(s, *refs),
            [shape((2, TILES, 128)), shape((NODES + 8, TILES, 128)), shape((8, 256))],
            "order",
            hbm=(0, 1, 2, 3),
            count=4,
            after=after,
            scratch=lists[:1]
            + [pltpu.VMEM(point_order.shape, jnp.int32)]
            + lists[1:]
            + [pltpu.SemaphoreType.DMA((4,))],
        )

    def interpolate(s, piece, after=0):
        begin, end = PIECES[s][piece]
        return call(
            lambda *refs: own_body(begin, *refs),
            shape((F, (end - begin) * E)),
            "own",
            count=3,
            after=after,
        )

    ordered = [requests(0)(*lists_in)]
    asked += swap(
        "fy",
        *call(column_body, [ask] * 2, "column", count=4)(*asked, mid, mass_faces),
    )
    table = call(
        table_body,
        table_shape,
        "table",
        hbm=(0,),
        count=1,
        scratch=[pltpu.VMEM(tracers.shape, F32), pltpu.SemaphoreType.DMA((1,))],
    )(in_hbm(tracers))
    far, near = call(reply_y_body, [answers] * 2, "reply_y", count=5, after=1)(
        table, *asked, ordered[0][2]
    )
    answers_y = swap("fy", far, near)
    inverse, scale = call(scale_body, [shape((NODES, E)), shape((8, 128))], "scale", count=5)(
        node_mass, *asked
    )
    for s in range(SUBSTEPS):
        picks, factors, face_picks = ordered[s]
        if s == 1:
            table = call(finish_body, table_shape, "finish", count=4)(summed, *edges_y, scale)
        own = call(
            lambda *refs, s=s: reply_x_body(s, *refs), shape((2 * F, 128)), "reply_x", count=5
        )(table, *asked)
        own_faces = call(own_faces_body, shape((F, 256)), "own_faces", count=2)(table, face_picks)
        own_a = interpolate(s, 0)(table, picks, factors)
        far, near = call(row_body, [answers] * 2, "row", count=3, after=3)(
            *answers_y, own, own_a, scale, own_faces
        )
        near = swap_near("fx", near)
        partial, message = call(
            face_near_body, [shape((F, 256)), shape((4 * F + 8, 128))], "faces_near", count=7
        )(own_faces, near, far, *answers_y, face_picks, mass_faces)
        far = swap_far("fx", message)
        own_b = interpolate(s, 1, after=1)(table, picks, factors, partial)
        if s == 0:
            ordered.append(requests(1, after=1)(*lists_in, partial))
        along_x, along_y, other = call(
            face_far_body, [face] * 3, "faces_far", count=5, after=2
        )(partial, far, message, face_picks, mass_faces, own_b, ordered[1][2])
        edges_x = (other, swap_near("fx", along_x))
        first, second = call(rim_body, [face] * 2, "rim", count=3)(along_y, *edges_x)
        edges_y = swap("fy", first, second)
        own_c = interpolate(s, 2, after=1)(table, picks, factors, second)
        weighted = call(
            lambda *refs, s=s: place_body(s, *refs), shape((F, POINTS)), "place", count=10
        )(
            own_a, own_b, own_c, far, near, *answers_y, picks, factors, node_mass
        )
        if s == 0:
            summed, early_table = call(
                sum_body, [shape((F, POINTS)), table_shape], "sum", count=4
            )(weighted, *edges_x, inverse)
            early = call(
                lambda *refs: early_body(1, *refs),
                [shape((8, F, 128)), shape((8, 128), jnp.int32), shape((4, 8, 128))],
                "early",
                count=5,
            )(early_table, *asked)
            far, near = call(late_body, [answers] * 2, "late", count=6)(
                *early, *edges_y, scale
            )
            answers_y = swap("fy", far, near)
        else:
            summed = call(sum_body, shape((F, POINTS)), "sum", count=4)(
                weighted, *edges_x, inverse
            )
            result = pl.pallas_call(
                last_body,
                out_shape=shape((F, NODES, E)),
                in_specs=[pl.BlockSpec(memory_space=pltpu.VMEM)] * 4,
                out_specs=pl.BlockSpec(memory_space=pltpu.HBM),
                scratch_shapes=[
                    pltpu.VMEM((F, NODES, E), F32),
                    pltpu.SemaphoreType.DMA((F // 8,)),
                ],
                name="last",
                compiler_params=pltpu.CompilerParams(vmem_limit_bytes=VMEM_LIMIT),
            )(summed, *edges_y, scale)
    return result


def solution(mesh):
    return jax.shard_map(
        per_device,
        mesh=mesh,
        in_specs=(
            P(None, None, ("fx", "fy")),
            P(None, ("fx", "fy")),
            P(None, ("fx", "fy"), None),
            P(None, ("fx", "fy"), None),
            P(None, ("fx", "fy")),
            P(None, None, ("fx", "fy")),
        ),
        out_specs=P(None, None, ("fx", "fy")),
        check_vma=False,
    )
```

profile of v0, /device:TPU:0, one launch (start us, length us, event | category | flops | bytes accessed | tf_op | source)
XLA Modules:
  0.0 67.3 jit_solution(2102116687837555368)
XLA Ops:
  0.0 1.2 %asks.1 = (f32[24,128]{1,0:T(8,128)S(1)}, f32[24,128]{1,0:T(8,128)S(1)}, f32[24,128]{1,0:T(8,128)S(1)}, f32[8,256]{1,0:T(8,128)S(1)}) custom-call(s32[2,1,10]{2,1,0:T(1,128)} %refs_0_.9, s32[2,4096]{1,0:T(2,128)} %refs_2_.5, s32[2,2,4096]{2,1,0:T(2,128)} %refs_3_.5, f32[16,256]{1,0:T(8,128)} %refs_9_.3), custom_call_target="tpu_custom_call" | custom-call | tf_op jit(solution)/shard_map/asks/pallas_call | solution.py:578
  1.2 2.6 %collective-permute-start = (f32[24,128]{1,0:T(8,128)S(1)}, f32[24,128]{1,0:T(8,128)S(1)}, u32[]{:S(2)}, u32[]{:S(2)}) collective-permute-start(f32[24,128]{1,0:T(8,128)S(1)} %get-tuple-element.49), channel_id=1, source_target_pairs={{0,112},{16,32},{32,16},{48,64},{64,48},{80,96},{96,80},{112,0},{1... | collective-permute-start | bytes 36872 | tf_op jit(solution)/shard_map/ppermute | solution.py:54
  3.8 1.8 %collective-permute-done.refs_0_.refs_1_ = f32[24,128]{1,0:T(8,128)S(1)} collective-permute-done((f32[24,128]{1,0:T(8,128)S(1)}, f32[24,128]{1,0:T(8,128)S(1)}, u32[]{:S(2)}, u32[]{:S(2)}) %collective-permute-start) | collective-permute-done | bytes 12320 | tf_op jit(solution)/shard_map/ppermute | solution.py:54
  5.7 6.4 %collective-permute-start.2 = (f32[24,128]{1,0:T(8,128)S(1)}, f32[24,128]{1,0:T(8,128)S(1)}, u32[]{:S(2)}, u32[]{:S(2)}) collective-permute-start(f32[24,128]{1,0:T(8,128)S(1)} %get-tuple-element.53), channel_id=1, source_target_pairs={{0,15},{1,2},{2,1},{3,4},{4,3},{5,6},{6,5},{7,8},{8,7},{9,10},{10,... | collective-permute-start | bytes 36872 | tf_op jit(solution)/shard_map/ppermute | solution.py:54
  12.0 1.9 %order.2 = (f32[2,32,128]{2,1,0:T(8,128)S(1)}, f32[24,32,128]{2,1,0:T(8,128)S(1)}, f32[8,256]{1,0:T(8,128)S(1)}) custom-call(s32[2,1,10]{2,1,0:T(1,128)} %refs_0_.9, s32[2,1,4096]{2,1,0:T(1,128)} %refs_1_.5, s32[2,4096]{1,0:T(2,128)} %refs_2_.5, s32[2,2,4096]{2,1,0:T(2,128)} %refs_3_.5), custom_call_target="tpu_custom_call" | custom-call | tf_op jit(solution)/shard_map/order/pallas_call | solution.py:619
  13.9 1.5 %table.1.refs_0_ = bf16[1024,512]{1,0:T(8,128)(2,1)S(1)} custom-call(f32[64,16,256]{2,1,0:T(8,128)} %refs_0_.5), custom_call_target="tpu_custom_call" | custom-call | tf_op jit(solution)/shard_map/table/pallas_call | solution.py:624
  15.5 0.2 collective-permute-done.3.refs_4_
  15.7 1.0 %reply_y.1 = (f32[192,128]{1,0:T(8,128)S(1)}, f32[192,128]{1,0:T(8,128)S(1)}) custom-call(bf16[1024,512]{1,0:T(8,128)(2,1)S(1)} %table.1.refs_0_, f32[24,128]{1,0:T(8,128)S(1)} %collective-permute-done.refs_0_.refs_1_, f32[24,128]{1,0:T(8,128)S(1)} %collective-permute-done.1.refs_1_.refs_2_, f32[24,128]{1,0:T(8,128)S(1)} %collective-permute-done.2.refs_3_, ...), custom_call_target="tpu_custom_call" | custom-call | tf_op jit(solution)/shard_map/reply_y/pallas_call | solution.py:632
  16.7 3.4 %collective-permute-start.4 = (f32[192,128]{1,0:T(8,128)S(1)}, f32[192,128]{1,0:T(8,128)S(1)}, u32[]{:S(2)}, u32[]{:S(2)}) collective-permute-start(f32[192,128]{1,0:T(8,128)S(1)} %get-tuple-element.55), channel_id=1, source_target_pairs={{0,15},{1,2},{2,1},{3,4},{4,3},{5,6},{6,5},{7,8},{8,7},{9,10},{10,... | collective-permute-start | bytes 294920 | tf_op jit(solution)/shard_map/ppermute | solution.py:54
  20.1 0.4 own_faces.2.refs_5_.refs_0_
  20.6 3.1 %own.6.refs_3_.refs_0_ = f32[64,2560]{1,0:T(8,128)S(1)} custom-call(bf16[1024,512]{1,0:T(8,128)(2,1)S(1)} %table.1.refs_0_, f32[2,32,128]{2,1,0:T(8,128)S(1)} %get-tuple-element.46.refs_1_.refs_7_, f32[24,32,128]{2,1,0:T(8,128)S(1)} %get-tuple-element.47.refs_2_.refs_8_), custom_call_target="tpu_custom_call" | custom-call | tf_op jit(solution)/shard_map/own/pallas_call | solution.py:647
  23.7 0.3 scale.1
  24.0 0.5 reply_x.2.refs_2_
  24.4 0.3 collective-permute-done.4.refs_0_.refs_3_.refs_5_
  24.9 1.3 %collective-permute-done.6.refs_1_.refs_4_ = f32[192,128]{1,0:T(8,128)S(1)} collective-permute-done((f32[192,128]{1,0:T(8,128)S(1)}, f32[192,128]{1,0:T(8,128)S(1)}, u32[]{:S(2)}, u32[]{:S(2)}) %collective-permute-start.6) | collective-permute-done | bytes 98336 | tf_op jit(solution)/shard_map/ppermute | solution.py:58
  26.2 0.2 faces_near.2
  26.4 2.3 %collective-permute-start.7 = (f32[264,128]{1,0:T(8,128)S(1)}, f32[264,128]{1,0:T(8,128)S(1)}, u32[]{:S(2)}, u32[]{:S(2)}) collective-permute-start(f32[264,128]{1,0:T(8,128)S(1)} %get-tuple-element.61.refs_2_), channel_id=1, source_target_pairs={{0,112},{16,32},{32,16},{48,64},{64,48},{80,96},{96,80},{112,0},{1... | collective-permute-start | bytes 405512 | tf_op jit(solution)/shard_map/ppermute | solution.py:54
  28.7 1.3 %own.7.refs_5_.refs_1_ = f32[64,1024]{1,0:T(8,128)S(1)} custom-call(bf16[1024,512]{1,0:T(8,128)(2,1)S(1)} %table.1.refs_0_, f32[2,32,128]{2,1,0:T(8,128)S(1)} %get-tuple-element.46.refs_1_.refs_7_, f32[24,32,128]{2,1,0:T(8,128)S(1)} %get-tuple-element.47.refs_2_.refs_8_, f32[64,256]{1,0:T(8,128)S(1)} %get-tuple-element.60.refs_3_.refs_4_.refs_0_), custom_call_target="tpu_custom_call" | custom-call | tf_op jit(solution)/shard_map/own/pallas_call | solution.py:656
  29.9 1.9 %order.3 = (f32[2,32,128]{2,1,0:T(8,128)S(1)}, f32[24,32,128]{2,1,0:T(8,128)S(1)}, f32[8,256]{1,0:T(8,128)S(1)}) custom-call(s32[2,1,10]{2,1,0:T(1,128)} %refs_0_.9, s32[2,1,4096]{2,1,0:T(1,128)} %refs_1_.5, s32[2,4096]{1,0:T(2,128)} %refs_2_.5, s32[2,2,4096]{2,1,0:T(2,128)} %refs_3_.5, f32[64,256]{1,0:T(8,128)S(1)} %get-tuple-element.60.refs_3_.refs_4_.refs_0_), custom_call_target="tpu_custom_call" | custom-call | tf_op jit(solution)/shard_map/order/pallas_call | solution.py:658
  31.8 0.3 collective-permute-done.7.refs_1_.refs_3_
  32.1 0.2 faces_far.2
  32.4 1.2 %collective-permute-done.8.refs_2_ = f32[64,128]{1,0:T(8,128)S(1)} collective-permute-done((f32[64,128]{1,0:T(8,128)S(1)}, f32[64,128]{1,0:T(8,128)S(1)}, u32[]{:S(2)}, u32[]{:S(2)}) %collective-permute-start.8) | collective-permute-done | bytes 32800 | tf_op jit(solution)/shard_map/ppermute | solution.py:58
  33.8 3.4 %collective-permute-start.9 = (f32[64,128]{1,0:T(8,128)S(1)}, f32[64,128]{1,0:T(8,128)S(1)}, u32[]{:S(2)}, u32[]{:S(2)}) collective-permute-start(f32[64,128]{1,0:T(8,128)S(1)} %get-tuple-element.69), channel_id=1, source_target_pairs={{0,15},{1,2},{2,1},{3,4},{4,3},{5,6},{6,5},{7,8},{8,7},{9,10},{10,... | collective-permute-start | bytes 98312 | tf_op jit(solution)/shard_map/ppermute | solution.py:54
  37.2 0.7 %own.8.refs_2_ = f32[64,512]{1,0:T(8,128)S(1)} custom-call(bf16[1024,512]{1,0:T(8,128)(2,1)S(1)} %table.1.refs_0_, f32[2,32,128]{2,1,0:T(8,128)S(1)} %get-tuple-element.46.refs_1_.refs_7_, f32[24,32,128]{2,1,0:T(8,128)S(1)} %get-tuple-element.47.refs_2_.refs_8_, f32[64,128]{1,0:T(8,128)S(1)} %get-tuple-element.66.refs_3_), custom_call_target="tpu_custom_call" | custom-call | tf_op jit(solution)/shard_map/own/pallas_call | solution.py:665
  37.9 1.3 %place.2.refs_0_ = f32[64,4096]{1,0:T(8,128)S(1)} custom-call(f32[64,2560]{1,0:T(8,128)S(1)} %own.6.refs_3_.refs_0_, f32[64,1024]{1,0:T(8,128)S(1)} %own.7.refs_5_.refs_1_, f32[64,512]{1,0:T(8,128)S(1)} %own.8.refs_2_, f32[264,128]{1,0:T(8,128)S(1)} %collective-permute-done.7.refs_1_.refs_3_, f32[192,128]{1,0:T(8,128)S(1)} %collective-permute-done.6.refs_1_.refs_4_, ...), custom_call_target="tpu_custom_call" | custom-call | tf_op jit(solution)/shard_map/place/pallas_call | solution.py:666
  39.2 0.5 sum.2
  39.7 1.0 %early.1 = (f32[8,64,128]{2,1,0:T(8,128)S(1)}, s32[8,128]{1,0:T(8,128)S(1)}, f32[4,8,128]{2,1,0:T(8,128)S(1)}) custom-call(bf16[1024,512]{1,0:T(8,128)(2,1)S(1)} %get-tuple-element.72.refs_0_, f32[24,128]{1,0:T(8,128)S(1)} %collective-permute-done.refs_0_.refs_1_, f32[24,128]{1,0:T(8,128)S(1)} %collective-permute-done.1.refs_1_.refs_2_, ...), custom_call_target="tpu_custom_call" | custom-call | tf_op jit(solution)/shard_map/early/pallas_call | solution.py:675
  40.7 0.3 collective-permute-done.9.refs_1_.refs_3_
  41.1 0.4 late.1
  41.5 3.4 %collective-permute-start.11 = (f32[192,128]{1,0:T(8,128)S(1)}, f32[192,128]{1,0:T(8,128)S(1)}, u32[]{:S(2)}, u32[]{:S(2)}) collective-permute-start(f32[192,128]{1,0:T(8,128)S(1)} %get-tuple-element.76), channel_id=1, source_target_pairs={{0,15},{1,2},{2,1},{3,4},{4,3},{5,6},{6,5},{7,8},{8,7},{9,10},{10,... | collective-permute-start | bytes 294920 | tf_op jit(solution)/shard_map/ppermute | solution.py:54
  44.9 0.4 finish.1.refs_0_
  45.3 0.4 own_faces.3.refs_5_.refs_0_
  45.7 2.5 %own.9.refs_3_.refs_0_ = f32[64,2048]{1,0:T(8,128)S(1)} custom-call(bf16[1024,512]{1,0:T(8,128)(2,1)S(1)} %finish.1.refs_0_, f32[2,32,128]{2,1,0:T(8,128)S(1)} %get-tuple-element.70.refs_1_.refs_7_, f32[24,32,128]{2,1,0:T(8,128)S(1)} %get-tuple-element.71.refs_2_.refs_8_), custom_call_target="tpu_custom_call" | custom-call | tf_op jit(solution)/shard_map/own/pallas_call | solution.py:647
  48.3 0.5 reply_x.3.refs_2_
  48.7 0.8 %collective-permute-done.11.refs_0_.refs_3_.refs_5_ = f32[192,128]{1,0:T(8,128)S(1)} collective-permute-done((f32[192,128]{1,0:T(8,128)S(1)}, f32[192,128]{1,0:T(8,128)S(1)}, u32[]{:S(2)}, u32[]{:S(2)}) %collective-permute-start.11) | collective-permute-done | bytes 98336 | tf_op jit(solution)/shard_map/ppermute | solution.py:54
  49.7 1.3 %collective-permute-done.13.refs_1_.refs_4_ = f32[192,128]{1,0:T(8,128)S(1)} collective-permute-done((f32[192,128]{1,0:T(8,128)S(1)}, f32[192,128]{1,0:T(8,128)S(1)}, u32[]{:S(2)}, u32[]{:S(2)}) %collective-permute-start.13) | collective-permute-done | bytes 98336 | tf_op jit(solution)/shard_map/ppermute | solution.py:58
  50.9 0.2 faces_near.3
  51.2 2.1 %collective-permute-start.14 = (f32[264,128]{1,0:T(8,128)S(1)}, f32[264,128]{1,0:T(8,128)S(1)}, u32[]{:S(2)}, u32[]{:S(2)}) collective-permute-start(f32[264,128]{1,0:T(8,128)S(1)} %get-tuple-element.81.refs_2_), channel_id=1, source_target_pairs={{0,112},{16,32},{32,16},{48,64},{64,48},{80,96},{96,80},{112,0},{1... | collective-permute-start | bytes 405512 | tf_op jit(solution)/shard_map/ppermute | solution.py:54
  53.2 2.0 %own.10.refs_5_.refs_1_ = f32[64,1536]{1,0:T(8,128)S(1)} custom-call(bf16[1024,512]{1,0:T(8,128)(2,1)S(1)} %finish.1.refs_0_, f32[2,32,128]{2,1,0:T(8,128)S(1)} %get-tuple-element.70.refs_1_.refs_7_, f32[24,32,128]{2,1,0:T(8,128)S(1)} %get-tuple-element.71.refs_2_.refs_8_, f32[64,256]{1,0:T(8,128)S(1)} %get-tuple-element.80.refs_3_.refs_0_), custom_call_target="tpu_custom_call" | custom-call | tf_op jit(solution)/shard_map/own/pallas_call | solution.py:656
  55.2 1.7 %collective-permute-done.14.refs_1_.refs_3_ = f32[264,128]{1,0:T(8,128)S(1)} collective-permute-done((f32[264,128]{1,0:T(8,128)S(1)}, f32[264,128]{1,0:T(8,128)S(1)}, u32[]{:S(2)}, u32[]{:S(2)}) %collective-permute-start.14) | collective-permute-done | bytes 135200 | tf_op jit(solution)/shard_map/ppermute | solution.py:54
  56.9 0.2 faces_far.3
  57.2 1.2 %collective-permute-done.15.refs_2_ = f32[64,128]{1,0:T(8,128)S(1)} collective-permute-done((f32[64,128]{1,0:T(8,128)S(1)}, f32[64,128]{1,0:T(8,128)S(1)}, u32[]{:S(2)}, u32[]{:S(2)}) %collective-permute-start.15) | collective-permute-done | bytes 32800 | tf_op jit(solution)/shard_map/ppermute | solution.py:58
  58.5 3.4 %collective-permute-start.16 = (f32[64,128]{1,0:T(8,128)S(1)}, f32[64,128]{1,0:T(8,128)S(1)}, u32[]{:S(2)}, u32[]{:S(2)}) collective-permute-start(f32[64,128]{1,0:T(8,128)S(1)} %get-tuple-element.86), channel_id=1, source_target_pairs={{0,15},{1,2},{2,1},{3,4},{4,3},{5,6},{6,5},{7,8},{8,7},{9,10},{10,... | collective-permute-start | bytes 98312 | tf_op jit(solution)/shard_map/ppermute | solution.py:54
  61.9 0.7 %own.11.refs_2_ = f32[64,512]{1,0:T(8,128)S(1)} custom-call(bf16[1024,512]{1,0:T(8,128)(2,1)S(1)} %finish.1.refs_0_, f32[2,32,128]{2,1,0:T(8,128)S(1)} %get-tuple-element.70.refs_1_.refs_7_, f32[24,32,128]{2,1,0:T(8,128)S(1)} %get-tuple-element.71.refs_2_.refs_8_, f32[64,128]{1,0:T(8,128)S(1)} %get-tuple-element.85.refs_3_), custom_call_target="tpu_custom_call" | custom-call | tf_op jit(solution)/shard_map/own/pallas_call | solution.py:665
  62.7 1.3 %place.3.refs_0_ = f32[64,4096]{1,0:T(8,128)S(1)} custom-call(f32[64,2048]{1,0:T(8,128)S(1)} %own.9.refs_3_.refs_0_, f32[64,1536]{1,0:T(8,128)S(1)} %own.10.refs_5_.refs_1_, f32[64,512]{1,0:T(8,128)S(1)} %own.11.refs_2_, f32[264,128]{1,0:T(8,128)S(1)} %collective-permute-done.14.refs_1_.refs_3_, f32[192,128]{1,0:T(8,128)S(1)} %collective-permute-done.13.refs_1_.refs_4_, ...), custom_call_target="tpu_custom_call" | custom-call | tf_op jit(solution)/shard_map/place/pallas_call | solution.py:666
  63.9 0.5 sum.3.summed
  64.4 1.4 %collective-permute-done.16.y_first = f32[64,128]{1,0:T(8,128)S(1)} collective-permute-done((f32[64,128]{1,0:T(8,128)S(1)}, f32[64,128]{1,0:T(8,128)S(1)}, u32[]{:S(2)}, u32[]{:S(2)}) %collective-permute-start.16) | collective-permute-done | bytes 32800 | tf_op jit(solution)/shard_map/ppermute | solution.py:54
  65.9 1.3 %last.1 = f32[64,16,256]{2,1,0:T(8,128)} custom-call(f32[64,4096]{1,0:T(8,128)S(1)} %sum.3.summed, f32[64,128]{1,0:T(8,128)S(1)} %collective-permute-done.16.y_first, f32[64,128]{1,0:T(8,128)S(1)} %collective-permute-done.17.y_second, f32[8,128]{1,0:T(8,128)S(1)} %get-tuple-element.57.refs_4_.refs_3_.refs_5_.scale), custom_call_target="tpu_custom_call" | custom-call | tf_op jit(solution)/shard_map/last/pallas_call | solution.py:689
  (23 shorter events, 0.8 us)
Async XLA Ops:
  1.2 4.4 %collective-permute-start = (f32[24,128]{1,0:T(8,128)S(1)}, f32[24,128]{1,0:T(8,128)S(1)}, u32[]{:S(2)}, u32[]{:S(2)}) collective-permute-start(f32[24,128]{1,0:T(8,128)S(1)} %get-tuple-element.49), channel_id=1, source_target_pairs={{0,112},{16,32},{32,16},{48,64},{64,48},{80,96},{96,80},{112,0},{1... | collective-permute-start | bytes 36872 | tf_op jit(solution)/shard_map/ppermute | solution.py:54
  3.8 1.8 %collective-permute-start.1 = (f32[24,128]{1,0:T(8,128)S(1)}, f32[24,128]{1,0:T(8,128)S(1)}, u32[]{:S(2)}, u32[]{:S(2)}) collective-permute-start(f32[24,128]{1,0:T(8,128)S(1)} %get-tuple-element.50), channel_id=1, source_target_pairs={{0,16},{16,0},{32,48},{48,32},{64,80},{80,64},{96,112},{112,96},{1... | collective-permute-start | bytes 36872 | tf_op jit(solution)/shard_map/ppermute | solution.py:58
  5.7 9.8 %collective-permute-start.2 = (f32[24,128]{1,0:T(8,128)S(1)}, f32[24,128]{1,0:T(8,128)S(1)}, u32[]{:S(2)}, u32[]{:S(2)}) collective-permute-start(f32[24,128]{1,0:T(8,128)S(1)} %get-tuple-element.53), channel_id=1, source_target_pairs={{0,15},{1,2},{2,1},{3,4},{4,3},{5,6},{6,5},{7,8},{8,7},{9,10},{10,... | collective-permute-start | bytes 36872 | tf_op jit(solution)/shard_map/ppermute | solution.py:54
  12.0 3.7 %collective-permute-start.3 = (f32[24,128]{1,0:T(8,128)S(1)}, f32[24,128]{1,0:T(8,128)S(1)}, u32[]{:S(2)}, u32[]{:S(2)}) collective-permute-start(f32[24,128]{1,0:T(8,128)S(1)} %get-tuple-element.54), channel_id=1, source_target_pairs={{0,1},{1,0},{2,3},{3,2},{4,5},{5,4},{6,7},{7,6},{8,9},{9,8},{10,11... | collective-permute-start | bytes 36872 | tf_op jit(solution)/shard_map/ppermute | solution.py:58
  16.7 8.0 %collective-permute-start.4 = (f32[192,128]{1,0:T(8,128)S(1)}, f32[192,128]{1,0:T(8,128)S(1)}, u32[]{:S(2)}, u32[]{:S(2)}) collective-permute-start(f32[192,128]{1,0:T(8,128)S(1)} %get-tuple-element.55), channel_id=1, source_target_pairs={{0,15},{1,2},{2,1},{3,4},{4,3},{5,6},{6,5},{7,8},{8,7},{9,10},{10,... | collective-permute-start | bytes 294920 | tf_op jit(solution)/shard_map/ppermute | solution.py:54
  20.1 4.6 %collective-permute-start.5 = (f32[192,128]{1,0:T(8,128)S(1)}, f32[192,128]{1,0:T(8,128)S(1)}, u32[]{:S(2)}, u32[]{:S(2)}) collective-permute-start(f32[192,128]{1,0:T(8,128)S(1)} %get-tuple-element.56), channel_id=1, source_target_pairs={{0,1},{1,0},{2,3},{3,2},{4,5},{5,4},{6,7},{7,6},{8,9},{9,8},{10,11... | collective-permute-start | bytes 294920 | tf_op jit(solution)/shard_map/ppermute | solution.py:58
  20.6 3.1 %copy-start = (f32[16,256]{1,0:T(8,128)S(1)}, f32[16,256]{1,0:T(8,128)}, u32[]{:S(2)}) copy-start(f32[16,256]{1,0:T(8,128)} %refs_9_.3) | copy-start | bytes 49156
  24.8 1.4 %collective-permute-start.6 = (f32[192,128]{1,0:T(8,128)S(1)}, f32[192,128]{1,0:T(8,128)S(1)}, u32[]{:S(2)}, u32[]{:S(2)}) collective-permute-start(f32[192,128]{1,0:T(8,128)S(1)} %get-tuple-element.58), channel_id=1, source_target_pairs={{0,16},{16,0},{32,48},{48,32},{64,80},{80,64},{96,112},{112,96},{1... | collective-permute-start | bytes 294920 | tf_op jit(solution)/shard_map/ppermute | solution.py:58
  26.4 5.7 %collective-permute-start.7 = (f32[264,128]{1,0:T(8,128)S(1)}, f32[264,128]{1,0:T(8,128)S(1)}, u32[]{:S(2)}, u32[]{:S(2)}) collective-permute-start(f32[264,128]{1,0:T(8,128)S(1)} %get-tuple-element.61.refs_2_), channel_id=1, source_target_pairs={{0,112},{16,32},{32,16},{48,64},{64,48},{80,96},{96,80},{112,0},{1... | collective-permute-start | bytes 405512 | tf_op jit(solution)/shard_map/ppermute | solution.py:54
  32.3 1.3 %collective-permute-start.8 = (f32[64,128]{1,0:T(8,128)S(1)}, f32[64,128]{1,0:T(8,128)S(1)}, u32[]{:S(2)}, u32[]{:S(2)}) collective-permute-start(f32[64,128]{1,0:T(8,128)S(1)} %get-tuple-element.65), channel_id=1, source_target_pairs={{0,16},{16,0},{32,48},{48,32},{64,80},{80,64},{96,112},{112,96},{1... | collective-permute-start | bytes 98312 | tf_op jit(solution)/shard_map/ppermute | solution.py:58
  33.8 7.3 %collective-permute-start.9 = (f32[64,128]{1,0:T(8,128)S(1)}, f32[64,128]{1,0:T(8,128)S(1)}, u32[]{:S(2)}, u32[]{:S(2)}) collective-permute-start(f32[64,128]{1,0:T(8,128)S(1)} %get-tuple-element.69), channel_id=1, source_target_pairs={{0,15},{1,2},{2,1},{3,4},{4,3},{5,6},{6,5},{7,8},{8,7},{9,10},{10,... | collective-permute-start | bytes 98312 | tf_op jit(solution)/shard_map/ppermute | solution.py:54
  37.2 3.9 %collective-permute-start.10 = (f32[64,128]{1,0:T(8,128)S(1)}, f32[64,128]{1,0:T(8,128)S(1)}, u32[]{:S(2)}, u32[]{:S(2)}) collective-permute-start(f32[64,128]{1,0:T(8,128)S(1)} %get-tuple-element.66.refs_3_), channel_id=1, source_target_pairs={{0,1},{1,0},{2,3},{3,2},{4,5},{5,4},{6,7},{7,6},{8,9},{9,8},{10,11... | collective-permute-start | bytes 98312 | tf_op jit(solution)/shard_map/ppermute | solution.py:58
  41.5 8.0 %collective-permute-start.11 = (f32[192,128]{1,0:T(8,128)S(1)}, f32[192,128]{1,0:T(8,128)S(1)}, u32[]{:S(2)}, u32[]{:S(2)}) collective-permute-start(f32[192,128]{1,0:T(8,128)S(1)} %get-tuple-element.76), channel_id=1, source_target_pairs={{0,15},{1,2},{2,1},{3,4},{4,3},{5,6},{6,5},{7,8},{8,7},{9,10},{10,... | collective-permute-start | bytes 294920 | tf_op jit(solution)/shard_map/ppermute | solution.py:54
  44.9 4.6 %collective-permute-start.12 = (f32[192,128]{1,0:T(8,128)S(1)}, f32[192,128]{1,0:T(8,128)S(1)}, u32[]{:S(2)}, u32[]{:S(2)}) collective-permute-start(f32[192,128]{1,0:T(8,128)S(1)} %get-tuple-element.77), channel_id=1, source_target_pairs={{0,1},{1,0},{2,3},{3,2},{4,5},{5,4},{6,7},{7,6},{8,9},{9,8},{10,11... | collective-permute-start | bytes 294920 | tf_op jit(solution)/shard_map/ppermute | solution.py:58
  49.6 1.4 %collective-permute-start.13 = (f32[192,128]{1,0:T(8,128)S(1)}, f32[192,128]{1,0:T(8,128)S(1)}, u32[]{:S(2)}, u32[]{:S(2)}) collective-permute-start(f32[192,128]{1,0:T(8,128)S(1)} %get-tuple-element.78), channel_id=1, source_target_pairs={{0,16},{16,0},{32,48},{48,32},{64,80},{80,64},{96,112},{112,96},{1... | collective-permute-start | bytes 294920 | tf_op jit(solution)/shard_map/ppermute | solution.py:58
  51.2 5.7 %collective-permute-start.14 = (f32[264,128]{1,0:T(8,128)S(1)}, f32[264,128]{1,0:T(8,128)S(1)}, u32[]{:S(2)}, u32[]{:S(2)}) collective-permute-start(f32[264,128]{1,0:T(8,128)S(1)} %get-tuple-element.81.refs_2_), channel_id=1, source_target_pairs={{0,112},{16,32},{32,16},{48,64},{64,48},{80,96},{96,80},{112,0},{1... | collective-permute-start | bytes 405512 | tf_op jit(solution)/shard_map/ppermute | solution.py:54
  57.1 1.3 %collective-permute-start.15 = (f32[64,128]{1,0:T(8,128)S(1)}, f32[64,128]{1,0:T(8,128)S(1)}, u32[]{:S(2)}, u32[]{:S(2)}) collective-permute-start(f32[64,128]{1,0:T(8,128)S(1)} %get-tuple-element.84), channel_id=1, source_target_pairs={{0,16},{16,0},{32,48},{48,32},{64,80},{80,64},{96,112},{112,96},{1... | collective-permute-start | bytes 98312 | tf_op jit(solution)/shard_map/ppermute | solution.py:58
  58.5 7.3 %collective-permute-start.16 = (f32[64,128]{1,0:T(8,128)S(1)}, f32[64,128]{1,0:T(8,128)S(1)}, u32[]{:S(2)}, u32[]{:S(2)}) collective-permute-start(f32[64,128]{1,0:T(8,128)S(1)} %get-tuple-element.86), channel_id=1, source_target_pairs={{0,15},{1,2},{2,1},{3,4},{4,3},{5,6},{6,5},{7,8},{8,7},{9,10},{10,... | collective-permute-start | bytes 98312 | tf_op jit(solution)/shard_map/ppermute | solution.py:54
  61.9 3.9 %collective-permute-start.17 = (f32[64,128]{1,0:T(8,128)S(1)}, f32[64,128]{1,0:T(8,128)S(1)}, u32[]{:S(2)}, u32[]{:S(2)}) collective-permute-start(f32[64,128]{1,0:T(8,128)S(1)} %get-tuple-element.85.refs_3_), channel_id=1, source_target_pairs={{0,1},{1,0},{2,3},{3,2},{4,5},{5,4},{6,7},{7,6},{8,9},{9,8},{10,11... | collective-permute-start | bytes 98312 | tf_op jit(solution)/shard_map/ppermute | solution.py:58
where the time goes:
time: 67.6 us; the launch traced here: 67.3 us
  Pallas kernels  27.7 us (41%)
  starting transfers between devices  27.3 us (40%)
  waiting for transfers between devices  11.8 us (17%)
    ppermute x8, starting transfers between devices, swap_far(): return lax.ppermute(block, axis, pairs)  26.9 us
    ppermute x8, waiting for transfers between devices, swap_far(): return lax.ppermute(block, axis, pairs)  6.62 us
    pallas_call x2, Pallas kernels, per_device(): own_a = interpolate(s, 0)(table, picks, factors)  5.6 us
    ppermute x10, waiting for transfers between devices, swap_near(): lax.ppermute(block, axis, [(i, i ^ 1) for i in range(lax.axis_size(axis))])  5.21 us
    pallas_call x2, Pallas kernels, per_device(): own_b = interpolate(s, 1, after=1)(table, picks, factors, partial)  3.24 us
    pallas_call x2, Pallas kernels, per_device(): call(lambda *refs, s=s: place_body(s, *refs), shape((F, POINTS)), 'place'...  2.56 us
    pallas_call x1, Pallas kernels, per_device(): ordered.append(requests(1, after=1)(*lists_in, partial))  1.91 us
    pallas_call x1, Pallas kernels, per_device(): ordered = [requests(0)(*lists_in)]  1.9 us
  transfers between devices with their start and end apart: 18, of which 12 were waited for; matrix products, arithmetic and copies ran while one was open for 0% of the time, Pallas kernels for 34%

commit v1 on v0

--- a/solution.py
+++ b/solution.py
@@ -14,7 +14,7 @@
 NODES = 16
 POINTS = 4096
 TILES = POINTS // 128
-PIECES = (((0, 10), (10, 14), (14, 16)), ((0, 8), (8, 14), (14, 16)))
+PIECES = (((0, 10), (10, 14), (14, 16)), ((0, 9), (9, 13), (13, 16)))
 GLL_NODES = (-1.0, -0.4472135954999579, 0.4472135954999579, 1.0)
 REMOTE = (0, 1, 2, 3, 5, 6, 7, 8)
 BF16 = jnp.bfloat16
@@ -224,31 +224,48 @@
 
 
 def order_body(
-    s, offsets_in, order_in, source_in, coords_in, picks, factors, face_picks,
+    offsets_in, order_in, source_in, coords_in, picks, factors, face_picks, later, later_starts,
     offsets, order, source, coords, sems,
 ):
     fetch(
         [(offsets_in, offsets), (order_in, order), (source_in, source), (coords_in, coords)], sems
     )
+    ordered(
+        order[0], source[0:1], coords[0, 0:1], coords[0, 1:2], offsets[0], picks, factors, face_picks
+    )
+    later[0:1, :] = order[1]
+    later[1:2, :] = source[1:2, :]
+    later[2:4, :] = coords[1]
+    later_starts[0:1, 0:10] = offsets[1]
+
+
+def later_body(lists, starts, picks, factors, face_picks):
+    ordered(
+        lists[0:1], lists[1:2], lists[2:3], lists[3:4], starts[0:1], picks, factors, face_picks
+    )
+
+
+def ordered(nodes, sources, xs, ys, starts, picks, factors, face_picks):
     chunk = 1024
     total = None
     for c in range(POINTS // chunk):
         lanes = slice(c * chunk, (c + 1) * chunk)
-        node = order[s, :, lanes]
+        node = nodes[:, lanes]
         tile_of = (node // 128).astype(F32).astype(BF16)
         lane_of = (node % 128).astype(F32).astype(BF16)
         position = lax.broadcasted_iota(jnp.int32, (1, chunk), 1) + c * chunk
         run = jnp.zeros((1, chunk), jnp.int32)
-        begin = jnp.zeros((1, chunk), jnp.int32) + offsets[s, 0, 0]
+        begin = jnp.broadcast_to(starts[:, 0:1], (1, chunk))
         for k in range(1, 9):
-            passed = position >= offsets[s, 0, k]
+            start = jnp.broadcast_to(starts[:, k : k + 1], (1, chunk))
+            passed = position >= start
             run = run + passed.astype(jnp.int32)
-            begin = jnp.where(passed, offsets[s, 0, k], begin)
+            begin = jnp.where(passed, start, begin)
         own = run == 4
         kind = jnp.where(own, 8, jnp.where(run > 4, run - 1, run))
-        pick = jnp.where(own, source[s : s + 1, lanes], position - begin)
-        cx = coords[s, 0:1, lanes]
-        cy = coords[s, 1:2, lanes]
+        pick = jnp.where(own, sources[:, lanes], position - begin)
+        cx = xs[:, lanes]
+        cy = ys[:, lanes]
         values = [pick, cx // 8, cx % 8, cy // 8, cy % 8, kind]
         tiles = lax.broadcasted_iota(jnp.int32, (TILES, chunk), 0).astype(F32).astype(BF16)
         here = tiles == tile_of
@@ -297,7 +314,7 @@
     first[...], second[...] = to_swaps("fy", *columns)
 
 
-def row_body(y_first, y_second, own, far, near):
+def row_body(y_first, y_second, own, near, far):
     low, high = from_swaps("fy", y_first[...], y_second[...])
     mine = own[...]
     ahead = jnp.concatenate([low[0:F], mine[0:F], high[0:F]], axis=0)
@@ -416,7 +433,7 @@
         return carry
 
     count = result.shape[1] // E
-    lax.fori_loop(0, count, block, 0, unroll=5 if count == 10 else 4 if count == 8 else 3 if count == 6 else count)
+    lax.fori_loop(0, count, block, 0, unroll=5 if count == 10 else 3 if count == 9 else count)
 
 
 def stacked(blocks):
@@ -465,7 +482,7 @@
 
 
 def face_near_body(
-    own, near, far, y_first, y_second, face_picks, mass_faces, partial, message
+    own, near, y_first, y_second, face_picks, mass_faces, partial, message
 ):
     even = lax.axis_index("fx") % 2 == 0
     masks = masks_of(face_picks[1:2, :], kinds(even, True) + [3.0, 4.0])
@@ -473,22 +490,21 @@
     moved = own[...] + placed(answers, face_slots(face_picks), masks)
     moved = moved * mass_faces[0:1, :]
     partial[...] = moved
-    message[0 : 3 * F, :] = far[...]
-    message[3 * F : 4 * F, :] = moved[:, 0:128]
-    message[4 * F : 4 * F + 8, :] = face_picks[:, 0:128]
-    message[4 * F + 2 : 4 * F + 3, :] = mass_faces[0:1, 0:128]
-
-
-def face_far_body(partial, far, sent, face_picks, mass_faces, along_x, along_y, other):
+    message[0:F, :] = moved[:, 0:128]
+    message[F : F + 8, :] = face_picks[:, 0:128]
+    message[F + 2 : F + 3, :] = mass_faces[0:1, 0:128]
+
+
+def face_far_body(partial, far, faces_in, sent, face_picks, mass_faces, along_x, along_y, other):
     even = lax.axis_index("fx") % 2 == 0
     masks = masks_of(face_picks[1:2, :], kinds(even, False))
     moved = placed(stacked(three(far)), face_slots(face_picks), masks) * mass_faces[0:1, :]
     result = partial[...] + moved
     along_x[...] = result[:, 0:128]
     along_y[...] = result[:, 128:256]
-    slot, kind, weight = [far[4 * F + q : 4 * F + q + 1, :] for q in range(3)]
+    slot, kind, weight = [faces_in[F + q : F + q + 1, :] for q in range(3)]
     moved = placed(stacked(three(sent)), [slot], masks_of(kind, kinds(even, True)))
-    other[...] = far[3 * F : 4 * F, :] + moved * weight
+    other[...] = faces_in[0:F, :] + moved * weight
 
 
 def place_body(
@@ -590,21 +606,17 @@
         ],
     )(*[in_hbm(a) for a in (offsets, source, coords, node_mass)])
     asked = swap("fx", first, second)
-    lists_in = [in_hbm(a) for a in (offsets, point_order, source, coords)]
-
-    def requests(s, after=0):
-        return call(
-            lambda *refs: order_body(s, *refs),
-            [shape((2, TILES, 128)), shape((NODES + 8, TILES, 128)), shape((8, 256))],
-            "order",
-            hbm=(0, 1, 2, 3),
-            count=4,
-            after=after,
-            scratch=lists[:1]
-            + [pltpu.VMEM(point_order.shape, jnp.int32)]
-            + lists[1:]
-            + [pltpu.SemaphoreType.DMA((4,))],
-        )
+    requests = [shape((2, TILES, 128)), shape((NODES + 8, TILES, 128)), shape((8, 256))]
+    *now, later, later_starts = call(
+        order_body,
+        requests + [shape((8, POINTS), jnp.int32), shape((8, 128), jnp.int32)],
+        "order",
+        hbm=(0, 1, 2, 3),
+        count=4,
+        scratch=[pltpu.VMEM(a.shape, jnp.int32) for a in (offsets, point_order, source, coords)]
+        + [pltpu.SemaphoreType.DMA((4,))],
+    )(*[in_hbm(a) for a in (offsets, point_order, source, coords)])
+    ordered_lists = [now]
 
     def interpolate(s, piece, after=0):
         begin, end = PIECES[s][piece]
@@ -616,7 +628,6 @@
             after=after,
         )
 
-    ordered = [requests(0)(*lists_in)]
     asked += swap(
         "fy",
         *call(column_body, [ask] * 2, "column", count=4)(*asked, mid, mass_faces),
@@ -630,14 +641,14 @@
         scratch=[pltpu.VMEM(tracers.shape, F32), pltpu.SemaphoreType.DMA((1,))],
     )(in_hbm(tracers))
     far, near = call(reply_y_body, [answers] * 2, "reply_y", count=5, after=1)(
-        table, *asked, ordered[0][2]
+        table, *asked, now[2]
     )
     answers_y = swap("fy", far, near)
     inverse, scale = call(scale_body, [shape((NODES, E)), shape((8, 128))], "scale", count=5)(
         node_mass, *asked
     )
     for s in range(SUBSTEPS):
-        picks, factors, face_picks = ordered[s]
+        picks, factors, face_picks = ordered_lists[s]
         if s == 1:
             table = call(finish_body, table_shape, "finish", count=4)(summed, *edges_y, scale)
         own = call(
@@ -645,20 +656,25 @@
         )(table, *asked)
         own_faces = call(own_faces_body, shape((F, 256)), "own_faces", count=2)(table, face_picks)
         own_a = interpolate(s, 0)(table, picks, factors)
-        far, near = call(row_body, [answers] * 2, "row", count=3, after=3)(
+        near_sent, far_sent = call(row_body, [answers] * 2, "row", count=3, after=3)(
             *answers_y, own, own_a, scale, own_faces
         )
-        near = swap_near("fx", near)
+        near = swap_near("fx", near_sent)
+        far = swap_far("fx", far_sent)
         partial, message = call(
-            face_near_body, [shape((F, 256)), shape((4 * F + 8, 128))], "faces_near", count=7
-        )(own_faces, near, far, *answers_y, face_picks, mass_faces)
-        far = swap_far("fx", message)
+            face_near_body, [shape((F, 256)), shape((F + 8, 128))], "faces_near", count=6
+        )(own_faces, near, *answers_y, face_picks, mass_faces)
+        faces_in = swap_far("fx", message)
         own_b = interpolate(s, 1, after=1)(table, picks, factors, partial)
         if s == 0:
-            ordered.append(requests(1, after=1)(*lists_in, partial))
+            ordered_lists.append(
+                call(later_body, requests, "order", count=2, after=1)(
+                    later, later_starts, partial
+                )
+            )
         along_x, along_y, other = call(
-            face_far_body, [face] * 3, "faces_far", count=5, after=2
-        )(partial, far, message, face_picks, mass_faces, own_b, ordered[1][2])
+            face_far_body, [face] * 3, "faces_far", count=6, after=2
+        )(partial, far, faces_in, far_sent, face_picks, mass_faces, own_b, ordered_lists[1][2])
         edges_x = (other, swap_near("fx", along_x))
         first, second = call(rim_body, [face] * 2, "rim", count=3)(along_y, *edges_x)
         edges_y = swap("fy", first, second)

time: 67.6 us -> 66.7 us (0.987)
  waiting for transfers between devices: 11.8 us -> 10.9 us
  Pallas kernels: 27.7 us -> 26.8 us
  starting transfers between devices: 27.3 us -> 28.2 us
    ppermute x10, waiting for transfers between devices: 5.21 us -> 2.83 us  [swap_near(): lax.ppermute(block, axis, [(i, i ^ 1) for i in range(lax.axis_size(axis))])]
    ppermute x8 -> x10, waiting for transfers between devices: 6.62 us -> 8.1 us  [swap_far(): return lax.ppermute(block, axis, pairs)]
    ppermute x8 -> x10, starting transfers between devices: 26.9 us -> 27.9 us  [swap_far(): return lax.ppermute(block, axis, pairs)]
    pallas_call x6, Pallas kernels: 4.67 us -> 3.77 us  [the longest x1 1.91 us: per_device(): call(order_body, requests + [shape((8, POINTS), jnp.int32), shape((8, 128...]
    pallas_call x2, Pallas kernels: 3.24 us -> 2.51 us  [per_device(): own_b = interpolate(s, 1, after=1)(table, picks, factors, partial)]
  transfers between devices with their start and end apart: 18 -> 20, of which waited for: 12 -> 12; matrix products, arithmetic and copies ran while one was open for 0% -> 0% of each run, Pallas kernels for 34% -> 33%
where the time goes in v1:
time: 66.7 us; the launch traced here: 66.5 us
  starting transfers between devices  28.2 us (42%)
  Pallas kernels  26.8 us (40%)
  waiting for transfers between devices  10.9 us (16%)
    ppermute x10, starting transfers between devices, swap_far(): return lax.ppermute(block, axis, pairs)  27.9 us
    ppermute x10, waiting for transfers between devices, swap_far(): return lax.ppermute(block, axis, pairs)  8.1 us
    pallas_call x2, Pallas kernels, per_device(): own_a = interpolate(s, 0)(table, picks, factors)  6.04 us
    ppermute x10, waiting for transfers between devices, swap_near(): lax.ppermute(block, axis, [(i, i ^ 1) for i in range(lax.axis_size(axis))])  2.83 us
    pallas_call x2, Pallas kernels, per_device(): call(lambda *refs, s=s: place_body(s, *refs), shape((F, POINTS)), 'place'...  2.57 us
    pallas_call x2, Pallas kernels, per_device(): own_b = interpolate(s, 1, after=1)(table, picks, factors, partial)  2.51 us
    pallas_call x1, Pallas kernels, per_device(): call(order_body, requests + [shape((8, POINTS), jnp.int32), shape((8, 128...  1.91 us
    pallas_call x2, Pallas kernels, per_device(): own_c = interpolate(s, 2, after=1)(table, picks, factors, second)  1.69 us
  transfers between devices with their start and end apart: 20, of which 12 were waited for; matrix products, arithmetic and copies ran while one was open for 0% of the time, Pallas kernels for 33%

profile of v1, /device:TPU:0, one launch (start us, length us, event | category | flops | bytes accessed | tf_op | source)
XLA Modules:
  0.0 66.5 jit_solution(10328962776784099868)
XLA Ops:
  0.0 1.2 %asks.1 = (f32[24,128]{1,0:T(8,128)S(1)}, f32[24,128]{1,0:T(8,128)S(1)}, f32[24,128]{1,0:T(8,128)S(1)}, f32[8,256]{1,0:T(8,128)S(1)}) custom-call(s32[2,1,10]{2,1,0:T(1,128)} %refs_0_.6, s32[2,4096]{1,0:T(2,128)} %refs_1_.3, s32[2,2,4096]{2,1,0:T(2,128)} %refs_2_.3, f32[16,256]{1,0:T(8,128)} %refs_9_.3), custom_call_target="tpu_custom_call" | custom-call | tf_op jit(solution)/shard_map/asks/pallas_call | solution.py:594
  1.2 2.6 %collective-permute-start = (f32[24,128]{1,0:T(8,128)S(1)}, f32[24,128]{1,0:T(8,128)S(1)}, u32[]{:S(2)}, u32[]{:S(2)}) collective-permute-start(f32[24,128]{1,0:T(8,128)S(1)} %get-tuple-element.51), channel_id=1, source_target_pairs={{0,112},{16,32},{32,16},{48,64},{64,48},{80,96},{96,80},{112,0},{1... | collective-permute-start | bytes 36872 | tf_op jit(solution)/shard_map/ppermute | solution.py:54
  3.8 1.8 %collective-permute-done.refs_0_.refs_1_ = f32[24,128]{1,0:T(8,128)S(1)} collective-permute-done((f32[24,128]{1,0:T(8,128)S(1)}, f32[24,128]{1,0:T(8,128)S(1)}, u32[]{:S(2)}, u32[]{:S(2)}) %collective-permute-start) | collective-permute-done | bytes 12320 | tf_op jit(solution)/shard_map/ppermute | solution.py:54
  5.7 6.4 %collective-permute-start.2 = (f32[24,128]{1,0:T(8,128)S(1)}, f32[24,128]{1,0:T(8,128)S(1)}, u32[]{:S(2)}, u32[]{:S(2)}) collective-permute-start(f32[24,128]{1,0:T(8,128)S(1)} %get-tuple-element.55), channel_id=1, source_target_pairs={{0,15},{1,2},{2,1},{3,4},{4,3},{5,6},{6,5},{7,8},{8,7},{9,10},{10,... | collective-permute-start | bytes 36872 | tf_op jit(solution)/shard_map/ppermute | solution.py:54
  12.0 1.9 %order.2 = (f32[2,32,128]{2,1,0:T(8,128)S(1)}, f32[24,32,128]{2,1,0:T(8,128)S(1)}, f32[8,256]{1,0:T(8,128)S(1)}, s32[8,4096]{1,0:T(8,128)S(1)}, s32[8,128]{1,0:T(8,128)S(1)}) custom-call(s32[2,1,10]{2,1,0:T(1,128)} %refs_0_.6, s32[2,1,4096]{2,1,0:T(1,128)} %refs_1_.2, s32[2,4096]{1,0:T(2,128)} %refs_1_.3, s32[2,2,4096]{2,1,0:T(2,128)} %refs_2_.3), custom_call_target="tpu_custom_call" | custom-call | tf_op jit(solution)/shard_map/order/pallas_call | solution.py:610
  13.9 1.5 %table.1.refs_0_ = bf16[1024,512]{1,0:T(8,128)(2,1)S(1)} custom-call(f32[64,16,256]{2,1,0:T(8,128)} %refs_0_.4), custom_call_target="tpu_custom_call" | custom-call | tf_op jit(solution)/shard_map/table/pallas_call | solution.py:635
  15.5 0.2 collective-permute-done.3.refs_4_
  15.7 1.0 %reply_y.1 = (f32[192,128]{1,0:T(8,128)S(1)}, f32[192,128]{1,0:T(8,128)S(1)}) custom-call(bf16[1024,512]{1,0:T(8,128)(2,1)S(1)} %table.1.refs_0_, f32[24,128]{1,0:T(8,128)S(1)} %collective-permute-done.refs_0_.refs_1_, f32[24,128]{1,0:T(8,128)S(1)} %collective-permute-done.1.refs_1_.refs_2_, f32[24,128]{1,0:T(8,128)S(1)} %collective-permute-done.2.refs_3_, ...), custom_call_target="tpu_custom_call" | custom-call | tf_op jit(solution)/shard_map/reply_y/pallas_call | solution.py:643
  16.7 3.4 %collective-permute-start.4 = (f32[192,128]{1,0:T(8,128)S(1)}, f32[192,128]{1,0:T(8,128)S(1)}, u32[]{:S(2)}, u32[]{:S(2)}) collective-permute-start(f32[192,128]{1,0:T(8,128)S(1)} %get-tuple-element.57), channel_id=1, source_target_pairs={{0,15},{1,2},{2,1},{3,4},{4,3},{5,6},{6,5},{7,8},{8,7},{9,10},{10,... | collective-permute-start | bytes 294920 | tf_op jit(solution)/shard_map/ppermute | solution.py:54
  20.1 0.4 own_faces.2.refs_5_.refs_0_
  20.6 3.1 %own.6.refs_3_.refs_0_ = f32[64,2560]{1,0:T(8,128)S(1)} custom-call(bf16[1024,512]{1,0:T(8,128)(2,1)S(1)} %table.1.refs_0_, f32[2,32,128]{2,1,0:T(8,128)S(1)} %get-tuple-element.48.refs_1_.refs_7_, f32[24,32,128]{2,1,0:T(8,128)S(1)} %get-tuple-element.49.refs_2_.refs_8_), custom_call_target="tpu_custom_call" | custom-call | tf_op jit(solution)/shard_map/own/pallas_call | solution.py:658
  23.7 0.3 scale.1
  24.0 0.5 reply_x.2.refs_2_
  24.4 0.3 collective-permute-done.4.refs_0_.refs_2_.refs_5_
  24.9 2.6 %collective-permute-start.7 = (f32[192,128]{1,0:T(8,128)S(1)}, f32[192,128]{1,0:T(8,128)S(1)}, u32[]{:S(2)}, u32[]{:S(2)}) collective-permute-start(f32[192,128]{1,0:T(8,128)S(1)} %get-tuple-element.62.refs_3_), channel_id=1, source_target_pairs={{0,112},{16,32},{32,16},{48,64},{64,48},{80,96},{96,80},{112,0},{1... | collective-permute-start | bytes 294920 | tf_op jit(solution)/shard_map/ppermute | solution.py:54
  27.4 0.2 faces_near.2
  27.7 1.0 %collective-permute-start.8 = (f32[72,128]{1,0:T(8,128)S(1)}, f32[72,128]{1,0:T(8,128)S(1)}, u32[]{:S(2)}, u32[]{:S(2)}) collective-permute-start(f32[72,128]{1,0:T(8,128)S(1)} %get-tuple-element.63), channel_id=1, source_target_pairs={{0,112},{16,32},{32,16},{48,64},{64,48},{80,96},{96,80},{112,0},{1... | collective-permute-start | bytes 110600 | tf_op jit(solution)/shard_map/ppermute | solution.py:54
  28.7 1.3 %own.7.refs_6_.refs_1_ = f32[64,1024]{1,0:T(8,128)S(1)} custom-call(bf16[1024,512]{1,0:T(8,128)(2,1)S(1)} %table.1.refs_0_, f32[2,32,128]{2,1,0:T(8,128)S(1)} %get-tuple-element.48.refs_1_.refs_7_, f32[24,32,128]{2,1,0:T(8,128)S(1)} %get-tuple-element.49.refs_2_.refs_8_, f32[64,256]{1,0:T(8,128)S(1)} %get-tuple-element.61.refs_3_.refs_2_.refs_0_), custom_call_target="tpu_custom_call" | custom-call | tf_op jit(solution)/shard_map/own/pallas_call | solution.py:668
  29.9 1.0 %order.3 = (f32[2,32,128]{2,1,0:T(8,128)S(1)}, f32[24,32,128]{2,1,0:T(8,128)S(1)}, f32[8,256]{1,0:T(8,128)S(1)}) custom-call(s32[8,4096]{1,0:T(8,128)S(1)} %get-tuple-element.64.refs_0_, s32[8,128]{1,0:T(8,128)S(1)} %get-tuple-element.65.refs_1_, f32[64,256]{1,0:T(8,128)S(1)} %get-tuple-element.61.refs_3_.refs_2_.refs_0_), custom_call_target="tpu_custom_call" | custom-call | tf_op jit(solution)/shard_map/order/pallas_call | solution.py:671
  30.9 1.4 %collective-permute-done.8.refs_2_ = f32[72,128]{1,0:T(8,128)S(1)} collective-permute-done((f32[72,128]{1,0:T(8,128)S(1)}, f32[72,128]{1,0:T(8,128)S(1)}, u32[]{:S(2)}, u32[]{:S(2)}) %collective-permute-start.8) | collective-permute-done | bytes 36896 | tf_op jit(solution)/shard_map/ppermute | solution.py:54
  32.3 0.2 faces_far.2
  32.7 1.2 %collective-permute-done.9.refs_2_ = f32[64,128]{1,0:T(8,128)S(1)} collective-permute-done((f32[64,128]{1,0:T(8,128)S(1)}, f32[64,128]{1,0:T(8,128)S(1)}, u32[]{:S(2)}, u32[]{:S(2)}) %collective-permute-start.9) | collective-permute-done | bytes 32800 | tf_op jit(solution)/shard_map/ppermute | solution.py:58
  34.0 3.0 %collective-permute-start.10 = (f32[64,128]{1,0:T(8,128)S(1)}, f32[64,128]{1,0:T(8,128)S(1)}, u32[]{:S(2)}, u32[]{:S(2)}) collective-permute-start(f32[64,128]{1,0:T(8,128)S(1)} %get-tuple-element.73), channel_id=1, source_target_pairs={{0,15},{1,2},{2,1},{3,4},{4,3},{5,6},{6,5},{7,8},{8,7},{9,10},{10,... | collective-permute-start | bytes 98312 | tf_op jit(solution)/shard_map/ppermute | solution.py:54
  37.0 0.7 %own.8.refs_2_ = f32[64,512]{1,0:T(8,128)S(1)} custom-call(bf16[1024,512]{1,0:T(8,128)(2,1)S(1)} %table.1.refs_0_, f32[2,32,128]{2,1,0:T(8,128)S(1)} %get-tuple-element.48.refs_1_.refs_7_, f32[24,32,128]{2,1,0:T(8,128)S(1)} %get-tuple-element.49.refs_2_.refs_8_, f32[64,128]{1,0:T(8,128)S(1)} %get-tuple-element.70.refs_3_), custom_call_target="tpu_custom_call" | custom-call | tf_op jit(solution)/shard_map/own/pallas_call | solution.py:681
  37.7 1.3 %place.2.refs_0_ = f32[64,4096]{1,0:T(8,128)S(1)} custom-call(f32[64,2560]{1,0:T(8,128)S(1)} %own.6.refs_3_.refs_0_, f32[64,1024]{1,0:T(8,128)S(1)} %own.7.refs_6_.refs_1_, f32[64,512]{1,0:T(8,128)S(1)} %own.8.refs_2_, f32[192,128]{1,0:T(8,128)S(1)} %collective-permute-done.7.refs_1_.refs_3_, f32[192,128]{1,0:T(8,128)S(1)} %collective-permute-done.6.refs_1_.refs_4_, ...), custom_call_target="tpu_custom_call" | custom-call | tf_op jit(solution)/shard_map/place/pallas_call | solution.py:682
  39.0 0.5 sum.2
  39.5 1.0 %early.1 = (f32[8,64,128]{2,1,0:T(8,128)S(1)}, s32[8,128]{1,0:T(8,128)S(1)}, f32[4,8,128]{2,1,0:T(8,128)S(1)}) custom-call(bf16[1024,512]{1,0:T(8,128)(2,1)S(1)} %get-tuple-element.76.refs_0_, f32[24,128]{1,0:T(8,128)S(1)} %collective-permute-done.refs_0_.refs_1_, f32[24,128]{1,0:T(8,128)S(1)} %collective-permute-done.1.refs_1_.refs_2_, ...), custom_call_target="tpu_custom_call" | custom-call | tf_op jit(solution)/shard_map/early/pallas_call | solution.py:691
  40.6 0.7 %collective-permute-done.10.refs_1_.refs_3_ = f32[64,128]{1,0:T(8,128)S(1)} collective-permute-done((f32[64,128]{1,0:T(8,128)S(1)}, f32[64,128]{1,0:T(8,128)S(1)}, u32[]{:S(2)}, u32[]{:S(2)}) %collective-permute-start.10) | collective-permute-done | bytes 32800 | tf_op jit(solution)/shard_map/ppermute | solution.py:54
  41.3 0.4 late.1
  41.7 3.0 %collective-permute-start.12 = (f32[192,128]{1,0:T(8,128)S(1)}, f32[192,128]{1,0:T(8,128)S(1)}, u32[]{:S(2)}, u32[]{:S(2)}) collective-permute-start(f32[192,128]{1,0:T(8,128)S(1)} %get-tuple-element.80), channel_id=1, source_target_pairs={{0,15},{1,2},{2,1},{3,4},{4,3},{5,6},{6,5},{7,8},{8,7},{9,10},{10,... | collective-permute-start | bytes 294920 | tf_op jit(solution)/shard_map/ppermute | solution.py:54
  44.7 0.4 finish.1.refs_0_
  45.1 0.4 own_faces.3.refs_5_.refs_0_
  45.6 3.0 %own.9.refs_3_.refs_0_ = f32[64,2304]{1,0:T(8,128)S(1)} custom-call(bf16[1024,512]{1,0:T(8,128)(2,1)S(1)} %finish.1.refs_0_, f32[2,32,128]{2,1,0:T(8,128)S(1)} %get-tuple-element.74.refs_1_.refs_7_, f32[24,32,128]{2,1,0:T(8,128)S(1)} %get-tuple-element.75.refs_2_.refs_8_), custom_call_target="tpu_custom_call" | custom-call | tf_op jit(solution)/shard_map/own/pallas_call | solution.py:658
  48.5 0.5 reply_x.3.refs_2_
  49.0 0.7 %collective-permute-done.12.refs_0_.refs_2_.refs_5_ = f32[192,128]{1,0:T(8,128)S(1)} collective-permute-done((f32[192,128]{1,0:T(8,128)S(1)}, f32[192,128]{1,0:T(8,128)S(1)}, u32[]{:S(2)}, u32[]{:S(2)}) %collective-permute-start.12) | collective-permute-done | bytes 98336 | tf_op jit(solution)/shard_map/ppermute | solution.py:54
  49.9 1.1 %collective-permute-start.15 = (f32[192,128]{1,0:T(8,128)S(1)}, f32[192,128]{1,0:T(8,128)S(1)}, u32[]{:S(2)}, u32[]{:S(2)}) collective-permute-start(f32[192,128]{1,0:T(8,128)S(1)} %get-tuple-element.84.refs_3_), channel_id=1, source_target_pairs={{0,112},{16,32},{32,16},{48,64},{64,48},{80,96},{96,80},{112,0},{1... | collective-permute-start | bytes 294920 | tf_op jit(solution)/shard_map/ppermute | solution.py:54
  51.4 1.8 %collective-permute-start.16 = (f32[72,128]{1,0:T(8,128)S(1)}, f32[72,128]{1,0:T(8,128)S(1)}, u32[]{:S(2)}, u32[]{:S(2)}) collective-permute-start(f32[72,128]{1,0:T(8,128)S(1)} %get-tuple-element.85), channel_id=1, source_target_pairs={{0,112},{16,32},{32,16},{48,64},{64,48},{80,96},{96,80},{112,0},{1... | collective-permute-start | bytes 110600 | tf_op jit(solution)/shard_map/ppermute | solution.py:54
  53.2 1.3 %own.10.refs_6_.refs_1_ = f32[64,1024]{1,0:T(8,128)S(1)} custom-call(bf16[1024,512]{1,0:T(8,128)(2,1)S(1)} %finish.1.refs_0_, f32[2,32,128]{2,1,0:T(8,128)S(1)} %get-tuple-element.74.refs_1_.refs_7_, f32[24,32,128]{2,1,0:T(8,128)S(1)} %get-tuple-element.75.refs_2_.refs_8_, f32[64,256]{1,0:T(8,128)S(1)} %get-tuple-element.83.refs_3_.refs_0_), custom_call_target="tpu_custom_call" | custom-call | tf_op jit(solution)/shard_map/own/pallas_call | solution.py:668
  54.5 0.7 %collective-permute-done.15.refs_1_.refs_3_ = f32[192,128]{1,0:T(8,128)S(1)} collective-permute-done((f32[192,128]{1,0:T(8,128)S(1)}, f32[192,128]{1,0:T(8,128)S(1)}, u32[]{:S(2)}, u32[]{:S(2)}) %collective-permute-start.15) | collective-permute-done | bytes 98336 | tf_op jit(solution)/shard_map/ppermute | solution.py:54
  55.2 0.9 %collective-permute-done.16.refs_2_ = f32[72,128]{1,0:T(8,128)S(1)} collective-permute-done((f32[72,128]{1,0:T(8,128)S(1)}, f32[72,128]{1,0:T(8,128)S(1)}, u32[]{:S(2)}, u32[]{:S(2)}) %collective-permute-start.16) | collective-permute-done | bytes 36896 | tf_op jit(solution)/shard_map/ppermute | solution.py:54
  56.1 0.2 faces_far.3
  56.4 1.2 %collective-permute-done.17.refs_2_ = f32[64,128]{1,0:T(8,128)S(1)} collective-permute-done((f32[64,128]{1,0:T(8,128)S(1)}, f32[64,128]{1,0:T(8,128)S(1)}, u32[]{:S(2)}, u32[]{:S(2)}) %collective-permute-start.17) | collective-permute-done | bytes 32800 | tf_op jit(solution)/shard_map/ppermute | solution.py:58
  57.7 3.0 %collective-permute-start.18 = (f32[64,128]{1,0:T(8,128)S(1)}, f32[64,128]{1,0:T(8,128)S(1)}, u32[]{:S(2)}, u32[]{:S(2)}) collective-permute-start(f32[64,128]{1,0:T(8,128)S(1)} %get-tuple-element.90), channel_id=1, source_target_pairs={{0,15},{1,2},{2,1},{3,4},{4,3},{5,6},{6,5},{7,8},{8,7},{9,10},{10,... | collective-permute-start | bytes 98312 | tf_op jit(solution)/shard_map/ppermute | solution.py:54
  60.7 1.0 %own.11.refs_2_ = f32[64,768]{1,0:T(8,128)S(1)} custom-call(bf16[1024,512]{1,0:T(8,128)(2,1)S(1)} %finish.1.refs_0_, f32[2,32,128]{2,1,0:T(8,128)S(1)} %get-tuple-element.74.refs_1_.refs_7_, f32[24,32,128]{2,1,0:T(8,128)S(1)} %get-tuple-element.75.refs_2_.refs_8_, f32[64,128]{1,0:T(8,128)S(1)} %get-tuple-element.89.refs_3_), custom_call_target="tpu_custom_call" | custom-call | tf_op jit(solution)/shard_map/own/pallas_call | solution.py:681
  61.7 1.3 %place.3.refs_0_ = f32[64,4096]{1,0:T(8,128)S(1)} custom-call(f32[64,2304]{1,0:T(8,128)S(1)} %own.9.refs_3_.refs_0_, f32[64,1024]{1,0:T(8,128)S(1)} %own.10.refs_6_.refs_1_, f32[64,768]{1,0:T(8,128)S(1)} %own.11.refs_2_, f32[192,128]{1,0:T(8,128)S(1)} %collective-permute-done.15.refs_1_.refs_3_, f32[192,128]{1,0:T(8,128)S(1)} %collective-permute-done.14.refs_1_.refs_4_, ...), custom_call_target="tpu_custom_call" | custom-call | tf_op jit(solution)/shard_map/place/pallas_call | solution.py:682
  63.0 0.5 sum.3.summed
  63.5 1.5 %collective-permute-done.18.y_first = f32[64,128]{1,0:T(8,128)S(1)} collective-permute-done((f32[64,128]{1,0:T(8,128)S(1)}, f32[64,128]{1,0:T(8,128)S(1)}, u32[]{:S(2)}, u32[]{:S(2)}) %collective-permute-start.18) | collective-permute-done | bytes 32800 | tf_op jit(solution)/shard_map/ppermute | solution.py:54
  65.0 1.3 %last.1 = f32[64,16,256]{2,1,0:T(8,128)} custom-call(f32[64,4096]{1,0:T(8,128)S(1)} %sum.3.summed, f32[64,128]{1,0:T(8,128)S(1)} %collective-permute-done.18.y_first, f32[64,128]{1,0:T(8,128)S(1)} %collective-permute-done.19.y_second, f32[8,128]{1,0:T(8,128)S(1)} %get-tuple-element.59.refs_4_.refs_3_.refs_5_.scale), custom_call_target="tpu_custom_call" | custom-call | tf_op jit(solution)/shard_map/last/pallas_call | solution.py:705
  (27 shorter events, 1.2 us)
Async XLA Ops:
  1.2 4.4 %collective-permute-start = (f32[24,128]{1,0:T(8,128)S(1)}, f32[24,128]{1,0:T(8,128)S(1)}, u32[]{:S(2)}, u32[]{:S(2)}) collective-permute-start(f32[24,128]{1,0:T(8,128)S(1)} %get-tuple-element.51), channel_id=1, source_target_pairs={{0,112},{16,32},{32,16},{48,64},{64,48},{80,96},{96,80},{112,0},{1... | collective-permute-start | bytes 36872 | tf_op jit(solution)/shard_map/ppermute | solution.py:54
  3.8 1.8 %collective-permute-start.1 = (f32[24,128]{1,0:T(8,128)S(1)}, f32[24,128]{1,0:T(8,128)S(1)}, u32[]{:S(2)}, u32[]{:S(2)}) collective-permute-start(f32[24,128]{1,0:T(8,128)S(1)} %get-tuple-element.52), channel_id=1, source_target_pairs={{0,16},{16,0},{32,48},{48,32},{64,80},{80,64},{96,112},{112,96},{1... | collective-permute-start | bytes 36872 | tf_op jit(solution)/shard_map/ppermute | solution.py:58
  5.7 9.8 %collective-permute-start.2 = (f32[24,128]{1,0:T(8,128)S(1)}, f32[24,128]{1,0:T(8,128)S(1)}, u32[]{:S(2)}, u32[]{:S(2)}) collective-permute-start(f32[24,128]{1,0:T(8,128)S(1)} %get-tuple-element.55), channel_id=1, source_target_pairs={{0,15},{1,2},{2,1},{3,4},{4,3},{5,6},{6,5},{7,8},{8,7},{9,10},{10,... | collective-permute-start | bytes 36872 | tf_op jit(solution)/shard_map/ppermute | solution.py:54
  12.0 3.7 %collective-permute-start.3 = (f32[24,128]{1,0:T(8,128)S(1)}, f32[24,128]{1,0:T(8,128)S(1)}, u32[]{:S(2)}, u32[]{:S(2)}) collective-permute-start(f32[24,128]{1,0:T(8,128)S(1)} %get-tuple-element.56), channel_id=1, source_target_pairs={{0,1},{1,0},{2,3},{3,2},{4,5},{5,4},{6,7},{7,6},{8,9},{9,8},{10,11... | collective-permute-start | bytes 36872 | tf_op jit(solution)/shard_map/ppermute | solution.py:58
  16.7 8.0 %collective-permute-start.4 = (f32[192,128]{1,0:T(8,128)S(1)}, f32[192,128]{1,0:T(8,128)S(1)}, u32[]{:S(2)}, u32[]{:S(2)}) collective-permute-start(f32[192,128]{1,0:T(8,128)S(1)} %get-tuple-element.57), channel_id=1, source_target_pairs={{0,15},{1,2},{2,1},{3,4},{4,3},{5,6},{6,5},{7,8},{8,7},{9,10},{10,... | collective-permute-start | bytes 294920 | tf_op jit(solution)/shard_map/ppermute | solution.py:54
  20.1 4.6 %collective-permute-start.5 = (f32[192,128]{1,0:T(8,128)S(1)}, f32[192,128]{1,0:T(8,128)S(1)}, u32[]{:S(2)}, u32[]{:S(2)}) collective-permute-start(f32[192,128]{1,0:T(8,128)S(1)} %get-tuple-element.58), channel_id=1, source_target_pairs={{0,1},{1,0},{2,3},{3,2},{4,5},{5,4},{6,7},{7,6},{8,9},{9,8},{10,11... | collective-permute-start | bytes 294920 | tf_op jit(solution)/shard_map/ppermute | solution.py:58
  20.6 3.1 %copy-start = (f32[16,256]{1,0:T(8,128)S(1)}, f32[16,256]{1,0:T(8,128)}, u32[]{:S(2)}) copy-start(f32[16,256]{1,0:T(8,128)} %refs_9_.3) | copy-start | bytes 49156
  24.8 2.7 %collective-permute-start.6 = (f32[192,128]{1,0:T(8,128)S(1)}, f32[192,128]{1,0:T(8,128)S(1)}, u32[]{:S(2)}, u32[]{:S(2)}) collective-permute-start(f32[192,128]{1,0:T(8,128)S(1)} %get-tuple-element.60), channel_id=1, source_target_pairs={{0,16},{16,0},{32,48},{48,32},{64,80},{80,64},{96,112},{112,96},{1... | collective-permute-start | bytes 294920 | tf_op jit(solution)/shard_map/ppermute | solution.py:58
  24.9 6.1 %collective-permute-start.7 = (f32[192,128]{1,0:T(8,128)S(1)}, f32[192,128]{1,0:T(8,128)S(1)}, u32[]{:S(2)}, u32[]{:S(2)}) collective-permute-start(f32[192,128]{1,0:T(8,128)S(1)} %get-tuple-element.62.refs_3_), channel_id=1, source_target_pairs={{0,112},{16,32},{32,16},{48,64},{64,48},{80,96},{96,80},{112,0},{1... | collective-permute-start | bytes 294920 | tf_op jit(solution)/shard_map/ppermute | solution.py:54
  27.7 4.7 %collective-permute-start.8 = (f32[72,128]{1,0:T(8,128)S(1)}, f32[72,128]{1,0:T(8,128)S(1)}, u32[]{:S(2)}, u32[]{:S(2)}) collective-permute-start(f32[72,128]{1,0:T(8,128)S(1)} %get-tuple-element.63), channel_id=1, source_target_pairs={{0,112},{16,32},{32,16},{48,64},{64,48},{80,96},{96,80},{112,0},{1... | collective-permute-start | bytes 110600 | tf_op jit(solution)/shard_map/ppermute | solution.py:54
  32.6 1.3 %collective-permute-start.9 = (f32[64,128]{1,0:T(8,128)S(1)}, f32[64,128]{1,0:T(8,128)S(1)}, u32[]{:S(2)}, u32[]{:S(2)}) collective-permute-start(f32[64,128]{1,0:T(8,128)S(1)} %get-tuple-element.69), channel_id=1, source_target_pairs={{0,16},{16,0},{32,48},{48,32},{64,80},{80,64},{96,112},{112,96},{1... | collective-permute-start | bytes 98312 | tf_op jit(solution)/shard_map/ppermute | solution.py:58
  34.0 7.3 %collective-permute-start.10 = (f32[64,128]{1,0:T(8,128)S(1)}, f32[64,128]{1,0:T(8,128)S(1)}, u32[]{:S(2)}, u32[]{:S(2)}) collective-permute-start(f32[64,128]{1,0:T(8,128)S(1)} %get-tuple-element.73), channel_id=1, source_target_pairs={{0,15},{1,2},{2,1},{3,4},{4,3},{5,6},{6,5},{7,8},{8,7},{9,10},{10,... | collective-permute-start | bytes 98312 | tf_op jit(solution)/shard_map/ppermute | solution.py:54
  37.0 4.3 %collective-permute-start.11 = (f32[64,128]{1,0:T(8,128)S(1)}, f32[64,128]{1,0:T(8,128)S(1)}, u32[]{:S(2)}, u32[]{:S(2)}) collective-permute-start(f32[64,128]{1,0:T(8,128)S(1)} %get-tuple-element.70.refs_3_), channel_id=1, source_target_pairs={{0,1},{1,0},{2,3},{3,2},{4,5},{5,4},{6,7},{7,6},{8,9},{9,8},{10,11... | collective-permute-start | bytes 98312 | tf_op jit(solution)/shard_map/ppermute | solution.py:58
  41.7 8.0 %collective-permute-start.12 = (f32[192,128]{1,0:T(8,128)S(1)}, f32[192,128]{1,0:T(8,128)S(1)}, u32[]{:S(2)}, u32[]{:S(2)}) collective-permute-start(f32[192,128]{1,0:T(8,128)S(1)} %get-tuple-element.80), channel_id=1, source_target_pairs={{0,15},{1,2},{2,1},{3,4},{4,3},{5,6},{6,5},{7,8},{8,7},{9,10},{10,... | collective-permute-start | bytes 294920 | tf_op jit(solution)/shard_map/ppermute | solution.py:54
  44.7 5.0 %collective-permute-start.13 = (f32[192,128]{1,0:T(8,128)S(1)}, f32[192,128]{1,0:T(8,128)S(1)}, u32[]{:S(2)}, u32[]{:S(2)}) collective-permute-start(f32[192,128]{1,0:T(8,128)S(1)} %get-tuple-element.81), channel_id=1, source_target_pairs={{0,1},{1,0},{2,3},{3,2},{4,5},{5,4},{6,7},{7,6},{8,9},{9,8},{10,11... | collective-permute-start | bytes 294920 | tf_op jit(solution)/shard_map/ppermute | solution.py:58
  49.8 1.4 %collective-permute-start.14 = (f32[192,128]{1,0:T(8,128)S(1)}, f32[192,128]{1,0:T(8,128)S(1)}, u32[]{:S(2)}, u32[]{:S(2)}) collective-permute-start(f32[192,128]{1,0:T(8,128)S(1)} %get-tuple-element.82), channel_id=1, source_target_pairs={{0,16},{16,0},{32,48},{48,32},{64,80},{80,64},{96,112},{112,96},{1... | collective-permute-start | bytes 294920 | tf_op jit(solution)/shard_map/ppermute | solution.py:58
  49.9 5.3 %collective-permute-start.15 = (f32[192,128]{1,0:T(8,128)S(1)}, f32[192,128]{1,0:T(8,128)S(1)}, u32[]{:S(2)}, u32[]{:S(2)}) collective-permute-start(f32[192,128]{1,0:T(8,128)S(1)} %get-tuple-element.84.refs_3_), channel_id=1, source_target_pairs={{0,112},{16,32},{32,16},{48,64},{64,48},{80,96},{96,80},{112,0},{1... | collective-permute-start | bytes 294920 | tf_op jit(solution)/shard_map/ppermute | solution.py:54
  51.4 4.7 %collective-permute-start.16 = (f32[72,128]{1,0:T(8,128)S(1)}, f32[72,128]{1,0:T(8,128)S(1)}, u32[]{:S(2)}, u32[]{:S(2)}) collective-permute-start(f32[72,128]{1,0:T(8,128)S(1)} %get-tuple-element.85), channel_id=1, source_target_pairs={{0,112},{16,32},{32,16},{48,64},{64,48},{80,96},{96,80},{112,0},{1... | collective-permute-start | bytes 110600 | tf_op jit(solution)/shard_map/ppermute | solution.py:54
  56.3 1.3 %collective-permute-start.17 = (f32[64,128]{1,0:T(8,128)S(1)}, f32[64,128]{1,0:T(8,128)S(1)}, u32[]{:S(2)}, u32[]{:S(2)}) collective-permute-start(f32[64,128]{1,0:T(8,128)S(1)} %get-tuple-element.88), channel_id=1, source_target_pairs={{0,16},{16,0},{32,48},{48,32},{64,80},{80,64},{96,112},{112,96},{1... | collective-permute-start | bytes 98312 | tf_op jit(solution)/shard_map/ppermute | solution.py:58
  57.7 7.3 %collective-permute-start.18 = (f32[64,128]{1,0:T(8,128)S(1)}, f32[64,128]{1,0:T(8,128)S(1)}, u32[]{:S(2)}, u32[]{:S(2)}) collective-permute-start(f32[64,128]{1,0:T(8,128)S(1)} %get-tuple-element.90), channel_id=1, source_target_pairs={{0,15},{1,2},{2,1},{3,4},{4,3},{5,6},{6,5},{7,8},{8,7},{9,10},{10,... | collective-permute-start | bytes 98312 | tf_op jit(solution)/shard_map/ppermute | solution.py:54
  60.7 4.3 %collective-permute-start.19 = (f32[64,128]{1,0:T(8,128)S(1)}, f32[64,128]{1,0:T(8,128)S(1)}, u32[]{:S(2)}, u32[]{:S(2)}) collective-permute-start(f32[64,128]{1,0:T(8,128)S(1)} %get-tuple-element.89.refs_3_), channel_id=1, source_target_pairs={{0,1},{1,0},{2,3},{3,2},{4,5},{5,4},{6,7},{7,6},{8,9},{9,8},{10,11... | collective-permute-start | bytes 98312 | tf_op jit(solution)/shard_map/ppermute | solution.py:58

commit v2 on v1

--- a/solution.py
+++ b/solution.py
@@ -14,7 +14,7 @@
 NODES = 16
 POINTS = 4096
 TILES = POINTS // 128
-PIECES = (((0, 10), (10, 14), (14, 16)), ((0, 9), (9, 13), (13, 16)))
+PIECES = (((0, 10), (10, 16)), ((0, 9), (9, 16)))
 GLL_NODES = (-1.0, -0.4472135954999579, 0.4472135954999579, 1.0)
 REMOTE = (0, 1, 2, 3, 5, 6, 7, 8)
 BF16 = jnp.bfloat16
@@ -302,7 +302,7 @@
             table[n * F + q : n * F + q + 16, E : 2 * E] = low
 
 
-def column_body(x_first, x_second, mid, mass_faces, first, second):
+def column_body(x_first, x_second, mid, mass_faces, first, second, kept):
     low, high = from_swaps("fx", x_first[...], x_second[...])
     masses = summed_faces(mass_faces[:, 128:256], low[8:16], high[8:16])[6:7]
     rows = lax.broadcasted_iota(jnp.int32, (8, 128), 0)
@@ -312,6 +312,7 @@
         center = jnp.where(rows == 6, masses, mid[block, :])
         columns.append(jnp.concatenate([high[block], center, low[block]], axis=0))
     first[...], second[...] = to_swaps("fy", *columns)
+    kept[...] = first[...]
 
 
 def row_body(y_first, y_second, own, near, far):
@@ -408,14 +409,49 @@
         shares[a] = jnp.where(element % 16 == 0, weights[4 * a], share)
 
 
-def late_body(values, lanes, shares, y_first, y_second, scale, far, near):
-    halo = halo_of(*from_swaps("fy", y_first[...], y_second[...])) * scale[0:1, :]
-    for d in range(6):
+def shared(values, lanes, shares, halo, rows):
+    for d in rows:
         index = jnp.broadcast_to(lanes[d : d + 1, :], (F, 128))
         value = values[d]
         for a in range(4):
             value = value + pick_lanes(halo, index + 16 * a) * shares[a, d : d + 1, :]
-        (far if d < 3 else near)[d % 3 * F : (d % 3 + 1) * F, :] = value
+        yield value
+
+
+def late_far_body(values, lanes, shares, near, scale, message):
+    even = lax.axis_index("fy") % 2 == 0
+    block = pltpu.roll(near[...], 64, 1) * scale[0:1, :]
+    lane = lane_index(F)
+    halo = jnp.where(jnp.where(even, lane - 64, 63 - lane) >= 0, block, 0.0)
+    for k, value in enumerate(shared(values, lanes, shares, halo, range(3))):
+        message[k * F : (k + 1) * F, :] = value
+
+
+def late_near_body(values, lanes, shares, far, near, scale, message):
+    halo = halo_of(*from_swaps("fy", far[...], near[...])) * scale[0:1, :]
+    for k, value in enumerate(shared(values, lanes, shares, halo, range(3, 6))):
+        message[k * F : (k + 1) * F, :] = value
+
+
+def fix_body(far, asked, rims, scale, result):
+    even = lax.axis_index("fy") % 2 == 0
+    pick, cx, cy = [
+        jnp.concatenate([asked[k * 8 + 3 + q : k * 8 + 4 + q, :] for k in range(3)], axis=0)
+        for q in range(3)
+    ]
+    weights = weights_of(cx, cy)
+    element = pick.astype(jnp.int32)
+    on_face = element % 16 == jnp.where(even, 15, 0)
+    lanes = element // 16 + jnp.where(even, 0, 64)
+    own = rims[...] * scale[0:1, :]
+    for k in range(3):
+        index = jnp.broadcast_to(lanes[k : k + 1], (F, 128))
+        value = far[k * F : (k + 1) * F, :]
+        for a in range(4):
+            weight = jnp.where(even, weights[4 * a + 3], weights[4 * a])
+            weight = jnp.where(on_face, weight, 0.0)
+            value = value + pick_lanes(own, index + 16 * a) * weight[k : k + 1]
+        result[k * F : (k + 1) * F, :] = value
 
 
 def own_body(begin, table, picks, factors, result):
@@ -433,7 +469,7 @@
         return carry
 
     count = result.shape[1] // E
-    lax.fori_loop(0, count, block, 0, unroll=5 if count == 10 else 3 if count == 9 else count)
+    lax.fori_loop(0, count, block, 0, unroll=5 if count == 10 else 3 if count in (6, 9) else count)
 
 
 def stacked(blocks):
@@ -508,7 +544,7 @@
 
 
 def place_body(
-    s, own_a, own_b, own_c, x_first, x_second, y_first, y_second, picks, factors, mass, result
+    s, own_a, own_b, x_first, x_second, y_first, y_second, picks, factors, mass, result
 ):
     answers = arrived(x_first, x_second, y_first, y_second)
     for n in range(NODES):
@@ -517,17 +553,18 @@
             jnp.concatenate([factors[NODES + d, t, :] for t in tiles], axis=1) for d in range(8)
         ]
         moved = placed(answers, [picks[1, t, :] for t in tiles], masks)
-        for ref, (begin, end) in zip((own_a, own_b, own_c), PIECES[s]):
+        for ref, (begin, end) in zip((own_a, own_b), PIECES[s]):
             if begin <= n < end:
                 own = ref[:, (n - begin) * E : (n - begin + 1) * E]
         result[:, n * E : (n + 1) * E] = (own + moved) * mass[n : n + 1, :]
 
 
-def rim_body(along_y, x_first, x_second, first, second):
+def rim_body(along_y, x_first, x_second, first, second, kept):
     low, high = from_swaps("fx", x_first[...], x_second[...])
     result = summed_faces(along_y[...], low, high)
     first[...] = result
     second[...] = result
+    kept[...] = result
 
 
 def scale_body(mass, x_first, x_second, y_first, y_second, inverse, on_faces):
@@ -628,10 +665,10 @@
             after=after,
         )
 
-    asked += swap(
-        "fy",
-        *call(column_body, [ask] * 2, "column", count=4)(*asked, mid, mass_faces),
-    )
+    column_far, column_near, column_kept = call(column_body, [ask] * 3, "column", count=4)(
+        *asked, mid, mass_faces
+    )
+    asked += swap("fy", column_far, column_near)
     table = call(
         table_body,
         table_shape,
@@ -676,14 +713,17 @@
             face_far_body, [face] * 3, "faces_far", count=6, after=2
         )(partial, far, faces_in, far_sent, face_picks, mass_faces, own_b, ordered_lists[1][2])
         edges_x = (other, swap_near("fx", along_x))
-        first, second = call(rim_body, [face] * 2, "rim", count=3)(along_y, *edges_x)
-        edges_y = swap("fy", first, second)
-        own_c = interpolate(s, 2, after=1)(table, picks, factors, second)
         weighted = call(
-            lambda *refs, s=s: place_body(s, *refs), shape((F, POINTS)), "place", count=10
-        )(
-            own_a, own_b, own_c, far, near, *answers_y, picks, factors, node_mass
+            lambda *refs, s=s: place_body(s, *refs),
+            shape((F, POINTS)),
+            "place",
+            count=9,
+            after=1,
+        )(own_a, own_b, far, near, *answers_y, picks, factors, node_mass, other)
+        rims_far, rims_near, rims_kept = call(rim_body, [face] * 3, "rim", count=3, after=1)(
+            along_y, *edges_x, weighted
         )
+        edges_y = swap("fy", rims_far, rims_near)
         if s == 0:
             summed, early_table = call(
                 sum_body, [shape((F, POINTS)), table_shape], "sum", count=4
@@ -694,10 +734,12 @@
                 "early",
                 count=5,
             )(early_table, *asked)
-            far, near = call(late_body, [answers] * 2, "late", count=6)(
-                *early, *edges_y, scale
-            )
-            answers_y = swap("fy", far, near)
+            far = call(late_far_body, answers, "late_far", count=5)(*early, edges_y[1], scale)
+            far = swap_far("fy", far)
+            near = call(late_near_body, answers, "late_near", count=6)(*early, *edges_y, scale)
+            near = swap_near("fy", near)
+            far = call(fix_body, answers, "fix", count=4)(far, column_kept, rims_kept, scale)
+            answers_y = (far, near)
         else:
             summed = call(sum_body, shape((F, POINTS)), "sum", count=4)(
                 weighted, *edges_x, inverse

time: 66.7 us -> 66 us (0.990)
  waiting for transfers between devices: 10.9 us -> 7.99 us
  starting transfers between devices: 28.2 us -> 29.3 us
  Pallas kernels: 26.8 us -> 27.6 us
    ppermute x10, waiting for transfers between devices: 2.83 us -> 0.25 us  [swap_near(): lax.ppermute(block, axis, [(i, i ^ 1) for i in range(lax.axis_size(axis))])]
    pallas_call x2, Pallas kernels: 2.51 us -> 4.05 us  [per_device(): own_b = interpolate(s, 1, after=1)(table, picks, factors, partial)]
    ppermute x10, starting transfers between devices: 0.36 us -> 1.64 us  [swap_near(): lax.ppermute(block, axis, [(i, i ^ 1) for i in range(lax.axis_size(axis))])]
    pallas_call x6, Pallas kernels: 2.44 us -> 1.71 us  [the longest x2 0.87 us: per_device(): call(rim_body, [face] * 3, 'rim', count=3, after=1)]
  transfers between devices with their start and end apart: 20 -> 20, of which waited for: 12 -> 7; matrix products, arithmetic and copies ran while one was open for 0% -> 0% of each run, Pallas kernels for 33% -> 35%
where the time goes in v2:
time: 66 us; the launch traced here: 65.5 us
  starting transfers between devices  29.3 us (44%)
  Pallas kernels  27.6 us (42%)
  waiting for transfers between devices  7.99 us (12%)
    ppermute x10, starting transfers between devices, swap_far(): return lax.ppermute(block, axis, pairs)  27.7 us
    ppermute x10, waiting for transfers between devices, swap_far(): return lax.ppermute(block, axis, pairs)  7.74 us
    pallas_call x2, Pallas kernels, per_device(): own_a = interpolate(s, 0)(table, picks, factors)  6.04 us
    pallas_call x2, Pallas kernels, per_device(): own_b = interpolate(s, 1, after=1)(table, picks, factors, partial)  4.05 us
    pallas_call x2, Pallas kernels, per_device(): call(lambda *refs, s=s: place_body(s, *refs), shape((F, POINTS)), 'place'...  2.56 us
    pallas_call x1, Pallas kernels, per_device(): call(order_body, requests + [shape((8, POINTS), jnp.int32), shape((8, 128...  1.91 us
    ppermute x10, starting transfers between devices, swap_near(): lax.ppermute(block, axis, [(i, i ^ 1) for i in range(lax.axis_size(axis))])  1.64 us
    pallas_call x1, Pallas kernels, per_device(): call(table_body, table_shape, 'table', hbm=(0,), count=1, scratch=[pltpu....  1.54 us
  transfers between devices with their start and end apart: 20, of which 7 were waited for; matrix products, arithmetic and copies ran while one was open for 0% of the time, Pallas kernels for 35%

profile of v2, /device:TPU:0, one launch (start us, length us, event | category | flops | bytes accessed | tf_op | source)
XLA Modules:
  0.0 65.5 jit_solution(2269469166974520294)
XLA Ops:
  0.0 1.2 %asks.1 = (f32[24,128]{1,0:T(8,128)S(1)}, f32[24,128]{1,0:T(8,128)S(1)}, f32[24,128]{1,0:T(8,128)S(1)}, f32[8,256]{1,0:T(8,128)S(1)}) custom-call(s32[2,1,10]{2,1,0:T(1,128)} %refs_0_.6, s32[2,4096]{1,0:T(2,128)} %refs_1_.3, s32[2,2,4096]{2,1,0:T(2,128)} %refs_2_.3, f32[16,256]{1,0:T(8,128)} %refs_8_.3), custom_call_target="tpu_custom_call" | custom-call | tf_op jit(solution)/shard_map/asks/pallas_call | solution.py:631
  1.2 2.6 %collective-permute-start = (f32[24,128]{1,0:T(8,128)S(1)}, f32[24,128]{1,0:T(8,128)S(1)}, u32[]{:S(2)}, u32[]{:S(2)}) collective-permute-start(f32[24,128]{1,0:T(8,128)S(1)} %get-tuple-element.51), channel_id=1, source_target_pairs={{0,112},{16,32},{32,16},{48,64},{64,48},{80,96},{96,80},{112,0},{1... | collective-permute-start | bytes 36872 | tf_op jit(solution)/shard_map/ppermute | solution.py:54
  3.8 1.8 %collective-permute-done.refs_0_.refs_1_ = f32[24,128]{1,0:T(8,128)S(1)} collective-permute-done((f32[24,128]{1,0:T(8,128)S(1)}, f32[24,128]{1,0:T(8,128)S(1)}, u32[]{:S(2)}, u32[]{:S(2)}) %collective-permute-start) | collective-permute-done | bytes 12320 | tf_op jit(solution)/shard_map/ppermute | solution.py:54
  5.7 6.4 %collective-permute-start.2 = (f32[24,128]{1,0:T(8,128)S(1)}, f32[24,128]{1,0:T(8,128)S(1)}, u32[]{:S(2)}, u32[]{:S(2)}) collective-permute-start(f32[24,128]{1,0:T(8,128)S(1)} %get-tuple-element.55), channel_id=1, source_target_pairs={{0,15},{1,2},{2,1},{3,4},{4,3},{5,6},{6,5},{7,8},{8,7},{9,10},{10,... | collective-permute-start | bytes 36872 | tf_op jit(solution)/shard_map/ppermute | solution.py:54
  12.0 1.9 %order.2 = (f32[2,32,128]{2,1,0:T(8,128)S(1)}, f32[24,32,128]{2,1,0:T(8,128)S(1)}, f32[8,256]{1,0:T(8,128)S(1)}, s32[8,4096]{1,0:T(8,128)S(1)}, s32[8,128]{1,0:T(8,128)S(1)}) custom-call(s32[2,1,10]{2,1,0:T(1,128)} %refs_0_.6, s32[2,1,4096]{2,1,0:T(1,128)} %refs_1_.2, s32[2,4096]{1,0:T(2,128)} %refs_1_.3, s32[2,2,4096]{2,1,0:T(2,128)} %refs_2_.3), custom_call_target="tpu_custom_call" | custom-call | tf_op jit(solution)/shard_map/order/pallas_call | solution.py:647
  13.9 1.5 %table.1.refs_0_ = bf16[1024,512]{1,0:T(8,128)(2,1)S(1)} custom-call(f32[64,16,256]{2,1,0:T(8,128)} %refs_0_.4), custom_call_target="tpu_custom_call" | custom-call | tf_op jit(solution)/shard_map/table/pallas_call | solution.py:672
  15.5 0.2 collective-permute-done.3.refs_4_
  15.7 1.0 %reply_y.1 = (f32[192,128]{1,0:T(8,128)S(1)}, f32[192,128]{1,0:T(8,128)S(1)}) custom-call(bf16[1024,512]{1,0:T(8,128)(2,1)S(1)} %table.1.refs_0_, f32[24,128]{1,0:T(8,128)S(1)} %collective-permute-done.refs_0_.refs_1_, f32[24,128]{1,0:T(8,128)S(1)} %collective-permute-done.1.refs_1_.refs_2_, f32[24,128]{1,0:T(8,128)S(1)} %collective-permute-done.2.refs_3_, ...), custom_call_target="tpu_custom_call" | custom-call | tf_op jit(solution)/shard_map/reply_y/pallas_call | solution.py:680
  16.7 3.4 %collective-permute-start.4 = (f32[192,128]{1,0:T(8,128)S(1)}, f32[192,128]{1,0:T(8,128)S(1)}, u32[]{:S(2)}, u32[]{:S(2)}) collective-permute-start(f32[192,128]{1,0:T(8,128)S(1)} %get-tuple-element.57), channel_id=1, source_target_pairs={{0,15},{1,2},{2,1},{3,4},{4,3},{5,6},{6,5},{7,8},{8,7},{9,10},{10,... | collective-permute-start | bytes 294920 | tf_op jit(solution)/shard_map/ppermute | solution.py:54
  20.1 0.4 own_faces.2.refs_5_.refs_0_
  20.6 3.1 %own.4.refs_3_.refs_0_ = f32[64,2560]{1,0:T(8,128)S(1)} custom-call(bf16[1024,512]{1,0:T(8,128)(2,1)S(1)} %table.1.refs_0_, f32[2,32,128]{2,1,0:T(8,128)S(1)} %get-tuple-element.48.refs_1_.refs_6_, f32[24,32,128]{2,1,0:T(8,128)S(1)} %get-tuple-element.49.refs_2_.refs_7_), custom_call_target="tpu_custom_call" | custom-call | tf_op jit(solution)/shard_map/own/pallas_call | solution.py:695
  23.7 0.3 scale.1
  24.0 0.5 reply_x.2.refs_2_
  24.4 0.3 collective-permute-done.4.refs_0_.refs_2_.refs_4_
  24.9 2.6 %collective-permute-start.7 = (f32[192,128]{1,0:T(8,128)S(1)}, f32[192,128]{1,0:T(8,128)S(1)}, u32[]{:S(2)}, u32[]{:S(2)}) collective-permute-start(f32[192,128]{1,0:T(8,128)S(1)} %get-tuple-element.62.refs_3_), channel_id=1, source_target_pairs={{0,112},{16,32},{32,16},{48,64},{64,48},{80,96},{96,80},{112,0},{1... | collective-permute-start | bytes 294920 | tf_op jit(solution)/shard_map/ppermute | solution.py:54
  27.4 0.2 faces_near.2
  27.7 1.0 %collective-permute-start.8 = (f32[72,128]{1,0:T(8,128)S(1)}, f32[72,128]{1,0:T(8,128)S(1)}, u32[]{:S(2)}, u32[]{:S(2)}) collective-permute-start(f32[72,128]{1,0:T(8,128)S(1)} %get-tuple-element.63), channel_id=1, source_target_pairs={{0,112},{16,32},{32,16},{48,64},{64,48},{80,96},{96,80},{112,0},{1... | collective-permute-start | bytes 110600 | tf_op jit(solution)/shard_map/ppermute | solution.py:54
  28.7 2.0 %own.5.refs_6_.refs_1_ = f32[64,1536]{1,0:T(8,128)S(1)} custom-call(bf16[1024,512]{1,0:T(8,128)(2,1)S(1)} %table.1.refs_0_, f32[2,32,128]{2,1,0:T(8,128)S(1)} %get-tuple-element.48.refs_1_.refs_6_, f32[24,32,128]{2,1,0:T(8,128)S(1)} %get-tuple-element.49.refs_2_.refs_7_, f32[64,256]{1,0:T(8,128)S(1)} %get-tuple-element.61.refs_3_.refs_2_.refs_0_), custom_call_target="tpu_custom_call" | custom-call | tf_op jit(solution)/shard_map/own/pallas_call | solution.py:705
  30.7 1.0 %order.3 = (f32[2,32,128]{2,1,0:T(8,128)S(1)}, f32[24,32,128]{2,1,0:T(8,128)S(1)}, f32[8,256]{1,0:T(8,128)S(1)}) custom-call(s32[8,4096]{1,0:T(8,128)S(1)} %get-tuple-element.64.refs_0_, s32[8,128]{1,0:T(8,128)S(1)} %get-tuple-element.65.refs_1_, f32[64,256]{1,0:T(8,128)S(1)} %get-tuple-element.61.refs_3_.refs_2_.refs_0_), custom_call_target="tpu_custom_call" | custom-call | tf_op jit(solution)/shard_map/order/pallas_call | solution.py:708
  31.7 0.7 %collective-permute-done.8.refs_2_ = f32[72,128]{1,0:T(8,128)S(1)} collective-permute-done((f32[72,128]{1,0:T(8,128)S(1)}, f32[72,128]{1,0:T(8,128)S(1)}, u32[]{:S(2)}, u32[]{:S(2)}) %collective-permute-start.8) | collective-permute-done | bytes 36896 | tf_op jit(solution)/shard_map/ppermute | solution.py:54
  32.3 0.2 faces_far.2
  32.7 1.3 %place.2.refs_0_.refs_3_ = f32[64,4096]{1,0:T(8,128)S(1)} custom-call(f32[64,2560]{1,0:T(8,128)S(1)} %own.4.refs_3_.refs_0_, f32[64,1536]{1,0:T(8,128)S(1)} %own.5.refs_6_.refs_1_, f32[192,128]{1,0:T(8,128)S(1)} %collective-permute-done.7.refs_1_.refs_2_, f32[192,128]{1,0:T(8,128)S(1)} %collective-permute-done.6.refs_1_.refs_3_, ...), custom_call_target="tpu_custom_call" | custom-call | tf_op jit(solution)/shard_map/place/pallas_call | solution.py:716
  34.0 0.1 rim.2
  34.1 1.2 %collective-permute-start.11 = (f32[64,128]{1,0:T(8,128)S(1)}, f32[64,128]{1,0:T(8,128)S(1)}, u32[]{:S(2)}, u32[]{:S(2)}) collective-permute-start(f32[64,128]{1,0:T(8,128)S(1)} %get-tuple-element.73), channel_id=1, source_target_pairs={{0,1},{1,0},{2,3},{3,2},{4,5},{5,4},{6,7},{7,6},{8,9},{9,8},{10,11... | collective-permute-start | bytes 98312 | tf_op jit(solution)/shard_map/ppermute | solution.py:58
  35.3 2.1 %collective-permute-start.10 = (f32[64,128]{1,0:T(8,128)S(1)}, f32[64,128]{1,0:T(8,128)S(1)}, u32[]{:S(2)}, u32[]{:S(2)}) collective-permute-start(f32[64,128]{1,0:T(8,128)S(1)} %get-tuple-element.72), channel_id=1, source_target_pairs={{0,15},{1,2},{2,1},{3,4},{4,3},{5,6},{6,5},{7,8},{8,7},{9,10},{10,... | collective-permute-start | bytes 98312 | tf_op jit(solution)/shard_map/ppermute | solution.py:54
  37.4 0.5 sum.2
  37.9 1.0 %early.1 = (f32[8,64,128]{2,1,0:T(8,128)S(1)}, s32[8,128]{1,0:T(8,128)S(1)}, f32[4,8,128]{2,1,0:T(8,128)S(1)}) custom-call(bf16[1024,512]{1,0:T(8,128)(2,1)S(1)} %get-tuple-element.76.refs_0_, f32[24,128]{1,0:T(8,128)S(1)} %collective-permute-done.refs_0_.refs_1_, f32[24,128]{1,0:T(8,128)S(1)} %collective-permute-done.1.refs_1_.refs_2_, ...), custom_call_target="tpu_custom_call" | custom-call | tf_op jit(solution)/shard_map/early/pallas_call | solution.py:731
  38.9 0.3 late_far.1
  39.2 3.4 %collective-permute-start.12 = (f32[192,128]{1,0:T(8,128)S(1)}, f32[192,128]{1,0:T(8,128)S(1)}, u32[]{:S(2)}, u32[]{:S(2)}) collective-permute-start(f32[192,128]{1,0:T(8,128)S(1)} %late_far.1), channel_id=1, source_target_pairs={{0,15},{1,2},{2,1},{3,4},{4,3},{5,6},{6,5},{7,8},{8,7},{9,10},{10,... | collective-permute-start | bytes 294920 | tf_op jit(solution)/shard_map/ppermute | solution.py:54
  42.6 0.3 late_near.1
  42.9 0.4 finish.1.refs_0_
  43.3 0.4 own_faces.3.refs_5_.refs_0_
  43.8 3.0 %own.6.refs_3_.refs_0_ = f32[64,2304]{1,0:T(8,128)S(1)} custom-call(bf16[1024,512]{1,0:T(8,128)(2,1)S(1)} %finish.1.refs_0_, f32[2,32,128]{2,1,0:T(8,128)S(1)} %get-tuple-element.74.refs_1_.refs_6_, f32[24,32,128]{2,1,0:T(8,128)S(1)} %get-tuple-element.75.refs_2_.refs_7_), custom_call_target="tpu_custom_call" | custom-call | tf_op jit(solution)/shard_map/own/pallas_call | solution.py:695
  46.7 0.5 reply_x.3.refs_2_
  47.2 0.3 collective-permute-done.12.refs_0_
  47.5 0.2 fix.1.refs_0_.refs_2_.refs_4_
  47.9 1.6 %collective-permute-start.15 = (f32[192,128]{1,0:T(8,128)S(1)}, f32[192,128]{1,0:T(8,128)S(1)}, u32[]{:S(2)}, u32[]{:S(2)}) collective-permute-start(f32[192,128]{1,0:T(8,128)S(1)} %get-tuple-element.84.refs_3_), channel_id=1, source_target_pairs={{0,112},{16,32},{32,16},{48,64},{64,48},{80,96},{96,80},{112,0},{1... | collective-permute-start | bytes 294920 | tf_op jit(solution)/shard_map/ppermute | solution.py:54
  49.5 0.2 faces_near.3
  49.8 1.5 %collective-permute-start.16 = (f32[72,128]{1,0:T(8,128)S(1)}, f32[72,128]{1,0:T(8,128)S(1)}, u32[]{:S(2)}, u32[]{:S(2)}) collective-permute-start(f32[72,128]{1,0:T(8,128)S(1)} %get-tuple-element.85), channel_id=1, source_target_pairs={{0,112},{16,32},{32,16},{48,64},{64,48},{80,96},{96,80},{112,0},{1... | collective-permute-start | bytes 110600 | tf_op jit(solution)/shard_map/ppermute | solution.py:54
  51.2 2.1 %own.7.refs_6_.refs_1_ = f32[64,1792]{1,0:T(8,128)S(1)} custom-call(bf16[1024,512]{1,0:T(8,128)(2,1)S(1)} %finish.1.refs_0_, f32[2,32,128]{2,1,0:T(8,128)S(1)} %get-tuple-element.74.refs_1_.refs_6_, f32[24,32,128]{2,1,0:T(8,128)S(1)} %get-tuple-element.75.refs_2_.refs_7_, f32[64,256]{1,0:T(8,128)S(1)} %get-tuple-element.83.refs_3_.refs_0_), custom_call_target="tpu_custom_call" | custom-call | tf_op jit(solution)/shard_map/own/pallas_call | solution.py:705
  53.3 1.1 %collective-permute-done.16.refs_2_ = f32[72,128]{1,0:T(8,128)S(1)} collective-permute-done((f32[72,128]{1,0:T(8,128)S(1)}, f32[72,128]{1,0:T(8,128)S(1)}, u32[]{:S(2)}, u32[]{:S(2)}) %collective-permute-start.16) | collective-permute-done | bytes 36896 | tf_op jit(solution)/shard_map/ppermute | solution.py:54
  54.4 0.2 faces_far.3
  54.7 1.3 %place.3.refs_0_.refs_3_ = f32[64,4096]{1,0:T(8,128)S(1)} custom-call(f32[64,2304]{1,0:T(8,128)S(1)} %own.6.refs_3_.refs_0_, f32[64,1792]{1,0:T(8,128)S(1)} %own.7.refs_6_.refs_1_, f32[192,128]{1,0:T(8,128)S(1)} %collective-permute-done.15.refs_1_.refs_2_, f32[192,128]{1,0:T(8,128)S(1)} %collective-permute-done.14.refs_1_.refs_3_, ...), custom_call_target="tpu_custom_call" | custom-call | tf_op jit(solution)/shard_map/place/pallas_call | solution.py:716
  56.0 0.7 %rim.3 = (f32[64,128]{1,0:T(8,128)S(1)}, f32[64,128]{1,0:T(8,128)S(1)}, f32[64,128]{1,0:T(8,128)}) custom-call(f32[64,128]{1,0:T(8,128)S(1)} %get-tuple-element.88.refs_0_, f32[64,128]{1,0:T(8,128)S(1)} %get-tuple-element.86.refs_9_.refs_1_, f32[64,128]{1,0:T(8,128)S(1)} %collective-permute-done.17.refs_2_, f32[64,4096]{1,0:T(8,128)S(1)} %place.3.refs_0_.refs_3_), custom_call_target="tpu_custom_call" | custom-call | tf_op jit(solution)/shard_map/rim/pallas_call | solution.py:723
  56.8 3.2 %collective-permute-start.18 = (f32[64,128]{1,0:T(8,128)S(1)}, f32[64,128]{1,0:T(8,128)S(1)}, u32[]{:S(2)}, u32[]{:S(2)}) collective-permute-start(f32[64,128]{1,0:T(8,128)S(1)} %get-tuple-element.89), channel_id=1, source_target_pairs={{0,15},{1,2},{2,1},{3,4},{4,3},{5,6},{6,5},{7,8},{8,7},{9,10},{10,... | collective-permute-start | bytes 98312 | tf_op jit(solution)/shard_map/ppermute | solution.py:54
  60.0 0.5 sum.3.summed
  60.5 3.6 %collective-permute-done.18.y_first = f32[64,128]{1,0:T(8,128)S(1)} collective-permute-done((f32[64,128]{1,0:T(8,128)S(1)}, f32[64,128]{1,0:T(8,128)S(1)}, u32[]{:S(2)}, u32[]{:S(2)}) %collective-permute-start.18) | collective-permute-done | bytes 32800 | tf_op jit(solution)/shard_map/ppermute | solution.py:54
  64.0 1.3 %last.1 = f32[64,16,256]{2,1,0:T(8,128)} custom-call(f32[64,4096]{1,0:T(8,128)S(1)} %sum.3.summed, f32[64,128]{1,0:T(8,128)S(1)} %collective-permute-done.18.y_first, f32[64,128]{1,0:T(8,128)S(1)} %collective-permute-done.19.y_second, f32[8,128]{1,0:T(8,128)S(1)} %get-tuple-element.59.refs_4_.refs_3_.refs_5_.scale), custom_call_target="tpu_custom_call" | custom-call | tf_op jit(solution)/shard_map/last/pallas_call | solution.py:747
  (27 shorter events, 0.6 us)
Async XLA Ops:
  1.2 4.4 %collective-permute-start = (f32[24,128]{1,0:T(8,128)S(1)}, f32[24,128]{1,0:T(8,128)S(1)}, u32[]{:S(2)}, u32[]{:S(2)}) collective-permute-start(f32[24,128]{1,0:T(8,128)S(1)} %get-tuple-element.51), channel_id=1, source_target_pairs={{0,112},{16,32},{32,16},{48,64},{64,48},{80,96},{96,80},{112,0},{1... | collective-permute-start | bytes 36872 | tf_op jit(solution)/shard_map/ppermute | solution.py:54
  3.8 1.8 %collective-permute-start.1 = (f32[24,128]{1,0:T(8,128)S(1)}, f32[24,128]{1,0:T(8,128)S(1)}, u32[]{:S(2)}, u32[]{:S(2)}) collective-permute-start(f32[24,128]{1,0:T(8,128)S(1)} %get-tuple-element.52), channel_id=1, source_target_pairs={{0,16},{16,0},{32,48},{48,32},{64,80},{80,64},{96,112},{112,96},{1... | collective-permute-start | bytes 36872 | tf_op jit(solution)/shard_map/ppermute | solution.py:58
  5.7 9.8 %collective-permute-start.2 = (f32[24,128]{1,0:T(8,128)S(1)}, f32[24,128]{1,0:T(8,128)S(1)}, u32[]{:S(2)}, u32[]{:S(2)}) collective-permute-start(f32[24,128]{1,0:T(8,128)S(1)} %get-tuple-element.55), channel_id=1, source_target_pairs={{0,15},{1,2},{2,1},{3,4},{4,3},{5,6},{6,5},{7,8},{8,7},{9,10},{10,... | collective-permute-start | bytes 36872 | tf_op jit(solution)/shard_map/ppermute | solution.py:54
  12.0 3.7 %collective-permute-start.3 = (f32[24,128]{1,0:T(8,128)S(1)}, f32[24,128]{1,0:T(8,128)S(1)}, u32[]{:S(2)}, u32[]{:S(2)}) collective-permute-start(f32[24,128]{1,0:T(8,128)S(1)} %get-tuple-element.56), channel_id=1, source_target_pairs={{0,1},{1,0},{2,3},{3,2},{4,5},{5,4},{6,7},{7,6},{8,9},{9,8},{10,11... | collective-permute-start | bytes 36872 | tf_op jit(solution)/shard_map/ppermute | solution.py:58
  16.7 8.0 %collective-permute-start.4 = (f32[192,128]{1,0:T(8,128)S(1)}, f32[192,128]{1,0:T(8,128)S(1)}, u32[]{:S(2)}, u32[]{:S(2)}) collective-permute-start(f32[192,128]{1,0:T(8,128)S(1)} %get-tuple-element.57), channel_id=1, source_target_pairs={{0,15},{1,2},{2,1},{3,4},{4,3},{5,6},{6,5},{7,8},{8,7},{9,10},{10,... | collective-permute-start | bytes 294920 | tf_op jit(solution)/shard_map/ppermute | solution.py:54
  20.1 4.6 %collective-permute-start.5 = (f32[192,128]{1,0:T(8,128)S(1)}, f32[192,128]{1,0:T(8,128)S(1)}, u32[]{:S(2)}, u32[]{:S(2)}) collective-permute-start(f32[192,128]{1,0:T(8,128)S(1)} %get-tuple-element.58), channel_id=1, source_target_pairs={{0,1},{1,0},{2,3},{3,2},{4,5},{5,4},{6,7},{7,6},{8,9},{9,8},{10,11... | collective-permute-start | bytes 294920 | tf_op jit(solution)/shard_map/ppermute | solution.py:58
  20.6 3.1 %copy-start = (f32[16,256]{1,0:T(8,128)S(1)}, f32[16,256]{1,0:T(8,128)}, u32[]{:S(2)}) copy-start(f32[16,256]{1,0:T(8,128)} %refs_8_.3) | copy-start | bytes 49156
  24.8 2.7 %collective-permute-start.6 = (f32[192,128]{1,0:T(8,128)S(1)}, f32[192,128]{1,0:T(8,128)S(1)}, u32[]{:S(2)}, u32[]{:S(2)}) collective-permute-start(f32[192,128]{1,0:T(8,128)S(1)} %get-tuple-element.60), channel_id=1, source_target_pairs={{0,16},{16,0},{32,48},{48,32},{64,80},{80,64},{96,112},{112,96},{1... | collective-permute-start | bytes 294920 | tf_op jit(solution)/shard_map/ppermute | solution.py:58
  24.9 6.8 %collective-permute-start.7 = (f32[192,128]{1,0:T(8,128)S(1)}, f32[192,128]{1,0:T(8,128)S(1)}, u32[]{:S(2)}, u32[]{:S(2)}) collective-permute-start(f32[192,128]{1,0:T(8,128)S(1)} %get-tuple-element.62.refs_3_), channel_id=1, source_target_pairs={{0,112},{16,32},{32,16},{48,64},{64,48},{80,96},{96,80},{112,0},{1... | collective-permute-start | bytes 294920 | tf_op jit(solution)/shard_map/ppermute | solution.py:54
  27.7 4.7 %collective-permute-start.8 = (f32[72,128]{1,0:T(8,128)S(1)}, f32[72,128]{1,0:T(8,128)S(1)}, u32[]{:S(2)}, u32[]{:S(2)}) collective-permute-start(f32[72,128]{1,0:T(8,128)S(1)} %get-tuple-element.63), channel_id=1, source_target_pairs={{0,112},{16,32},{32,16},{48,64},{64,48},{80,96},{96,80},{112,0},{1... | collective-permute-start | bytes 110600 | tf_op jit(solution)/shard_map/ppermute | solution.py:54
  32.6 1.4 %collective-permute-start.9 = (f32[64,128]{1,0:T(8,128)S(1)}, f32[64,128]{1,0:T(8,128)S(1)}, u32[]{:S(2)}, u32[]{:S(2)}) collective-permute-start(f32[64,128]{1,0:T(8,128)S(1)} %get-tuple-element.68), channel_id=1, source_target_pairs={{0,16},{16,0},{32,48},{48,32},{64,80},{80,64},{96,112},{112,96},{1... | collective-permute-start | bytes 98312 | tf_op jit(solution)/shard_map/ppermute | solution.py:58
  34.1 4.8 %collective-permute-start.11 = (f32[64,128]{1,0:T(8,128)S(1)}, f32[64,128]{1,0:T(8,128)S(1)}, u32[]{:S(2)}, u32[]{:S(2)}) collective-permute-start(f32[64,128]{1,0:T(8,128)S(1)} %get-tuple-element.73), channel_id=1, source_target_pairs={{0,1},{1,0},{2,3},{3,2},{4,5},{5,4},{6,7},{7,6},{8,9},{9,8},{10,11... | collective-permute-start | bytes 98312 | tf_op jit(solution)/shard_map/ppermute | solution.py:58
  35.3 7.3 %collective-permute-start.10 = (f32[64,128]{1,0:T(8,128)S(1)}, f32[64,128]{1,0:T(8,128)S(1)}, u32[]{:S(2)}, u32[]{:S(2)}) collective-permute-start(f32[64,128]{1,0:T(8,128)S(1)} %get-tuple-element.72), channel_id=1, source_target_pairs={{0,15},{1,2},{2,1},{3,4},{4,3},{5,6},{6,5},{7,8},{8,7},{9,10},{10,... | collective-permute-start | bytes 98312 | tf_op jit(solution)/shard_map/ppermute | solution.py:54
  39.2 8.3 %collective-permute-start.12 = (f32[192,128]{1,0:T(8,128)S(1)}, f32[192,128]{1,0:T(8,128)S(1)}, u32[]{:S(2)}, u32[]{:S(2)}) collective-permute-start(f32[192,128]{1,0:T(8,128)S(1)} %late_far.1), channel_id=1, source_target_pairs={{0,15},{1,2},{2,1},{3,4},{4,3},{5,6},{6,5},{7,8},{8,7},{9,10},{10,... | collective-permute-start | bytes 294920 | tf_op jit(solution)/shard_map/ppermute | solution.py:54
  42.9 4.9 %collective-permute-start.13 = (f32[192,128]{1,0:T(8,128)S(1)}, f32[192,128]{1,0:T(8,128)S(1)}, u32[]{:S(2)}, u32[]{:S(2)}) collective-permute-start(f32[192,128]{1,0:T(8,128)S(1)} %late_near.1), channel_id=1, source_target_pairs={{0,1},{1,0},{2,3},{3,2},{4,5},{5,4},{6,7},{7,6},{8,9},{9,8},{10,11... | collective-permute-start | bytes 294920 | tf_op jit(solution)/shard_map/ppermute | solution.py:58
  47.8 1.7 %collective-permute-start.14 = (f32[192,128]{1,0:T(8,128)S(1)}, f32[192,128]{1,0:T(8,128)S(1)}, u32[]{:S(2)}, u32[]{:S(2)}) collective-permute-start(f32[192,128]{1,0:T(8,128)S(1)} %get-tuple-element.82), channel_id=1, source_target_pairs={{0,16},{16,0},{32,48},{48,32},{64,80},{80,64},{96,112},{112,96},{1... | collective-permute-start | bytes 294920 | tf_op jit(solution)/shard_map/ppermute | solution.py:58
  47.9 5.4 %collective-permute-start.15 = (f32[192,128]{1,0:T(8,128)S(1)}, f32[192,128]{1,0:T(8,128)S(1)}, u32[]{:S(2)}, u32[]{:S(2)}) collective-permute-start(f32[192,128]{1,0:T(8,128)S(1)} %get-tuple-element.84.refs_3_), channel_id=1, source_target_pairs={{0,112},{16,32},{32,16},{48,64},{64,48},{80,96},{96,80},{112,0},{1... | collective-permute-start | bytes 294920 | tf_op jit(solution)/shard_map/ppermute | solution.py:54
  49.8 4.7 %collective-permute-start.16 = (f32[72,128]{1,0:T(8,128)S(1)}, f32[72,128]{1,0:T(8,128)S(1)}, u32[]{:S(2)}, u32[]{:S(2)}) collective-permute-start(f32[72,128]{1,0:T(8,128)S(1)} %get-tuple-element.85), channel_id=1, source_target_pairs={{0,112},{16,32},{32,16},{48,64},{64,48},{80,96},{96,80},{112,0},{1... | collective-permute-start | bytes 110600 | tf_op jit(solution)/shard_map/ppermute | solution.py:54
  54.7 1.4 %collective-permute-start.17 = (f32[64,128]{1,0:T(8,128)S(1)}, f32[64,128]{1,0:T(8,128)S(1)}, u32[]{:S(2)}, u32[]{:S(2)}) collective-permute-start(f32[64,128]{1,0:T(8,128)S(1)} %get-tuple-element.87), channel_id=1, source_target_pairs={{0,16},{16,0},{32,48},{48,32},{64,80},{80,64},{96,112},{112,96},{1... | collective-permute-start | bytes 98312 | tf_op jit(solution)/shard_map/ppermute | solution.py:58
  56.8 7.2 %collective-permute-start.18 = (f32[64,128]{1,0:T(8,128)S(1)}, f32[64,128]{1,0:T(8,128)S(1)}, u32[]{:S(2)}, u32[]{:S(2)}) collective-permute-start(f32[64,128]{1,0:T(8,128)S(1)} %get-tuple-element.89), channel_id=1, source_target_pairs={{0,15},{1,2},{2,1},{3,4},{4,3},{5,6},{6,5},{7,8},{8,7},{9,10},{10,... | collective-permute-start | bytes 98312 | tf_op jit(solution)/shard_map/ppermute | solution.py:54
  60.0 4.0 %collective-permute-start.19 = (f32[64,128]{1,0:T(8,128)S(1)}, f32[64,128]{1,0:T(8,128)S(1)}, u32[]{:S(2)}, u32[]{:S(2)}) collective-permute-start(f32[64,128]{1,0:T(8,128)S(1)} %get-tuple-element.90), channel_id=1, source_target_pairs={{0,1},{1,0},{2,3},{3,2},{4,5},{5,4},{6,7},{7,6},{8,9},{9,8},{10,11... | collective-permute-start | bytes 98312 | tf_op jit(solution)/shard_map/ppermute | solution.py:58

commit v3 on v2

--- a/solution.py
+++ b/solution.py
@@ -14,7 +14,7 @@
 NODES = 16
 POINTS = 4096
 TILES = POINTS // 128
-PIECES = (((0, 10), (10, 16)), ((0, 9), (9, 16)))
+PIECES = (((0, 10), (10, 16)), ((0, 7), (7, 16)))
 GLL_NODES = (-1.0, -0.4472135954999579, 0.4472135954999579, 1.0)
 REMOTE = (0, 1, 2, 3, 5, 6, 7, 8)
 BF16 = jnp.bfloat16
@@ -371,12 +371,16 @@
 SIDES = (1, 6)
 
 
-def sides_first(rows):
+def side(rows, far):
     even = lax.axis_index("fy") % 2 == 0
     pairs = [(rows[b : b + 1], rows[a : a + 1]) for b, a in zip(BEHIND, AHEAD)]
-    far = [jnp.where(even, behind, ahead) for behind, ahead in pairs]
-    near = [jnp.where(even, ahead, behind) for behind, ahead in pairs]
-    return jnp.concatenate(far + near + [rows[0:2]], axis=0)
+    if far:
+        return [jnp.where(even, behind, ahead) for behind, ahead in pairs]
+    return [jnp.where(even, ahead, behind) for behind, ahead in pairs]
+
+
+def sides_first(rows):
+    return jnp.concatenate(side(rows, True) + side(rows, False) + [rows[0:2]], axis=0)
 
 
 def reply_y_body(table, x_first, x_second, y_first, y_second, far, near):
@@ -395,11 +399,11 @@
         own[k * F : (k + 1) * F, :] = values[d]
 
 
-def early_body(s, table, x_first, x_second, y_first, y_second, values, lanes, shares):
-    rows = asked_rows(s, asked_blocks(x_first, x_second, y_first, y_second))
-    pick, cx, cy = [sides_first(block) for block in rows]
+def early_body(far, table, x_first, x_second, y_first, y_second, values, lanes, shares):
+    rows = asked_rows(1, asked_blocks(x_first, x_second, y_first, y_second))
+    pick, cx, cy = [jnp.concatenate(side(block, far) + [block[0:5]], axis=0) for block in rows]
     weights = weights_of(cx, cy)
-    found = answer(table, pick, weights, ((0, 1), (2, 3), (4, 5)))
+    found = answer(table, pick, weights, ((0, 1), (2,)))
     for d, value in found.items():
         values[d] = value
     element = pick.astype(jnp.int32)
@@ -409,13 +413,13 @@
         shares[a] = jnp.where(element % 16 == 0, weights[4 * a], share)
 
 
-def shared(values, lanes, shares, halo, rows):
-    for d in rows:
+def shared(values, lanes, shares, halo, message):
+    for d in range(3):
         index = jnp.broadcast_to(lanes[d : d + 1, :], (F, 128))
         value = values[d]
         for a in range(4):
             value = value + pick_lanes(halo, index + 16 * a) * shares[a, d : d + 1, :]
-        yield value
+        message[d * F : (d + 1) * F, :] = value
 
 
 def late_far_body(values, lanes, shares, near, scale, message):
@@ -423,14 +427,12 @@
     block = pltpu.roll(near[...], 64, 1) * scale[0:1, :]
     lane = lane_index(F)
     halo = jnp.where(jnp.where(even, lane - 64, 63 - lane) >= 0, block, 0.0)
-    for k, value in enumerate(shared(values, lanes, shares, halo, range(3))):
-        message[k * F : (k + 1) * F, :] = value
+    shared(values, lanes, shares, halo, message)
 
 
 def late_near_body(values, lanes, shares, far, near, scale, message):
     halo = halo_of(*from_swaps("fy", far[...], near[...])) * scale[0:1, :]
-    for k, value in enumerate(shared(values, lanes, shares, halo, range(3, 6))):
-        message[k * F : (k + 1) * F, :] = value
+    shared(values, lanes, shares, halo, message)
 
 
 def fix_body(far, asked, rims, scale, result):
@@ -559,12 +561,11 @@
         result[:, n * E : (n + 1) * E] = (own + moved) * mass[n : n + 1, :]
 
 
-def rim_body(along_y, x_first, x_second, first, second, kept):
+def rim_body(along_y, x_first, x_second, *results):
     low, high = from_swaps("fx", x_first[...], x_second[...])
     result = summed_faces(along_y[...], low, high)
-    first[...] = result
-    second[...] = result
-    kept[...] = result
+    for ref in results:
+        ref[...] = result
 
 
 def scale_body(mass, x_first, x_second, y_first, y_second, inverse, on_faces):
@@ -602,16 +603,31 @@
         table[n * F : (n + 1) * F, E : 2 * E] = low
 
 
-def last_body(summed, y_first, y_second, scale, result, block, sems):
+FACE_NODES = tuple(n for n in range(NODES) if n % 4 in (0, 3))
+INNER_NODES = tuple(n for n in range(NODES) if n % 4 in (1, 2))
+
+
+def inner_body(weighted, x_first, x_second, inverse, part, result, block, sems):
+    low, high = from_swaps("fx", x_first[...], x_second[...])
+    nodes = summed_nodes([weighted[:, n * E : (n + 1) * E] for n in range(NODES)], low, high)
+    copies = []
+    for i, n in enumerate(INNER_NODES):
+        block[i] = nodes[n] * inverse[n : n + 1, :]
+        copy = pltpu.make_async_copy(block.at[i], result.at[:, n, :], sems.at[i])
+        copy.start()
+        copies.append(copy)
+    for i, n in enumerate(FACE_NODES):
+        part[:, i * E : (i + 1) * E] = nodes[n] * inverse[n : n + 1, :]
+    for copy in copies:
+        copy.wait()
+
+
+def last_body(part, y_first, y_second, scale, begun, result, block, sems):
     halo = halo_of(*from_swaps("fy", y_first[...], y_second[...])) * scale[0:1, :]
     copies = []
-    for i in range(F // 8):
-        rows = slice(i * 8, (i + 1) * 8)
-        nodes = [
-            with_halo(n, summed[rows, n * E : (n + 1) * E], halo[rows]) for n in range(NODES)
-        ]
-        block[rows] = jnp.swapaxes(jnp.stack(nodes), 0, 1)
-        copy = pltpu.make_async_copy(block.at[rows], result.at[rows], sems.at[i])
+    for i, n in enumerate(FACE_NODES):
+        block[i] = with_halo(n, part[:, i * E : (i + 1) * E], halo)
+        copy = pltpu.make_async_copy(block.at[i], result.at[:, n, :], sems.at[i])
         copy.start()
         copies.append(copy)
     for copy in copies:
@@ -713,49 +729,64 @@
             face_far_body, [face] * 3, "faces_far", count=6, after=2
         )(partial, far, faces_in, far_sent, face_picks, mass_faces, own_b, ordered_lists[1][2])
         edges_x = (other, swap_near("fx", along_x))
-        weighted = call(
+        place = call(
             lambda *refs, s=s: place_body(s, *refs),
             shape((F, POINTS)),
             "place",
             count=9,
             after=1,
-        )(own_a, own_b, far, near, *answers_y, picks, factors, node_mass, other)
-        rims_far, rims_near, rims_kept = call(rim_body, [face] * 3, "rim", count=3, after=1)(
-            along_y, *edges_x, weighted
         )
+        moved = (own_a, own_b, far, near, *answers_y, picks, factors, node_mass)
+        if s == 0:
+            weighted = place(*moved, other)
+            rims_far, rims_near, rims_kept = call(rim_body, [face] * 3, "rim", count=3, after=1)(
+                along_y, *edges_x, weighted
+            )
+        else:
+            rims_far, rims_near = call(rim_body, [face] * 2, "rim", count=3)(along_y, *edges_x)
+            weighted = place(*moved, rims_near)
         edges_y = swap("fy", rims_far, rims_near)
         if s == 0:
             summed, early_table = call(
                 sum_body, [shape((F, POINTS)), table_shape], "sum", count=4
             )(weighted, *edges_x, inverse)
+            early_shapes = [shape((3, F, 128)), shape((8, 128), jnp.int32), shape((4, 8, 128))]
             early = call(
-                lambda *refs: early_body(1, *refs),
-                [shape((8, F, 128)), shape((8, 128), jnp.int32), shape((4, 8, 128))],
-                "early",
-                count=5,
+                lambda *refs: early_body(True, *refs), early_shapes, "early_far", count=5
             )(early_table, *asked)
-            far = call(late_far_body, answers, "late_far", count=5)(*early, edges_y[1], scale)
-            far = swap_far("fy", far)
+            sent = call(late_far_body, answers, "late_far", count=5)(*early, edges_y[1], scale)
+            far = swap_far("fy", sent)
+            early = call(
+                lambda *refs: early_body(False, *refs), early_shapes, "early_near", count=5, after=1
+            )(early_table, *asked, sent)
             near = call(late_near_body, answers, "late_near", count=6)(*early, *edges_y, scale)
             near = swap_near("fy", near)
             far = call(fix_body, answers, "fix", count=4)(far, column_kept, rims_kept, scale)
             answers_y = (far, near)
         else:
-            summed = call(sum_body, shape((F, POINTS)), "sum", count=4)(
-                weighted, *edges_x, inverse
-            )
+            scratch = [pltpu.VMEM((8, F, E), F32), pltpu.SemaphoreType.DMA((8,))]
+            vmem = pl.BlockSpec(memory_space=pltpu.VMEM)
+            hbm = pl.BlockSpec(memory_space=pltpu.HBM)
+            params = pltpu.CompilerParams(vmem_limit_bytes=VMEM_LIMIT)
+            part, begun = pl.pallas_call(
+                inner_body,
+                out_shape=[shape((F, 8 * E)), shape((F, NODES, E))],
+                in_specs=[vmem] * 4,
+                out_specs=[vmem, hbm],
+                scratch_shapes=scratch,
+                name="inner",
+                compiler_params=params,
+            )(weighted, *edges_x, inverse)
             result = pl.pallas_call(
                 last_body,
                 out_shape=shape((F, NODES, E)),
-                in_specs=[pl.BlockSpec(memory_space=pltpu.VMEM)] * 4,
-                out_specs=pl.BlockSpec(memory_space=pltpu.HBM),
-                scratch_shapes=[
-                    pltpu.VMEM((F, NODES, E), F32),
-                    pltpu.SemaphoreType.DMA((F // 8,)),
-                ],
+                in_specs=[vmem] * 4 + [hbm],
+                out_specs=hbm,
+                scratch_shapes=scratch,
+                input_output_aliases={4: 0},
                 name="last",
-                compiler_params=pltpu.CompilerParams(vmem_limit_bytes=VMEM_LIMIT),
-            )(summed, *edges_y, scale)
+                compiler_params=params,
+            )(part, *edges_y, scale, begun)
     return result
 
 

time: 66 us -> 65.3 us (0.989)
    ppermute x10, waiting for transfers between devices: 0.25 us -> 1.98 us  [swap_near(): lax.ppermute(block, axis, [(i, i ^ 1) for i in range(lax.axis_size(axis))])]
    ppermute x10, waiting for transfers between devices: 7.74 us -> 6.1 us  [swap_far(): return lax.ppermute(block, axis, pairs)]
    pallas_call x5 -> x7, Pallas kernels: 5.33 us -> 6.24 us  [the longest x1 1.28 us: per_device(): weighted = place(*moved, other)]
    pallas_call x2, Pallas kernels: 6.04 us -> 5.14 us  [per_device(): own_a = interpolate(s, 0)(table, picks, factors)]
    pallas_call x2, Pallas kernels: 4.05 us -> 4.96 us  [per_device(): own_b = interpolate(s, 1, after=1)(table, picks, factors, partial)]
    pallas_call x2 -> x1, Pallas kernels: 0.87 us -> 0.13 us  [per_device(): call(rim_body, [face] * 3, 'rim', count=3, after=1)]
    ppermute x10, starting transfers between devices: 27.7 us -> 27 us  [swap_far(): return lax.ppermute(block, axis, pairs)]
  transfers between devices with their start and end apart: 20 -> 20, of which waited for: 7 -> 9; matrix products, arithmetic and copies ran while one was open for 0% -> 0% of each run, Pallas kernels for 35% -> 37%
where the time goes in v3:
time: 65.3 us; the launch traced here: 65 us
  starting transfers between devices  28.7 us (44%)
  Pallas kernels  27.8 us (43%)
  waiting for transfers between devices  8.08 us (12%)
    ppermute x10, starting transfers between devices, swap_far(): return lax.ppermute(block, axis, pairs)  27 us
    ppermute x10, waiting for transfers between devices, swap_far(): return lax.ppermute(block, axis, pairs)  6.1 us
    pallas_call x2, Pallas kernels, per_device(): own_a = interpolate(s, 0)(table, picks, factors)  5.14 us
    pallas_call x2, Pallas kernels, per_device(): own_b = interpolate(s, 1, after=1)(table, picks, factors, partial)  4.96 us
    ppermute x10, waiting for transfers between devices, swap_near(): lax.ppermute(block, axis, [(i, i ^ 1) for i in range(lax.axis_size(axis))])  1.98 us
    pallas_call x1, Pallas kernels, per_device(): call(order_body, requests + [shape((8, POINTS), jnp.int32), shape((8, 128...  1.91 us
    ppermute x10, starting transfers between devices, swap_near(): lax.ppermute(block, axis, [(i, i ^ 1) for i in range(lax.axis_size(axis))])  1.64 us
    pallas_call x1, Pallas kernels, per_device(): call(table_body, table_shape, 'table', hbm=(0,), count=1, scratch=[pltpu....  1.54 us
  transfers between devices with their start and end apart: 20, of which 9 were waited for; matrix products, arithmetic and copies ran while one was open for 0% of the time, Pallas kernels for 37%

profile of v3, /device:TPU:0, one launch (start us, length us, event | category | flops | bytes accessed | tf_op | source)
XLA Modules:
  0.0 65.0 jit_solution(1755269596000460945)
XLA Ops:
  0.0 1.2 %asks.1 = (f32[24,128]{1,0:T(8,128)S(1)}, f32[24,128]{1,0:T(8,128)S(1)}, f32[24,128]{1,0:T(8,128)S(1)}, f32[8,256]{1,0:T(8,128)S(1)}) custom-call(s32[2,1,10]{2,1,0:T(1,128)} %refs_0_.6, s32[2,4096]{1,0:T(2,128)} %refs_1_.3, s32[2,2,4096]{2,1,0:T(2,128)} %refs_2_.3, f32[16,256]{1,0:T(8,128)} %refs_8_.3), custom_call_target="tpu_custom_call" | custom-call | tf_op jit(solution)/shard_map/asks/pallas_call | solution.py:647
  1.2 2.6 %collective-permute-start = (f32[24,128]{1,0:T(8,128)S(1)}, f32[24,128]{1,0:T(8,128)S(1)}, u32[]{:S(2)}, u32[]{:S(2)}) collective-permute-start(f32[24,128]{1,0:T(8,128)S(1)} %get-tuple-element.56), channel_id=1, source_target_pairs={{0,112},{16,32},{32,16},{48,64},{64,48},{80,96},{96,80},{112,0},{1... | collective-permute-start | bytes 36872 | tf_op jit(solution)/shard_map/ppermute | solution.py:54
  3.8 1.8 %collective-permute-done.refs_0_.refs_1_ = f32[24,128]{1,0:T(8,128)S(1)} collective-permute-done((f32[24,128]{1,0:T(8,128)S(1)}, f32[24,128]{1,0:T(8,128)S(1)}, u32[]{:S(2)}, u32[]{:S(2)}) %collective-permute-start) | collective-permute-done | bytes 12320 | tf_op jit(solution)/shard_map/ppermute | solution.py:54
  5.7 6.4 %collective-permute-start.2 = (f32[24,128]{1,0:T(8,128)S(1)}, f32[24,128]{1,0:T(8,128)S(1)}, u32[]{:S(2)}, u32[]{:S(2)}) collective-permute-start(f32[24,128]{1,0:T(8,128)S(1)} %get-tuple-element.60), channel_id=1, source_target_pairs={{0,15},{1,2},{2,1},{3,4},{4,3},{5,6},{6,5},{7,8},{8,7},{9,10},{10,... | collective-permute-start | bytes 36872 | tf_op jit(solution)/shard_map/ppermute | solution.py:54
  12.0 1.9 %order.2 = (f32[2,32,128]{2,1,0:T(8,128)S(1)}, f32[24,32,128]{2,1,0:T(8,128)S(1)}, f32[8,256]{1,0:T(8,128)S(1)}, s32[8,4096]{1,0:T(8,128)S(1)}, s32[8,128]{1,0:T(8,128)S(1)}) custom-call(s32[2,1,10]{2,1,0:T(1,128)} %refs_0_.6, s32[2,1,4096]{2,1,0:T(1,128)} %refs_1_.2, s32[2,4096]{1,0:T(2,128)} %refs_1_.3, s32[2,2,4096]{2,1,0:T(2,128)} %refs_2_.3), custom_call_target="tpu_custom_call" | custom-call | tf_op jit(solution)/shard_map/order/pallas_call | solution.py:663
  13.9 1.5 %table.1.refs_0_ = bf16[1024,512]{1,0:T(8,128)(2,1)S(1)} custom-call(f32[64,16,256]{2,1,0:T(8,128)} %refs_0_.4), custom_call_target="tpu_custom_call" | custom-call | tf_op jit(solution)/shard_map/table/pallas_call | solution.py:688
  15.5 0.2 collective-permute-done.3.refs_4_
  15.7 1.0 %reply_y.1 = (f32[192,128]{1,0:T(8,128)S(1)}, f32[192,128]{1,0:T(8,128)S(1)}) custom-call(bf16[1024,512]{1,0:T(8,128)(2,1)S(1)} %table.1.refs_0_, f32[24,128]{1,0:T(8,128)S(1)} %collective-permute-done.refs_0_.refs_1_, f32[24,128]{1,0:T(8,128)S(1)} %collective-permute-done.1.refs_1_.refs_2_, f32[24,128]{1,0:T(8,128)S(1)} %collective-permute-done.2.refs_3_, ...), custom_call_target="tpu_custom_call" | custom-call | tf_op jit(solution)/shard_map/reply_y/pallas_call | solution.py:696
  16.7 3.4 %collective-permute-start.4 = (f32[192,128]{1,0:T(8,128)S(1)}, f32[192,128]{1,0:T(8,128)S(1)}, u32[]{:S(2)}, u32[]{:S(2)}) collective-permute-start(f32[192,128]{1,0:T(8,128)S(1)} %get-tuple-element.62), channel_id=1, source_target_pairs={{0,15},{1,2},{2,1},{3,4},{4,3},{5,6},{6,5},{7,8},{8,7},{9,10},{10,... | collective-permute-start | bytes 294920 | tf_op jit(solution)/shard_map/ppermute | solution.py:54
  20.1 0.4 own_faces.2.refs_5_.refs_0_
  20.6 3.1 %own.4.refs_3_.refs_0_ = f32[64,2560]{1,0:T(8,128)S(1)} custom-call(bf16[1024,512]{1,0:T(8,128)(2,1)S(1)} %table.1.refs_0_, f32[2,32,128]{2,1,0:T(8,128)S(1)} %get-tuple-element.53.refs_1_.refs_6_, f32[24,32,128]{2,1,0:T(8,128)S(1)} %get-tuple-element.54.refs_2_.refs_7_), custom_call_target="tpu_custom_call" | custom-call | tf_op jit(solution)/shard_map/own/pallas_call | solution.py:711
  23.7 0.3 scale.1
  24.0 0.5 reply_x.2.refs_2_
  24.4 0.3 collective-permute-done.4.refs_0_.refs_2_.refs_4_
  24.9 2.6 %collective-permute-start.7 = (f32[192,128]{1,0:T(8,128)S(1)}, f32[192,128]{1,0:T(8,128)S(1)}, u32[]{:S(2)}, u32[]{:S(2)}) collective-permute-start(f32[192,128]{1,0:T(8,128)S(1)} %get-tuple-element.67.refs_3_), channel_id=1, source_target_pairs={{0,112},{16,32},{32,16},{48,64},{64,48},{80,96},{96,80},{112,0},{1... | collective-permute-start | bytes 294920 | tf_op jit(solution)/shard_map/ppermute | solution.py:54
  27.4 0.2 faces_near.2
  27.7 1.0 %collective-permute-start.8 = (f32[72,128]{1,0:T(8,128)S(1)}, f32[72,128]{1,0:T(8,128)S(1)}, u32[]{:S(2)}, u32[]{:S(2)}) collective-permute-start(f32[72,128]{1,0:T(8,128)S(1)} %get-tuple-element.68), channel_id=1, source_target_pairs={{0,112},{16,32},{32,16},{48,64},{64,48},{80,96},{96,80},{112,0},{1... | collective-permute-start | bytes 110600 | tf_op jit(solution)/shard_map/ppermute | solution.py:54
  28.7 2.0 %own.5.refs_6_.refs_1_ = f32[64,1536]{1,0:T(8,128)S(1)} custom-call(bf16[1024,512]{1,0:T(8,128)(2,1)S(1)} %table.1.refs_0_, f32[2,32,128]{2,1,0:T(8,128)S(1)} %get-tuple-element.53.refs_1_.refs_6_, f32[24,32,128]{2,1,0:T(8,128)S(1)} %get-tuple-element.54.refs_2_.refs_7_, f32[64,256]{1,0:T(8,128)S(1)} %get-tuple-element.66.refs_3_.refs_2_.refs_0_), custom_call_target="tpu_custom_call" | custom-call | tf_op jit(solution)/shard_map/own/pallas_call | solution.py:721
  30.7 1.0 %order.3 = (f32[2,32,128]{2,1,0:T(8,128)S(1)}, f32[24,32,128]{2,1,0:T(8,128)S(1)}, f32[8,256]{1,0:T(8,128)S(1)}) custom-call(s32[8,4096]{1,0:T(8,128)S(1)} %get-tuple-element.69.refs_0_, s32[8,128]{1,0:T(8,128)S(1)} %get-tuple-element.70.refs_1_, f32[64,256]{1,0:T(8,128)S(1)} %get-tuple-element.66.refs_3_.refs_2_.refs_0_), custom_call_target="tpu_custom_call" | custom-call | tf_op jit(solution)/shard_map/order/pallas_call | solution.py:724
  31.7 0.7 %collective-permute-done.8.refs_2_ = f32[72,128]{1,0:T(8,128)S(1)} collective-permute-done((f32[72,128]{1,0:T(8,128)S(1)}, f32[72,128]{1,0:T(8,128)S(1)}, u32[]{:S(2)}, u32[]{:S(2)}) %collective-permute-start.8) | collective-permute-done | bytes 36896 | tf_op jit(solution)/shard_map/ppermute | solution.py:54
  32.3 0.2 faces_far.2
  32.7 1.3 %place.2.refs_0_.refs_3_ = f32[64,4096]{1,0:T(8,128)S(1)} custom-call(f32[64,2560]{1,0:T(8,128)S(1)} %own.4.refs_3_.refs_0_, f32[64,1536]{1,0:T(8,128)S(1)} %own.5.refs_6_.refs_1_, f32[192,128]{1,0:T(8,128)S(1)} %collective-permute-done.7.refs_1_.refs_2_, f32[192,128]{1,0:T(8,128)S(1)} %collective-permute-done.6.refs_1_.refs_3_, ...), custom_call_target="tpu_custom_call" | custom-call | tf_op jit(solution)/shard_map/place/pallas_call | solution.py:741
  34.1 1.2 %collective-permute-start.11 = (f32[64,128]{1,0:T(8,128)S(1)}, f32[64,128]{1,0:T(8,128)S(1)}, u32[]{:S(2)}, u32[]{:S(2)}) collective-permute-start(f32[64,128]{1,0:T(8,128)S(1)} %get-tuple-element.78), channel_id=1, source_target_pairs={{0,1},{1,0},{2,3},{3,2},{4,5},{5,4},{6,7},{7,6},{8,9},{9,8},{10,11... | collective-permute-start | bytes 98312 | tf_op jit(solution)/shard_map/ppermute | solution.py:58
  35.3 2.1 %collective-permute-start.10 = (f32[64,128]{1,0:T(8,128)S(1)}, f32[64,128]{1,0:T(8,128)S(1)}, u32[]{:S(2)}, u32[]{:S(2)}) collective-permute-start(f32[64,128]{1,0:T(8,128)S(1)} %get-tuple-element.77), channel_id=1, source_target_pairs={{0,15},{1,2},{2,1},{3,4},{4,3},{5,6},{6,5},{7,8},{8,7},{9,10},{10,... | collective-permute-start | bytes 98312 | tf_op jit(solution)/shard_map/ppermute | solution.py:54
  37.4 0.5 sum.1
  37.9 0.7 %early_far.1 = (f32[3,64,128]{2,1,0:T(8,128)S(1)}, s32[8,128]{1,0:T(8,128)S(1)}, f32[4,8,128]{2,1,0:T(8,128)S(1)}) custom-call(bf16[1024,512]{1,0:T(8,128)(2,1)S(1)} %get-tuple-element.81.refs_0_, f32[24,128]{1,0:T(8,128)S(1)} %collective-permute-done.refs_0_.refs_1_, f32[24,128]{1,0:T(8,128)S(1)} %collective-permute-done.1.refs_1_.refs_2_, ...), custom_call_target="tpu_custom_call" | custom-call | tf_op jit(solution)/shard_map/early_far/pallas_call | solution.py:754
  38.7 0.3 late_far.1.refs_5_
  38.9 3.3 %collective-permute-start.12 = (f32[192,128]{1,0:T(8,128)S(1)}, f32[192,128]{1,0:T(8,128)S(1)}, u32[]{:S(2)}, u32[]{:S(2)}) collective-permute-start(f32[192,128]{1,0:T(8,128)S(1)} %late_far.1.refs_5_), channel_id=1, source_target_pairs={{0,15},{1,2},{2,1},{3,4},{4,3},{5,6},{6,5},{7,8},{8,7},{9,10},{10,... | collective-permute-start | bytes 294920 | tf_op jit(solution)/shard_map/ppermute | solution.py:54
  42.3 0.7 %early_near.1 = (f32[3,64,128]{2,1,0:T(8,128)S(1)}, s32[8,128]{1,0:T(8,128)S(1)}, f32[4,8,128]{2,1,0:T(8,128)S(1)}) custom-call(bf16[1024,512]{1,0:T(8,128)(2,1)S(1)} %get-tuple-element.81.refs_0_, f32[24,128]{1,0:T(8,128)S(1)} %collective-permute-done.refs_0_.refs_1_, f32[24,128]{1,0:T(8,128)S(1)} %collective-permute-done.1.refs_1_.refs_2_, ...), custom_call_target="tpu_custom_call" | custom-call | tf_op jit(solution)/shard_map/early_near/pallas_call | solution.py:759
  43.0 0.3 late_near.1
  43.4 0.4 finish.1.refs_0_
  43.8 0.4 own_faces.3.refs_5_.refs_0_
  44.2 2.1 %own.6.refs_3_.refs_0_ = f32[64,1792]{1,0:T(8,128)S(1)} custom-call(bf16[1024,512]{1,0:T(8,128)(2,1)S(1)} %finish.1.refs_0_, f32[2,32,128]{2,1,0:T(8,128)S(1)} %get-tuple-element.79.refs_1_.refs_6_, f32[24,32,128]{2,1,0:T(8,128)S(1)} %get-tuple-element.80.refs_2_.refs_7_), custom_call_target="tpu_custom_call" | custom-call | tf_op jit(solution)/shard_map/own/pallas_call | solution.py:711
  46.3 0.5 reply_x.3.refs_2_
  46.8 0.5 collective-permute-done.12.refs_0_
  47.2 0.2 fix.1.refs_0_.refs_2_.refs_4_
  47.5 0.5 collective-permute-done.13.refs_1_.refs_3_.refs_5_
  48.1 1.8 %collective-permute-start.15 = (f32[192,128]{1,0:T(8,128)S(1)}, f32[192,128]{1,0:T(8,128)S(1)}, u32[]{:S(2)}, u32[]{:S(2)}) collective-permute-start(f32[192,128]{1,0:T(8,128)S(1)} %get-tuple-element.92.refs_3_), channel_id=1, source_target_pairs={{0,112},{16,32},{32,16},{48,64},{64,48},{80,96},{96,80},{112,0},{1... | collective-permute-start | bytes 294920 | tf_op jit(solution)/shard_map/ppermute | solution.py:54
  50.2 1.3 %collective-permute-start.16 = (f32[72,128]{1,0:T(8,128)S(1)}, f32[72,128]{1,0:T(8,128)S(1)}, u32[]{:S(2)}, u32[]{:S(2)}) collective-permute-start(f32[72,128]{1,0:T(8,128)S(1)} %get-tuple-element.93), channel_id=1, source_target_pairs={{0,112},{16,32},{32,16},{48,64},{64,48},{80,96},{96,80},{112,0},{1... | collective-permute-start | bytes 110600 | tf_op jit(solution)/shard_map/ppermute | solution.py:54
  51.5 3.0 %own.7.refs_6_.refs_1_ = f32[64,2304]{1,0:T(8,128)S(1)} custom-call(bf16[1024,512]{1,0:T(8,128)(2,1)S(1)} %finish.1.refs_0_, f32[2,32,128]{2,1,0:T(8,128)S(1)} %get-tuple-element.79.refs_1_.refs_6_, f32[24,32,128]{2,1,0:T(8,128)S(1)} %get-tuple-element.80.refs_2_.refs_7_, f32[64,256]{1,0:T(8,128)S(1)} %get-tuple-element.91.refs_3_.refs_0_), custom_call_target="tpu_custom_call" | custom-call | tf_op jit(solution)/shard_map/own/pallas_call | solution.py:721
  54.5 0.4 collective-permute-done.16.refs_2_
  54.9 0.2 faces_far.3
  55.2 1.2 %collective-permute-done.17.refs_2_.x_second = f32[64,128]{1,0:T(8,128)S(1)} collective-permute-done((f32[64,128]{1,0:T(8,128)S(1)}, f32[64,128]{1,0:T(8,128)S(1)}, u32[]{:S(2)}, u32[]{:S(2)}) %collective-permute-start.17) | collective-permute-done | bytes 32800 | tf_op jit(solution)/shard_map/ppermute | solution.py:58
  56.5 2.5 %collective-permute-start.18 = (f32[64,128]{1,0:T(8,128)S(1)}, f32[64,128]{1,0:T(8,128)S(1)}, u32[]{:S(2)}, u32[]{:S(2)}) collective-permute-start(f32[64,128]{1,0:T(8,128)S(1)} %get-tuple-element.99), channel_id=1, source_target_pairs={{0,15},{1,2},{2,1},{3,4},{4,3},{5,6},{6,5},{7,8},{8,7},{9,10},{10,... | collective-permute-start | bytes 98312 | tf_op jit(solution)/shard_map/ppermute | solution.py:54
  59.1 1.3 %place.3.weighted = f32[64,4096]{1,0:T(8,128)S(1)} custom-call(f32[64,1792]{1,0:T(8,128)S(1)} %own.6.refs_3_.refs_0_, f32[64,2304]{1,0:T(8,128)S(1)} %own.7.refs_6_.refs_1_, f32[192,128]{1,0:T(8,128)S(1)} %collective-permute-done.15.refs_1_.refs_2_, f32[192,128]{1,0:T(8,128)S(1)} %collective-permute-done.14.refs_1_.refs_3_, ...), custom_call_target="tpu_custom_call" | custom-call | tf_op jit(solution)/shard_map/place/pallas_call | solution.py:747
  60.3 1.1 %inner.1 = (f32[64,2048]{1,0:T(8,128)S(1)}, f32[64,16,256]{2,1,0:T(8,128)}) custom-call(f32[64,4096]{1,0:T(8,128)S(1)} %place.3.weighted, f32[64,128]{1,0:T(8,128)S(1)} %get-tuple-element.95.refs_1_.x_first, f32[64,128]{1,0:T(8,128)S(1)} %collective-permute-done.17.refs_2_.x_second, f32[16,256]{1,0:T(8,128)S(1)} %get-tuple-element.74.refs_3_.inverse), custom_call_target="tpu_custom_call" | custom-call | tf_op jit(solution)/shard_map/inner/pallas_call | solution.py:771
  61.4 2.4 %collective-permute-done.18.y_first = f32[64,128]{1,0:T(8,128)S(1)} collective-permute-done((f32[64,128]{1,0:T(8,128)S(1)}, f32[64,128]{1,0:T(8,128)S(1)}, u32[]{:S(2)}, u32[]{:S(2)}) %collective-permute-start.18) | collective-permute-done | bytes 32800 | tf_op jit(solution)/shard_map/ppermute | solution.py:54
  63.8 1.0 %last.1 = f32[64,16,256]{2,1,0:T(8,128)} custom-call(f32[64,2048]{1,0:T(8,128)S(1)} %get-tuple-element.98.part, f32[64,128]{1,0:T(8,128)S(1)} %collective-permute-done.18.y_first, f32[64,128]{1,0:T(8,128)S(1)} %collective-permute-done.19.y_second, f32[8,128]{1,0:T(8,128)S(1)} %get-tuple-element.64.refs_4_.refs_3_.refs_5_.scale, ...), custom_call_target="tpu_custom_call", output_to_operand_aliasing={{}: (4, {})} | custom-call | tf_op jit(solution)/shard_map/last/pallas_call | solution.py:780
  (28 shorter events, 1.1 us)
Async XLA Ops:
  1.2 4.4 %collective-permute-start = (f32[24,128]{1,0:T(8,128)S(1)}, f32[24,128]{1,0:T(8,128)S(1)}, u32[]{:S(2)}, u32[]{:S(2)}) collective-permute-start(f32[24,128]{1,0:T(8,128)S(1)} %get-tuple-element.56), channel_id=1, source_target_pairs={{0,112},{16,32},{32,16},{48,64},{64,48},{80,96},{96,80},{112,0},{1... | collective-permute-start | bytes 36872 | tf_op jit(solution)/shard_map/ppermute | solution.py:54
  3.8 1.8 %collective-permute-start.1 = (f32[24,128]{1,0:T(8,128)S(1)}, f32[24,128]{1,0:T(8,128)S(1)}, u32[]{:S(2)}, u32[]{:S(2)}) collective-permute-start(f32[24,128]{1,0:T(8,128)S(1)} %get-tuple-element.57), channel_id=1, source_target_pairs={{0,16},{16,0},{32,48},{48,32},{64,80},{80,64},{96,112},{112,96},{1... | collective-permute-start | bytes 36872 | tf_op jit(solution)/shard_map/ppermute | solution.py:58
  5.7 9.8 %collective-permute-start.2 = (f32[24,128]{1,0:T(8,128)S(1)}, f32[24,128]{1,0:T(8,128)S(1)}, u32[]{:S(2)}, u32[]{:S(2)}) collective-permute-start(f32[24,128]{1,0:T(8,128)S(1)} %get-tuple-element.60), channel_id=1, source_target_pairs={{0,15},{1,2},{2,1},{3,4},{4,3},{5,6},{6,5},{7,8},{8,7},{9,10},{10,... | collective-permute-start | bytes 36872 | tf_op jit(solution)/shard_map/ppermute | solution.py:54
  12.0 3.7 %collective-permute-start.3 = (f32[24,128]{1,0:T(8,128)S(1)}, f32[24,128]{1,0:T(8,128)S(1)}, u32[]{:S(2)}, u32[]{:S(2)}) collective-permute-start(f32[24,128]{1,0:T(8,128)S(1)} %get-tuple-element.61), channel_id=1, source_target_pairs={{0,1},{1,0},{2,3},{3,2},{4,5},{5,4},{6,7},{7,6},{8,9},{9,8},{10,11... | collective-permute-start | bytes 36872 | tf_op jit(solution)/shard_map/ppermute | solution.py:58
  16.7 8.0 %collective-permute-start.4 = (f32[192,128]{1,0:T(8,128)S(1)}, f32[192,128]{1,0:T(8,128)S(1)}, u32[]{:S(2)}, u32[]{:S(2)}) collective-permute-start(f32[192,128]{1,0:T(8,128)S(1)} %get-tuple-element.62), channel_id=1, source_target_pairs={{0,15},{1,2},{2,1},{3,4},{4,3},{5,6},{6,5},{7,8},{8,7},{9,10},{10,... | collective-permute-start | bytes 294920 | tf_op jit(solution)/shard_map/ppermute | solution.py:54
  20.1 4.6 %collective-permute-start.5 = (f32[192,128]{1,0:T(8,128)S(1)}, f32[192,128]{1,0:T(8,128)S(1)}, u32[]{:S(2)}, u32[]{:S(2)}) collective-permute-start(f32[192,128]{1,0:T(8,128)S(1)} %get-tuple-element.63), channel_id=1, source_target_pairs={{0,1},{1,0},{2,3},{3,2},{4,5},{5,4},{6,7},{7,6},{8,9},{9,8},{10,11... | collective-permute-start | bytes 294920 | tf_op jit(solution)/shard_map/ppermute | solution.py:58
  20.6 3.1 %copy-start = (f32[16,256]{1,0:T(8,128)S(1)}, f32[16,256]{1,0:T(8,128)}, u32[]{:S(2)}) copy-start(f32[16,256]{1,0:T(8,128)} %refs_8_.3) | copy-start | bytes 49156
  24.8 2.7 %collective-permute-start.6 = (f32[192,128]{1,0:T(8,128)S(1)}, f32[192,128]{1,0:T(8,128)S(1)}, u32[]{:S(2)}, u32[]{:S(2)}) collective-permute-start(f32[192,128]{1,0:T(8,128)S(1)} %get-tuple-element.65), channel_id=1, source_target_pairs={{0,16},{16,0},{32,48},{48,32},{64,80},{80,64},{96,112},{112,96},{1... | collective-permute-start | bytes 294920 | tf_op jit(solution)/shard_map/ppermute | solution.py:58
  24.9 6.8 %collective-permute-start.7 = (f32[192,128]{1,0:T(8,128)S(1)}, f32[192,128]{1,0:T(8,128)S(1)}, u32[]{:S(2)}, u32[]{:S(2)}) collective-permute-start(f32[192,128]{1,0:T(8,128)S(1)} %get-tuple-element.67.refs_3_), channel_id=1, source_target_pairs={{0,112},{16,32},{32,16},{48,64},{64,48},{80,96},{96,80},{112,0},{1... | collective-permute-start | bytes 294920 | tf_op jit(solution)/shard_map/ppermute | solution.py:54
  27.7 4.7 %collective-permute-start.8 = (f32[72,128]{1,0:T(8,128)S(1)}, f32[72,128]{1,0:T(8,128)S(1)}, u32[]{:S(2)}, u32[]{:S(2)}) collective-permute-start(f32[72,128]{1,0:T(8,128)S(1)} %get-tuple-element.68), channel_id=1, source_target_pairs={{0,112},{16,32},{32,16},{48,64},{64,48},{80,96},{96,80},{112,0},{1... | collective-permute-start | bytes 110600 | tf_op jit(solution)/shard_map/ppermute | solution.py:54
  32.6 1.4 %collective-permute-start.9 = (f32[64,128]{1,0:T(8,128)S(1)}, f32[64,128]{1,0:T(8,128)S(1)}, u32[]{:S(2)}, u32[]{:S(2)}) collective-permute-start(f32[64,128]{1,0:T(8,128)S(1)} %get-tuple-element.73), channel_id=1, source_target_pairs={{0,16},{16,0},{32,48},{48,32},{64,80},{80,64},{96,112},{112,96},{1... | collective-permute-start | bytes 98312 | tf_op jit(solution)/shard_map/ppermute | solution.py:58
  34.1 4.5 %collective-permute-start.11 = (f32[64,128]{1,0:T(8,128)S(1)}, f32[64,128]{1,0:T(8,128)S(1)}, u32[]{:S(2)}, u32[]{:S(2)}) collective-permute-start(f32[64,128]{1,0:T(8,128)S(1)} %get-tuple-element.78), channel_id=1, source_target_pairs={{0,1},{1,0},{2,3},{3,2},{4,5},{5,4},{6,7},{7,6},{8,9},{9,8},{10,11... | collective-permute-start | bytes 98312 | tf_op jit(solution)/shard_map/ppermute | solution.py:58
  35.3 7.7 %collective-permute-start.10 = (f32[64,128]{1,0:T(8,128)S(1)}, f32[64,128]{1,0:T(8,128)S(1)}, u32[]{:S(2)}, u32[]{:S(2)}) collective-permute-start(f32[64,128]{1,0:T(8,128)S(1)} %get-tuple-element.77), channel_id=1, source_target_pairs={{0,15},{1,2},{2,1},{3,4},{4,3},{5,6},{6,5},{7,8},{8,7},{9,10},{10,... | collective-permute-start | bytes 98312 | tf_op jit(solution)/shard_map/ppermute | solution.py:54
  38.9 8.3 %collective-permute-start.12 = (f32[192,128]{1,0:T(8,128)S(1)}, f32[192,128]{1,0:T(8,128)S(1)}, u32[]{:S(2)}, u32[]{:S(2)}) collective-permute-start(f32[192,128]{1,0:T(8,128)S(1)} %late_far.1.refs_5_), channel_id=1, source_target_pairs={{0,15},{1,2},{2,1},{3,4},{4,3},{5,6},{6,5},{7,8},{8,7},{9,10},{10,... | collective-permute-start | bytes 294920 | tf_op jit(solution)/shard_map/ppermute | solution.py:54
  43.3 4.7 %collective-permute-start.13 = (f32[192,128]{1,0:T(8,128)S(1)}, f32[192,128]{1,0:T(8,128)S(1)}, u32[]{:S(2)}, u32[]{:S(2)}) collective-permute-start(f32[192,128]{1,0:T(8,128)S(1)} %late_near.1), channel_id=1, source_target_pairs={{0,1},{1,0},{2,3},{3,2},{4,5},{5,4},{6,7},{7,6},{8,9},{9,8},{10,11... | collective-permute-start | bytes 294920 | tf_op jit(solution)/shard_map/ppermute | solution.py:58
  48.0 1.9 %collective-permute-start.14 = (f32[192,128]{1,0:T(8,128)S(1)}, f32[192,128]{1,0:T(8,128)S(1)}, u32[]{:S(2)}, u32[]{:S(2)}) collective-permute-start(f32[192,128]{1,0:T(8,128)S(1)} %get-tuple-element.90), channel_id=1, source_target_pairs={{0,16},{16,0},{32,48},{48,32},{64,80},{80,64},{96,112},{112,96},{1... | collective-permute-start | bytes 294920 | tf_op jit(solution)/shard_map/ppermute | solution.py:58
  48.1 6.3 %collective-permute-start.15 = (f32[192,128]{1,0:T(8,128)S(1)}, f32[192,128]{1,0:T(8,128)S(1)}, u32[]{:S(2)}, u32[]{:S(2)}) collective-permute-start(f32[192,128]{1,0:T(8,128)S(1)} %get-tuple-element.92.refs_3_), channel_id=1, source_target_pairs={{0,112},{16,32},{32,16},{48,64},{64,48},{80,96},{96,80},{112,0},{1... | collective-permute-start | bytes 294920 | tf_op jit(solution)/shard_map/ppermute | solution.py:54
  50.2 4.7 %collective-permute-start.16 = (f32[72,128]{1,0:T(8,128)S(1)}, f32[72,128]{1,0:T(8,128)S(1)}, u32[]{:S(2)}, u32[]{:S(2)}) collective-permute-start(f32[72,128]{1,0:T(8,128)S(1)} %get-tuple-element.93), channel_id=1, source_target_pairs={{0,112},{16,32},{32,16},{48,64},{64,48},{80,96},{96,80},{112,0},{1... | collective-permute-start | bytes 110600 | tf_op jit(solution)/shard_map/ppermute | solution.py:54
  55.1 1.3 %collective-permute-start.17 = (f32[64,128]{1,0:T(8,128)S(1)}, f32[64,128]{1,0:T(8,128)S(1)}, u32[]{:S(2)}, u32[]{:S(2)}) collective-permute-start(f32[64,128]{1,0:T(8,128)S(1)} %get-tuple-element.96), channel_id=1, source_target_pairs={{0,16},{16,0},{32,48},{48,32},{64,80},{80,64},{96,112},{112,96},{1... | collective-permute-start | bytes 98312 | tf_op jit(solution)/shard_map/ppermute | solution.py:58
  56.5 7.3 %collective-permute-start.18 = (f32[64,128]{1,0:T(8,128)S(1)}, f32[64,128]{1,0:T(8,128)S(1)}, u32[]{:S(2)}, u32[]{:S(2)}) collective-permute-start(f32[64,128]{1,0:T(8,128)S(1)} %get-tuple-element.99), channel_id=1, source_target_pairs={{0,15},{1,2},{2,1},{3,4},{4,3},{5,6},{6,5},{7,8},{8,7},{9,10},{10,... | collective-permute-start | bytes 98312 | tf_op jit(solution)/shard_map/ppermute | solution.py:54
  59.1 4.8 %collective-permute-start.19 = (f32[64,128]{1,0:T(8,128)S(1)}, f32[64,128]{1,0:T(8,128)S(1)}, u32[]{:S(2)}, u32[]{:S(2)}) collective-permute-start(f32[64,128]{1,0:T(8,128)S(1)} %get-tuple-element.97.refs_9_), channel_id=1, source_target_pairs={{0,1},{1,0},{2,3},{3,2},{4,5},{5,4},{6,7},{7,6},{8,9},{9,8},{10,11... | collective-permute-start | bytes 98312 | tf_op jit(solution)/shard_map/ppermute | solution.py:58

commit v4 on v3

--- a/solution.py
+++ b/solution.py
@@ -399,18 +399,44 @@
         own[k * F : (k + 1) * F, :] = values[d]
 
 
-def early_body(far, table, x_first, x_second, y_first, y_second, values, lanes, shares):
-    rows = asked_rows(1, asked_blocks(x_first, x_second, y_first, y_second))
-    pick, cx, cy = [jnp.concatenate(side(block, far) + [block[0:5]], axis=0) for block in rows]
+def partner_rows(s, asked):
+    return [
+        jnp.concatenate([asked[k * 8 + 3 * s + q : k * 8 + 3 * s + q + 1, :] for k in range(3)], axis=0)
+        for q in range(3)
+    ]
+
+
+def between_body(
+    weighted, x_first, x_second, inverse, asked_far, asked_near, rims_near, scale,
+    summed, message, values, lanes, shares, table,
+):
+    sum_body(weighted, x_first, x_second, inverse, summed, table)
+    pick, cx, cy = [
+        jnp.concatenate(pair, axis=0)
+        for pair in zip(partner_rows(1, asked_far), partner_rows(1, asked_near))
+    ]
     weights = weights_of(cx, cy)
-    found = answer(table, pick, weights, ((0, 1), (2,)))
-    for d, value in found.items():
-        values[d] = value
+    found = answer(table, pick, weights, ((0, 1), (2, 3), (4, 5)))
     element = pick.astype(jnp.int32)
-    lanes[...] = element // 16 + jnp.where(element % 16 == 15, 64, 0)
+    lane_of = element // 16 + jnp.where(element % 16 == 15, 64, 0)
+    share_of = []
     for a in range(4):
         share = jnp.where(element % 16 == 15, weights[4 * a + 3], 0.0)
-        shares[a] = jnp.where(element % 16 == 0, weights[4 * a], share)
+        share_of.append(jnp.where(element % 16 == 0, weights[4 * a], share))
+    even = lax.axis_index("fy") % 2 == 0
+    block = pltpu.roll(rims_near[...], 64, 1) * scale[0:1, :]
+    lane = lane_index(F)
+    halo = jnp.where(jnp.where(even, lane - 64, 63 - lane) >= 0, block, 0.0)
+    for d in range(3):
+        index = jnp.broadcast_to(lane_of[d : d + 1], (F, 128))
+        value = found[d]
+        for a in range(4):
+            value = value + pick_lanes(halo, index + 16 * a) * share_of[a][d : d + 1]
+        message[d * F : (d + 1) * F, :] = value
+        values[d] = found[3 + d]
+    lanes[0:3, :] = lane_of[3:6]
+    for a in range(4):
+        shares[a, 0:3, :] = share_of[a][3:6]
 
 
 def shared(values, lanes, shares, halo, message):
@@ -422,14 +448,6 @@
         message[d * F : (d + 1) * F, :] = value
 
 
-def late_far_body(values, lanes, shares, near, scale, message):
-    even = lax.axis_index("fy") % 2 == 0
-    block = pltpu.roll(near[...], 64, 1) * scale[0:1, :]
-    lane = lane_index(F)
-    halo = jnp.where(jnp.where(even, lane - 64, 63 - lane) >= 0, block, 0.0)
-    shared(values, lanes, shares, halo, message)
-
-
 def late_near_body(values, lanes, shares, far, near, scale, message):
     halo = halo_of(*from_swaps("fy", far[...], near[...])) * scale[0:1, :]
     shared(values, lanes, shares, halo, message)
@@ -437,10 +455,7 @@
 
 def fix_body(far, asked, rims, scale, result):
     even = lax.axis_index("fy") % 2 == 0
-    pick, cx, cy = [
-        jnp.concatenate([asked[k * 8 + 3 + q : k * 8 + 4 + q, :] for k in range(3)], axis=0)
-        for q in range(3)
-    ]
+    pick, cx, cy = partner_rows(1, asked)
     weights = weights_of(cx, cy)
     element = pick.astype(jnp.int32)
     on_face = element % 16 == jnp.where(even, 15, 0)
@@ -747,18 +762,20 @@
             weighted = place(*moved, rims_near)
         edges_y = swap("fy", rims_far, rims_near)
         if s == 0:
-            summed, early_table = call(
-                sum_body, [shape((F, POINTS)), table_shape], "sum", count=4
-            )(weighted, *edges_x, inverse)
-            early_shapes = [shape((3, F, 128)), shape((8, 128), jnp.int32), shape((4, 8, 128))]
-            early = call(
-                lambda *refs: early_body(True, *refs), early_shapes, "early_far", count=5
-            )(early_table, *asked)
-            sent = call(late_far_body, answers, "late_far", count=5)(*early, edges_y[1], scale)
+            summed, sent, *early = call(
+                between_body,
+                [
+                    shape((F, POINTS)),
+                    answers,
+                    shape((3, F, 128)),
+                    shape((8, 128), jnp.int32),
+                    shape((4, 8, 128)),
+                ],
+                "between",
+                count=8,
+                scratch=[pltpu.VMEM((NODES * F, 2 * E), BF16)],
+            )(weighted, *edges_x, inverse, asked[2], asked[3], edges_y[1], scale)
             far = swap_far("fy", sent)
-            early = call(
-                lambda *refs: early_body(False, *refs), early_shapes, "early_near", count=5, after=1
-            )(early_table, *asked, sent)
             near = call(late_near_body, answers, "late_near", count=6)(*early, *edges_y, scale)
             near = swap_near("fy", near)
             far = call(fix_body, answers, "fix", count=4)(far, column_kept, rims_kept, scale)

time: 65.3 us -> 65 us (level)
  Pallas kernels: 27.8 us -> 26.7 us
    pallas_call x4 -> x1, Pallas kernels: 2.25 us -> 1.2 us  [per_device(): call(between_body, [shape((F, POINTS)), answers, shape((3, F, 128)), shap...]
  transfers between devices with their start and end apart: 20 -> 20, of which waited for: 9 -> 9; matrix products, arithmetic and copies ran while one was open for 0% -> 0% of each run, Pallas kernels for 37% -> 35%
where the time goes in v4:
time: 65 us; the launch traced here: 64.8 us
  starting transfers between devices  28.9 us (44%)
  Pallas kernels  26.7 us (41%)
  waiting for transfers between devices  8.67 us (13%)
    ppermute x10, starting transfers between devices, swap_far(): return lax.ppermute(block, axis, pairs)  27.2 us
    ppermute x10, waiting for transfers between devices, swap_far(): return lax.ppermute(block, axis, pairs)  6.41 us
    pallas_call x2, Pallas kernels, per_device(): own_a = interpolate(s, 0)(table, picks, factors)  5.14 us
    pallas_call x2, Pallas kernels, per_device(): own_b = interpolate(s, 1, after=1)(table, picks, factors, partial)  4.96 us
    ppermute x10, waiting for transfers between devices, swap_near(): lax.ppermute(block, axis, [(i, i ^ 1) for i in range(lax.axis_size(axis))])  2.26 us
    pallas_call x1, Pallas kernels, per_device(): call(order_body, requests + [shape((8, POINTS), jnp.int32), shape((8, 128...  1.91 us
    ppermute x10, starting transfers between devices, swap_near(): lax.ppermute(block, axis, [(i, i ^ 1) for i in range(lax.axis_size(axis))])  1.64 us
    pallas_call x1, Pallas kernels, per_device(): call(table_body, table_shape, 'table', hbm=(0,), count=1, scratch=[pltpu....  1.54 us
  transfers between devices with their start and end apart: 20, of which 9 were waited for; matrix products, arithmetic and copies ran while one was open for 0% of the time, Pallas kernels for 35%

profile of v4, /device:TPU:0, one launch (start us, length us, event | category | flops | bytes accessed | tf_op | source)
XLA Modules:
  0.0 64.8 jit_solution(12892315132400633681)
XLA Ops:
  0.0 1.2 %asks.1 = (f32[24,128]{1,0:T(8,128)S(1)}, f32[24,128]{1,0:T(8,128)S(1)}, f32[24,128]{1,0:T(8,128)S(1)}, f32[8,256]{1,0:T(8,128)S(1)}) custom-call(s32[2,1,10]{2,1,0:T(1,128)} %refs_0_.6, s32[2,4096]{1,0:T(2,128)} %refs_1_.3, s32[2,2,4096]{2,1,0:T(2,128)} %refs_2_.3, f32[16,256]{1,0:T(8,128)} %refs_8_.3), custom_call_target="tpu_custom_call" | custom-call | tf_op jit(solution)/shard_map/asks/pallas_call | solution.py:662
  1.2 2.6 %collective-permute-start = (f32[24,128]{1,0:T(8,128)S(1)}, f32[24,128]{1,0:T(8,128)S(1)}, u32[]{:S(2)}, u32[]{:S(2)}) collective-permute-start(f32[24,128]{1,0:T(8,128)S(1)} %get-tuple-element.53), channel_id=1, source_target_pairs={{0,112},{16,32},{32,16},{48,64},{64,48},{80,96},{96,80},{112,0},{1... | collective-permute-start | bytes 36872 | tf_op jit(solution)/shard_map/ppermute | solution.py:54
  3.8 1.8 %collective-permute-done.refs_0_.refs_1_ = f32[24,128]{1,0:T(8,128)S(1)} collective-permute-done((f32[24,128]{1,0:T(8,128)S(1)}, f32[24,128]{1,0:T(8,128)S(1)}, u32[]{:S(2)}, u32[]{:S(2)}) %collective-permute-start) | collective-permute-done | bytes 12320 | tf_op jit(solution)/shard_map/ppermute | solution.py:54
  5.7 6.4 %collective-permute-start.2 = (f32[24,128]{1,0:T(8,128)S(1)}, f32[24,128]{1,0:T(8,128)S(1)}, u32[]{:S(2)}, u32[]{:S(2)}) collective-permute-start(f32[24,128]{1,0:T(8,128)S(1)} %get-tuple-element.57), channel_id=1, source_target_pairs={{0,15},{1,2},{2,1},{3,4},{4,3},{5,6},{6,5},{7,8},{8,7},{9,10},{10,... | collective-permute-start | bytes 36872 | tf_op jit(solution)/shard_map/ppermute | solution.py:54
  12.0 1.9 %order.2 = (f32[2,32,128]{2,1,0:T(8,128)S(1)}, f32[24,32,128]{2,1,0:T(8,128)S(1)}, f32[8,256]{1,0:T(8,128)S(1)}, s32[8,4096]{1,0:T(8,128)S(1)}, s32[8,128]{1,0:T(8,128)S(1)}) custom-call(s32[2,1,10]{2,1,0:T(1,128)} %refs_0_.6, s32[2,1,4096]{2,1,0:T(1,128)} %refs_1_.2, s32[2,4096]{1,0:T(2,128)} %refs_1_.3, s32[2,2,4096]{2,1,0:T(2,128)} %refs_2_.3), custom_call_target="tpu_custom_call" | custom-call | tf_op jit(solution)/shard_map/order/pallas_call | solution.py:678
  13.9 1.5 %table.1.refs_0_ = bf16[1024,512]{1,0:T(8,128)(2,1)S(1)} custom-call(f32[64,16,256]{2,1,0:T(8,128)} %refs_0_.4), custom_call_target="tpu_custom_call" | custom-call | tf_op jit(solution)/shard_map/table/pallas_call | solution.py:703
  15.5 0.2 collective-permute-done.3.refs_4_.refs_5_
  15.7 1.0 %reply_y.1 = (f32[192,128]{1,0:T(8,128)S(1)}, f32[192,128]{1,0:T(8,128)S(1)}) custom-call(bf16[1024,512]{1,0:T(8,128)(2,1)S(1)} %table.1.refs_0_, f32[24,128]{1,0:T(8,128)S(1)} %collective-permute-done.refs_0_.refs_1_, f32[24,128]{1,0:T(8,128)S(1)} %collective-permute-done.1.refs_1_.refs_2_, f32[24,128]{1,0:T(8,128)S(1)} %collective-permute-done.2.refs_3_.refs_4_, ...), custom_call_target="tpu_custom_call" | custom-call | tf_op jit(solution)/shard_map/reply_y/pallas_call | solution.py:711
  16.7 3.4 %collective-permute-start.4 = (f32[192,128]{1,0:T(8,128)S(1)}, f32[192,128]{1,0:T(8,128)S(1)}, u32[]{:S(2)}, u32[]{:S(2)}) collective-permute-start(f32[192,128]{1,0:T(8,128)S(1)} %get-tuple-element.59), channel_id=1, source_target_pairs={{0,15},{1,2},{2,1},{3,4},{4,3},{5,6},{6,5},{7,8},{8,7},{9,10},{10,... | collective-permute-start | bytes 294920 | tf_op jit(solution)/shard_map/ppermute | solution.py:54
  20.1 0.4 own_faces.2.refs_5_.refs_0_
  20.6 3.1 %own.4.refs_3_.refs_0_ = f32[64,2560]{1,0:T(8,128)S(1)} custom-call(bf16[1024,512]{1,0:T(8,128)(2,1)S(1)} %table.1.refs_0_, f32[2,32,128]{2,1,0:T(8,128)S(1)} %get-tuple-element.50.refs_1_.refs_6_, f32[24,32,128]{2,1,0:T(8,128)S(1)} %get-tuple-element.51.refs_2_.refs_7_), custom_call_target="tpu_custom_call" | custom-call | tf_op jit(solution)/shard_map/own/pallas_call | solution.py:726
  23.7 0.3 scale.1
  24.0 0.5 reply_x.2.refs_2_
  24.4 0.3 collective-permute-done.4.refs_0_.refs_2_.refs_4_
  24.9 2.6 %collective-permute-start.7 = (f32[192,128]{1,0:T(8,128)S(1)}, f32[192,128]{1,0:T(8,128)S(1)}, u32[]{:S(2)}, u32[]{:S(2)}) collective-permute-start(f32[192,128]{1,0:T(8,128)S(1)} %get-tuple-element.64.refs_3_), channel_id=1, source_target_pairs={{0,112},{16,32},{32,16},{48,64},{64,48},{80,96},{96,80},{112,0},{1... | collective-permute-start | bytes 294920 | tf_op jit(solution)/shard_map/ppermute | solution.py:54
  27.4 0.2 faces_near.2
  27.7 1.0 %collective-permute-start.8 = (f32[72,128]{1,0:T(8,128)S(1)}, f32[72,128]{1,0:T(8,128)S(1)}, u32[]{:S(2)}, u32[]{:S(2)}) collective-permute-start(f32[72,128]{1,0:T(8,128)S(1)} %get-tuple-element.65), channel_id=1, source_target_pairs={{0,112},{16,32},{32,16},{48,64},{64,48},{80,96},{96,80},{112,0},{1... | collective-permute-start | bytes 110600 | tf_op jit(solution)/shard_map/ppermute | solution.py:54
  28.7 2.0 %own.5.refs_6_.refs_1_ = f32[64,1536]{1,0:T(8,128)S(1)} custom-call(bf16[1024,512]{1,0:T(8,128)(2,1)S(1)} %table.1.refs_0_, f32[2,32,128]{2,1,0:T(8,128)S(1)} %get-tuple-element.50.refs_1_.refs_6_, f32[24,32,128]{2,1,0:T(8,128)S(1)} %get-tuple-element.51.refs_2_.refs_7_, f32[64,256]{1,0:T(8,128)S(1)} %get-tuple-element.63.refs_3_.refs_2_.refs_0_), custom_call_target="tpu_custom_call" | custom-call | tf_op jit(solution)/shard_map/own/pallas_call | solution.py:736
  30.7 1.0 %order.3 = (f32[2,32,128]{2,1,0:T(8,128)S(1)}, f32[24,32,128]{2,1,0:T(8,128)S(1)}, f32[8,256]{1,0:T(8,128)S(1)}) custom-call(s32[8,4096]{1,0:T(8,128)S(1)} %get-tuple-element.66.refs_0_, s32[8,128]{1,0:T(8,128)S(1)} %get-tuple-element.67.refs_1_, f32[64,256]{1,0:T(8,128)S(1)} %get-tuple-element.63.refs_3_.refs_2_.refs_0_), custom_call_target="tpu_custom_call" | custom-call | tf_op jit(solution)/shard_map/order/pallas_call | solution.py:739
  31.7 0.7 %collective-permute-done.8.refs_2_ = f32[72,128]{1,0:T(8,128)S(1)} collective-permute-done((f32[72,128]{1,0:T(8,128)S(1)}, f32[72,128]{1,0:T(8,128)S(1)}, u32[]{:S(2)}, u32[]{:S(2)}) %collective-permute-start.8) | collective-permute-done | bytes 36896 | tf_op jit(solution)/shard_map/ppermute | solution.py:54
  32.3 0.2 faces_far.2
  32.7 1.3 %place.2.refs_3_.refs_0_ = f32[64,4096]{1,0:T(8,128)S(1)} custom-call(f32[64,2560]{1,0:T(8,128)S(1)} %own.4.refs_3_.refs_0_, f32[64,1536]{1,0:T(8,128)S(1)} %own.5.refs_6_.refs_1_, f32[192,128]{1,0:T(8,128)S(1)} %collective-permute-done.7.refs_1_.refs_2_, f32[192,128]{1,0:T(8,128)S(1)} %collective-permute-done.6.refs_1_.refs_3_, ...), custom_call_target="tpu_custom_call" | custom-call | tf_op jit(solution)/shard_map/place/pallas_call | solution.py:756
  34.0 0.1 rim.2
  34.1 1.2 %collective-permute-start.10 = (f32[64,128]{1,0:T(8,128)S(1)}, f32[64,128]{1,0:T(8,128)S(1)}, u32[]{:S(2)}, u32[]{:S(2)}) collective-permute-start(f32[64,128]{1,0:T(8,128)S(1)} %get-tuple-element.73), channel_id=1, source_target_pairs={{0,1},{1,0},{2,3},{3,2},{4,5},{5,4},{6,7},{7,6},{8,9},{9,8},{10,11... | collective-permute-start | bytes 98312 | tf_op jit(solution)/shard_map/ppermute | solution.py:58
  35.3 2.0 %collective-permute-start.11 = (f32[64,128]{1,0:T(8,128)S(1)}, f32[64,128]{1,0:T(8,128)S(1)}, u32[]{:S(2)}, u32[]{:S(2)}) collective-permute-start(f32[64,128]{1,0:T(8,128)S(1)} %get-tuple-element.75), channel_id=1, source_target_pairs={{0,15},{1,2},{2,1},{3,4},{4,3},{5,6},{6,5},{7,8},{8,7},{9,10},{10,... | collective-permute-start | bytes 98312 | tf_op jit(solution)/shard_map/ppermute | solution.py:54
  37.3 0.8 %collective-permute-done.10.refs_6_.refs_2_.refs_4_ = f32[64,128]{1,0:T(8,128)S(1)} collective-permute-done((f32[64,128]{1,0:T(8,128)S(1)}, f32[64,128]{1,0:T(8,128)S(1)}, u32[]{:S(2)}, u32[]{:S(2)}) %collective-permute-start.10) | collective-permute-done | bytes 32800 | tf_op jit(solution)/shard_map/ppermute | solution.py:58
  38.1 1.2 %between.1 = (f32[64,4096]{1,0:T(8,128)S(1)}, f32[192,128]{1,0:T(8,128)S(1)}, f32[3,64,128]{2,1,0:T(8,128)S(1)}, s32[8,128]{1,0:T(8,128)S(1)}, f32[4,8,128]{2,1,0:T(8,128)S(1)}) custom-call(f32[64,4096]{1,0:T(8,128)S(1)} %place.2.refs_3_.refs_0_, f32[64,128]{1,0:T(8,128)S(1)} %get-tuple-element.69.refs_9_.refs_1_, ...), custom_call_target="tpu_custom_call" | custom-call | tf_op jit(solution)/shard_map/between/pallas_call | solution.py:765
  39.3 3.2 %collective-permute-start.12 = (f32[192,128]{1,0:T(8,128)S(1)}, f32[192,128]{1,0:T(8,128)S(1)}, u32[]{:S(2)}, u32[]{:S(2)}) collective-permute-start(f32[192,128]{1,0:T(8,128)S(1)} %get-tuple-element.78), channel_id=1, source_target_pairs={{0,15},{1,2},{2,1},{3,4},{4,3},{5,6},{6,5},{7,8},{8,7},{9,10},{10,... | collective-permute-start | bytes 294920 | tf_op jit(solution)/shard_map/ppermute | solution.py:54
  42.5 0.3 late_near.1
  42.9 0.4 finish.1.refs_0_
  43.3 0.4 own_faces.3.refs_5_.refs_0_
  43.7 2.1 %own.6.refs_3_.refs_0_ = f32[64,1792]{1,0:T(8,128)S(1)} custom-call(bf16[1024,512]{1,0:T(8,128)(2,1)S(1)} %finish.1.refs_0_, f32[2,32,128]{2,1,0:T(8,128)S(1)} %get-tuple-element.76.refs_1_.refs_6_, f32[24,32,128]{2,1,0:T(8,128)S(1)} %get-tuple-element.77.refs_2_.refs_7_), custom_call_target="tpu_custom_call" | custom-call | tf_op jit(solution)/shard_map/own/pallas_call | solution.py:726
  45.8 0.5 reply_x.3.refs_2_
  46.3 1.2 %collective-permute-done.12.refs_0_ = f32[192,128]{1,0:T(8,128)S(1)} collective-permute-done((f32[192,128]{1,0:T(8,128)S(1)}, f32[192,128]{1,0:T(8,128)S(1)}, u32[]{:S(2)}, u32[]{:S(2)}) %collective-permute-start.12) | collective-permute-done | bytes 98336 | tf_op jit(solution)/shard_map/ppermute | solution.py:54
  47.5 0.2 fix.1.refs_0_.refs_2_.refs_4_
  47.9 1.9 %collective-permute-start.15 = (f32[192,128]{1,0:T(8,128)S(1)}, f32[192,128]{1,0:T(8,128)S(1)}, u32[]{:S(2)}, u32[]{:S(2)}) collective-permute-start(f32[192,128]{1,0:T(8,128)S(1)} %get-tuple-element.86.refs_3_), channel_id=1, source_target_pairs={{0,112},{16,32},{32,16},{48,64},{64,48},{80,96},{96,80},{112,0},{1... | collective-permute-start | bytes 294920 | tf_op jit(solution)/shard_map/ppermute | solution.py:54
  49.7 0.2 faces_near.3
  49.9 1.3 %collective-permute-start.16 = (f32[72,128]{1,0:T(8,128)S(1)}, f32[72,128]{1,0:T(8,128)S(1)}, u32[]{:S(2)}, u32[]{:S(2)}) collective-permute-start(f32[72,128]{1,0:T(8,128)S(1)} %get-tuple-element.87), channel_id=1, source_target_pairs={{0,112},{16,32},{32,16},{48,64},{64,48},{80,96},{96,80},{112,0},{1... | collective-permute-start | bytes 110600 | tf_op jit(solution)/shard_map/ppermute | solution.py:54
  51.2 3.0 %own.7.refs_6_.refs_1_ = f32[64,2304]{1,0:T(8,128)S(1)} custom-call(bf16[1024,512]{1,0:T(8,128)(2,1)S(1)} %finish.1.refs_0_, f32[2,32,128]{2,1,0:T(8,128)S(1)} %get-tuple-element.76.refs_1_.refs_6_, f32[24,32,128]{2,1,0:T(8,128)S(1)} %get-tuple-element.77.refs_2_.refs_7_, f32[64,256]{1,0:T(8,128)S(1)} %get-tuple-element.85.refs_3_.refs_0_), custom_call_target="tpu_custom_call" | custom-call | tf_op jit(solution)/shard_map/own/pallas_call | solution.py:736
  54.2 0.4 collective-permute-done.16.refs_2_
  54.6 0.2 faces_far.3
  54.9 1.2 %collective-permute-done.17.refs_2_.x_second = f32[64,128]{1,0:T(8,128)S(1)} collective-permute-done((f32[64,128]{1,0:T(8,128)S(1)}, f32[64,128]{1,0:T(8,128)S(1)}, u32[]{:S(2)}, u32[]{:S(2)}) %collective-permute-start.17) | collective-permute-done | bytes 32800 | tf_op jit(solution)/shard_map/ppermute | solution.py:58
  56.1 0.1 rim.3
  56.3 3.0 %collective-permute-start.18 = (f32[64,128]{1,0:T(8,128)S(1)}, f32[64,128]{1,0:T(8,128)S(1)}, u32[]{:S(2)}, u32[]{:S(2)}) collective-permute-start(f32[64,128]{1,0:T(8,128)S(1)} %get-tuple-element.93), channel_id=1, source_target_pairs={{0,15},{1,2},{2,1},{3,4},{4,3},{5,6},{6,5},{7,8},{8,7},{9,10},{10,... | collective-permute-start | bytes 98312 | tf_op jit(solution)/shard_map/ppermute | solution.py:54
  59.3 1.3 %place.3.weighted = f32[64,4096]{1,0:T(8,128)S(1)} custom-call(f32[64,1792]{1,0:T(8,128)S(1)} %own.6.refs_3_.refs_0_, f32[64,2304]{1,0:T(8,128)S(1)} %own.7.refs_6_.refs_1_, f32[192,128]{1,0:T(8,128)S(1)} %collective-permute-done.15.refs_1_.refs_2_, f32[192,128]{1,0:T(8,128)S(1)} %collective-permute-done.14.refs_1_.refs_3_, ...), custom_call_target="tpu_custom_call" | custom-call | tf_op jit(solution)/shard_map/place/pallas_call | solution.py:762
  60.6 1.1 %inner.1 = (f32[64,2048]{1,0:T(8,128)S(1)}, f32[64,16,256]{2,1,0:T(8,128)}) custom-call(f32[64,4096]{1,0:T(8,128)S(1)} %place.3.weighted, f32[64,128]{1,0:T(8,128)S(1)} %get-tuple-element.89.refs_1_.x_first, f32[64,128]{1,0:T(8,128)S(1)} %collective-permute-done.17.refs_2_.x_second, f32[16,256]{1,0:T(8,128)S(1)} %get-tuple-element.71.refs_3_.inverse), custom_call_target="tpu_custom_call" | custom-call | tf_op jit(solution)/shard_map/inner/pallas_call | solution.py:788
  61.6 1.9 %collective-permute-done.18.y_first = f32[64,128]{1,0:T(8,128)S(1)} collective-permute-done((f32[64,128]{1,0:T(8,128)S(1)}, f32[64,128]{1,0:T(8,128)S(1)}, u32[]{:S(2)}, u32[]{:S(2)}) %collective-permute-start.18) | collective-permute-done | bytes 32800 | tf_op jit(solution)/shard_map/ppermute | solution.py:54
  63.6 1.0 %last.1 = f32[64,16,256]{2,1,0:T(8,128)} custom-call(f32[64,2048]{1,0:T(8,128)S(1)} %get-tuple-element.92.part, f32[64,128]{1,0:T(8,128)S(1)} %collective-permute-done.18.y_first, f32[64,128]{1,0:T(8,128)S(1)} %collective-permute-done.19.y_second, ...), custom_call_target="tpu_custom_call", output_to_operand_aliasing={{}: (4, {})} | custom-call | tf_op jit(solution)/shard_map/last/pallas_call | solution.py:797
  (25 shorter events, 0.7 us)
Async XLA Ops:
  1.2 4.4 %collective-permute-start = (f32[24,128]{1,0:T(8,128)S(1)}, f32[24,128]{1,0:T(8,128)S(1)}, u32[]{:S(2)}, u32[]{:S(2)}) collective-permute-start(f32[24,128]{1,0:T(8,128)S(1)} %get-tuple-element.53), channel_id=1, source_target_pairs={{0,112},{16,32},{32,16},{48,64},{64,48},{80,96},{96,80},{112,0},{1... | collective-permute-start | bytes 36872 | tf_op jit(solution)/shard_map/ppermute | solution.py:54
  3.8 1.8 %collective-permute-start.1 = (f32[24,128]{1,0:T(8,128)S(1)}, f32[24,128]{1,0:T(8,128)S(1)}, u32[]{:S(2)}, u32[]{:S(2)}) collective-permute-start(f32[24,128]{1,0:T(8,128)S(1)} %get-tuple-element.54), channel_id=1, source_target_pairs={{0,16},{16,0},{32,48},{48,32},{64,80},{80,64},{96,112},{112,96},{1... | collective-permute-start | bytes 36872 | tf_op jit(solution)/shard_map/ppermute | solution.py:58
  5.7 9.8 %collective-permute-start.2 = (f32[24,128]{1,0:T(8,128)S(1)}, f32[24,128]{1,0:T(8,128)S(1)}, u32[]{:S(2)}, u32[]{:S(2)}) collective-permute-start(f32[24,128]{1,0:T(8,128)S(1)} %get-tuple-element.57), channel_id=1, source_target_pairs={{0,15},{1,2},{2,1},{3,4},{4,3},{5,6},{6,5},{7,8},{8,7},{9,10},{10,... | collective-permute-start | bytes 36872 | tf_op jit(solution)/shard_map/ppermute | solution.py:54
  12.0 3.7 %collective-permute-start.3 = (f32[24,128]{1,0:T(8,128)S(1)}, f32[24,128]{1,0:T(8,128)S(1)}, u32[]{:S(2)}, u32[]{:S(2)}) collective-permute-start(f32[24,128]{1,0:T(8,128)S(1)} %get-tuple-element.58), channel_id=1, source_target_pairs={{0,1},{1,0},{2,3},{3,2},{4,5},{5,4},{6,7},{7,6},{8,9},{9,8},{10,11... | collective-permute-start | bytes 36872 | tf_op jit(solution)/shard_map/ppermute | solution.py:58
  16.7 8.0 %collective-permute-start.4 = (f32[192,128]{1,0:T(8,128)S(1)}, f32[192,128]{1,0:T(8,128)S(1)}, u32[]{:S(2)}, u32[]{:S(2)}) collective-permute-start(f32[192,128]{1,0:T(8,128)S(1)} %get-tuple-element.59), channel_id=1, source_target_pairs={{0,15},{1,2},{2,1},{3,4},{4,3},{5,6},{6,5},{7,8},{8,7},{9,10},{10,... | collective-permute-start | bytes 294920 | tf_op jit(solution)/shard_map/ppermute | solution.py:54
  20.1 4.6 %collective-permute-start.5 = (f32[192,128]{1,0:T(8,128)S(1)}, f32[192,128]{1,0:T(8,128)S(1)}, u32[]{:S(2)}, u32[]{:S(2)}) collective-permute-start(f32[192,128]{1,0:T(8,128)S(1)} %get-tuple-element.60), channel_id=1, source_target_pairs={{0,1},{1,0},{2,3},{3,2},{4,5},{5,4},{6,7},{7,6},{8,9},{9,8},{10,11... | collective-permute-start | bytes 294920 | tf_op jit(solution)/shard_map/ppermute | solution.py:58
  20.6 3.1 %copy-start = (f32[16,256]{1,0:T(8,128)S(1)}, f32[16,256]{1,0:T(8,128)}, u32[]{:S(2)}) copy-start(f32[16,256]{1,0:T(8,128)} %refs_8_.3) | copy-start | bytes 49156
  24.8 2.7 %collective-permute-start.6 = (f32[192,128]{1,0:T(8,128)S(1)}, f32[192,128]{1,0:T(8,128)S(1)}, u32[]{:S(2)}, u32[]{:S(2)}) collective-permute-start(f32[192,128]{1,0:T(8,128)S(1)} %get-tuple-element.62), channel_id=1, source_target_pairs={{0,16},{16,0},{32,48},{48,32},{64,80},{80,64},{96,112},{112,96},{1... | collective-permute-start | bytes 294920 | tf_op jit(solution)/shard_map/ppermute | solution.py:58
  24.9 6.8 %collective-permute-start.7 = (f32[192,128]{1,0:T(8,128)S(1)}, f32[192,128]{1,0:T(8,128)S(1)}, u32[]{:S(2)}, u32[]{:S(2)}) collective-permute-start(f32[192,128]{1,0:T(8,128)S(1)} %get-tuple-element.64.refs_3_), channel_id=1, source_target_pairs={{0,112},{16,32},{32,16},{48,64},{64,48},{80,96},{96,80},{112,0},{1... | collective-permute-start | bytes 294920 | tf_op jit(solution)/shard_map/ppermute | solution.py:54
  27.7 4.7 %collective-permute-start.8 = (f32[72,128]{1,0:T(8,128)S(1)}, f32[72,128]{1,0:T(8,128)S(1)}, u32[]{:S(2)}, u32[]{:S(2)}) collective-permute-start(f32[72,128]{1,0:T(8,128)S(1)} %get-tuple-element.65), channel_id=1, source_target_pairs={{0,112},{16,32},{32,16},{48,64},{64,48},{80,96},{96,80},{112,0},{1... | collective-permute-start | bytes 110600 | tf_op jit(solution)/shard_map/ppermute | solution.py:54
  32.6 1.4 %collective-permute-start.9 = (f32[64,128]{1,0:T(8,128)S(1)}, f32[64,128]{1,0:T(8,128)S(1)}, u32[]{:S(2)}, u32[]{:S(2)}) collective-permute-start(f32[64,128]{1,0:T(8,128)S(1)} %get-tuple-element.70), channel_id=1, source_target_pairs={{0,16},{16,0},{32,48},{48,32},{64,80},{80,64},{96,112},{112,96},{1... | collective-permute-start | bytes 98312 | tf_op jit(solution)/shard_map/ppermute | solution.py:58
  34.1 4.0 %collective-permute-start.10 = (f32[64,128]{1,0:T(8,128)S(1)}, f32[64,128]{1,0:T(8,128)S(1)}, u32[]{:S(2)}, u32[]{:S(2)}) collective-permute-start(f32[64,128]{1,0:T(8,128)S(1)} %get-tuple-element.73), channel_id=1, source_target_pairs={{0,1},{1,0},{2,3},{3,2},{4,5},{5,4},{6,7},{7,6},{8,9},{9,8},{10,11... | collective-permute-start | bytes 98312 | tf_op jit(solution)/shard_map/ppermute | solution.py:58
  35.3 7.2 %collective-permute-start.11 = (f32[64,128]{1,0:T(8,128)S(1)}, f32[64,128]{1,0:T(8,128)S(1)}, u32[]{:S(2)}, u32[]{:S(2)}) collective-permute-start(f32[64,128]{1,0:T(8,128)S(1)} %get-tuple-element.75), channel_id=1, source_target_pairs={{0,15},{1,2},{2,1},{3,4},{4,3},{5,6},{6,5},{7,8},{8,7},{9,10},{10,... | collective-permute-start | bytes 98312 | tf_op jit(solution)/shard_map/ppermute | solution.py:54
  39.3 8.2 %collective-permute-start.12 = (f32[192,128]{1,0:T(8,128)S(1)}, f32[192,128]{1,0:T(8,128)S(1)}, u32[]{:S(2)}, u32[]{:S(2)}) collective-permute-start(f32[192,128]{1,0:T(8,128)S(1)} %get-tuple-element.78), channel_id=1, source_target_pairs={{0,15},{1,2},{2,1},{3,4},{4,3},{5,6},{6,5},{7,8},{8,7},{9,10},{10,... | collective-permute-start | bytes 294920 | tf_op jit(solution)/shard_map/ppermute | solution.py:54
  42.8 4.9 %collective-permute-start.13 = (f32[192,128]{1,0:T(8,128)S(1)}, f32[192,128]{1,0:T(8,128)S(1)}, u32[]{:S(2)}, u32[]{:S(2)}) collective-permute-start(f32[192,128]{1,0:T(8,128)S(1)} %late_near.1), channel_id=1, source_target_pairs={{0,1},{1,0},{2,3},{3,2},{4,5},{5,4},{6,7},{7,6},{8,9},{9,8},{10,11... | collective-permute-start | bytes 294920 | tf_op jit(solution)/shard_map/ppermute | solution.py:58
  47.8 1.9 %collective-permute-start.14 = (f32[192,128]{1,0:T(8,128)S(1)}, f32[192,128]{1,0:T(8,128)S(1)}, u32[]{:S(2)}, u32[]{:S(2)}) collective-permute-start(f32[192,128]{1,0:T(8,128)S(1)} %get-tuple-element.84), channel_id=1, source_target_pairs={{0,16},{16,0},{32,48},{48,32},{64,80},{80,64},{96,112},{112,96},{1... | collective-permute-start | bytes 294920 | tf_op jit(solution)/shard_map/ppermute | solution.py:58
  47.9 6.3 %collective-permute-start.15 = (f32[192,128]{1,0:T(8,128)S(1)}, f32[192,128]{1,0:T(8,128)S(1)}, u32[]{:S(2)}, u32[]{:S(2)}) collective-permute-start(f32[192,128]{1,0:T(8,128)S(1)} %get-tuple-element.86.refs_3_), channel_id=1, source_target_pairs={{0,112},{16,32},{32,16},{48,64},{64,48},{80,96},{96,80},{112,0},{1... | collective-permute-start | bytes 294920 | tf_op jit(solution)/shard_map/ppermute | solution.py:54
  49.9 4.7 %collective-permute-start.16 = (f32[72,128]{1,0:T(8,128)S(1)}, f32[72,128]{1,0:T(8,128)S(1)}, u32[]{:S(2)}, u32[]{:S(2)}) collective-permute-start(f32[72,128]{1,0:T(8,128)S(1)} %get-tuple-element.87), channel_id=1, source_target_pairs={{0,112},{16,32},{32,16},{48,64},{64,48},{80,96},{96,80},{112,0},{1... | collective-permute-start | bytes 110600 | tf_op jit(solution)/shard_map/ppermute | solution.py:54
  54.8 1.3 %collective-permute-start.17 = (f32[64,128]{1,0:T(8,128)S(1)}, f32[64,128]{1,0:T(8,128)S(1)}, u32[]{:S(2)}, u32[]{:S(2)}) collective-permute-start(f32[64,128]{1,0:T(8,128)S(1)} %get-tuple-element.90), channel_id=1, source_target_pairs={{0,16},{16,0},{32,48},{48,32},{64,80},{80,64},{96,112},{112,96},{1... | collective-permute-start | bytes 98312 | tf_op jit(solution)/shard_map/ppermute | solution.py:58
  56.3 7.3 %collective-permute-start.18 = (f32[64,128]{1,0:T(8,128)S(1)}, f32[64,128]{1,0:T(8,128)S(1)}, u32[]{:S(2)}, u32[]{:S(2)}) collective-permute-start(f32[64,128]{1,0:T(8,128)S(1)} %get-tuple-element.93), channel_id=1, source_target_pairs={{0,15},{1,2},{2,1},{3,4},{4,3},{5,6},{6,5},{7,8},{8,7},{9,10},{10,... | collective-permute-start | bytes 98312 | tf_op jit(solution)/shard_map/ppermute | solution.py:54
  59.3 4.3 %collective-permute-start.19 = (f32[64,128]{1,0:T(8,128)S(1)}, f32[64,128]{1,0:T(8,128)S(1)}, u32[]{:S(2)}, u32[]{:S(2)}) collective-permute-start(f32[64,128]{1,0:T(8,128)S(1)} %get-tuple-element.91.refs_9_), channel_id=1, source_target_pairs={{0,1},{1,0},{2,3},{3,2},{4,5},{5,4},{6,7},{7,6},{8,9},{9,8},{10,11... | collective-permute-start | bytes 98312 | tf_op jit(solution)/shard_map/ppermute | solution.py:58

commit v5 on v4

--- a/solution.py
+++ b/solution.py
@@ -407,8 +407,7 @@
 
 
 def between_body(
-    weighted, x_first, x_second, inverse, asked_far, asked_near, rims_near, scale,
-    summed, message, values, lanes, shares, table,
+    weighted, x_first, x_second, inverse, asked_far, asked_near, summed, values, lanes, shares, table
 ):
     sum_body(weighted, x_first, x_second, inverse, summed, table)
     pick, cx, cy = [
@@ -416,41 +415,36 @@
         for pair in zip(partner_rows(1, asked_far), partner_rows(1, asked_near))
     ]
     weights = weights_of(cx, cy)
-    found = answer(table, pick, weights, ((0, 1), (2, 3), (4, 5)))
+    for d, value in answer(table, pick, weights, ((0, 1), (2, 3), (4, 5))).items():
+        values[d] = value
     element = pick.astype(jnp.int32)
-    lane_of = element // 16 + jnp.where(element % 16 == 15, 64, 0)
-    share_of = []
+    lanes[0:6, :] = element // 16 + jnp.where(element % 16 == 15, 64, 0)
     for a in range(4):
         share = jnp.where(element % 16 == 15, weights[4 * a + 3], 0.0)
-        share_of.append(jnp.where(element % 16 == 0, weights[4 * a], share))
-    even = lax.axis_index("fy") % 2 == 0
-    block = pltpu.roll(rims_near[...], 64, 1) * scale[0:1, :]
-    lane = lane_index(F)
-    halo = jnp.where(jnp.where(even, lane - 64, 63 - lane) >= 0, block, 0.0)
-    for d in range(3):
-        index = jnp.broadcast_to(lane_of[d : d + 1], (F, 128))
-        value = found[d]
-        for a in range(4):
-            value = value + pick_lanes(halo, index + 16 * a) * share_of[a][d : d + 1]
-        message[d * F : (d + 1) * F, :] = value
-        values[d] = found[3 + d]
-    lanes[0:3, :] = lane_of[3:6]
-    for a in range(4):
-        shares[a, 0:3, :] = share_of[a][3:6]
-
-
-def shared(values, lanes, shares, halo, message):
-    for d in range(3):
+        shares[a, 0:6, :] = jnp.where(element % 16 == 0, weights[4 * a], share)
+
+
+def shared(values, lanes, shares, halo, start, message):
+    for k in range(3):
+        d = start + k
         index = jnp.broadcast_to(lanes[d : d + 1, :], (F, 128))
         value = values[d]
         for a in range(4):
             value = value + pick_lanes(halo, index + 16 * a) * shares[a, d : d + 1, :]
-        message[d * F : (d + 1) * F, :] = value
+        message[k * F : (k + 1) * F, :] = value
+
+
+def late_far_body(values, lanes, shares, near, scale, message):
+    even = lax.axis_index("fy") % 2 == 0
+    block = pltpu.roll(near[...], 64, 1) * scale[0:1, :]
+    lane = lane_index(F)
+    halo = jnp.where(jnp.where(even, lane - 64, 63 - lane) >= 0, block, 0.0)
+    shared(values, lanes, shares, halo, 0, message)
 
 
 def late_near_body(values, lanes, shares, far, near, scale, message):
     halo = halo_of(*from_swaps("fy", far[...], near[...])) * scale[0:1, :]
-    shared(values, lanes, shares, halo, message)
+    shared(values, lanes, shares, halo, 3, message)
 
 
 def fix_body(far, asked, rims, scale, result):
@@ -762,20 +756,20 @@
             weighted = place(*moved, rims_near)
         edges_y = swap("fy", rims_far, rims_near)
         if s == 0:
-            summed, sent, *early = call(
+            summed, *early = call(
                 between_body,
                 [
                     shape((F, POINTS)),
-                    answers,
-                    shape((3, F, 128)),
+                    shape((6, F, 128)),
                     shape((8, 128), jnp.int32),
                     shape((4, 8, 128)),
                 ],
                 "between",
-                count=8,
+                count=6,
                 scratch=[pltpu.VMEM((NODES * F, 2 * E), BF16)],
-            )(weighted, *edges_x, inverse, asked[2], asked[3], edges_y[1], scale)
-            far = swap_far("fy", sent)
+            )(weighted, *edges_x, inverse, asked[2], asked[3])
+            far = call(late_far_body, answers, "late_far", count=5)(*early, edges_y[1], scale)
+            far = swap_far("fy", far)
             near = call(late_near_body, answers, "late_near", count=6)(*early, *edges_y, scale)
             near = swap_near("fy", near)
             far = call(fix_body, answers, "fix", count=4)(far, column_kept, rims_kept, scale)

time: 65 us -> 64.8 us (level)
  waiting for transfers between devices: 8.67 us -> 7.62 us
    ppermute x10, waiting for transfers between devices: 2.26 us -> 1.53 us  [swap_near(): lax.ppermute(block, axis, [(i, i ^ 1) for i in range(lax.axis_size(axis))])]
    pallas_call x1 -> x2, Pallas kernels: 1.2 us -> 1.46 us  [the longest x1 1.19 us: per_device(): call(between_body, [shape((F, POINTS)), shape((6, F, 128)), shape((8, 128...]
  transfers between devices with their start and end apart: 20 -> 20, of which waited for: 9 -> 10; matrix products, arithmetic and copies ran while one was open for 0% -> 0% of each run, Pallas kernels for 35% -> 36%
where the time goes in v5:
time: 64.8 us; the launch traced here: 64.5 us
  starting transfers between devices  29.4 us (45%)
  Pallas kernels  27 us (42%)
  waiting for transfers between devices  7.62 us (12%)
    ppermute x10, starting transfers between devices, swap_far(): return lax.ppermute(block, axis, pairs)  27.8 us
    ppermute x10, waiting for transfers between devices, swap_far(): return lax.ppermute(block, axis, pairs)  6.09 us
    pallas_call x2, Pallas kernels, per_device(): own_a = interpolate(s, 0)(table, picks, factors)  5.13 us
    pallas_call x2, Pallas kernels, per_device(): own_b = interpolate(s, 1, after=1)(table, picks, factors, partial)  4.96 us
    pallas_call x1, Pallas kernels, per_device(): call(order_body, requests + [shape((8, POINTS), jnp.int32), shape((8, 128...  1.91 us
    ppermute x10, starting transfers between devices, swap_near(): lax.ppermute(block, axis, [(i, i ^ 1) for i in range(lax.axis_size(axis))])  1.63 us
    pallas_call x1, Pallas kernels, per_device(): call(table_body, table_shape, 'table', hbm=(0,), count=1, scratch=[pltpu....  1.54 us
    ppermute x10, waiting for transfers between devices, swap_near(): lax.ppermute(block, axis, [(i, i ^ 1) for i in range(lax.axis_size(axis))])  1.53 us
  transfers between devices with their start and end apart: 20, of which 10 were waited for; matrix products, arithmetic and copies ran while one was open for 0% of the time, Pallas kernels for 36%

profile of v5, /device:TPU:0, one launch (start us, length us, event | category | flops | bytes accessed | tf_op | source)
XLA Modules:
  0.0 64.5 jit_solution(15305086025370346159)
XLA Ops:
  0.0 1.2 %asks.1 = (f32[24,128]{1,0:T(8,128)S(1)}, f32[24,128]{1,0:T(8,128)S(1)}, f32[24,128]{1,0:T(8,128)S(1)}, f32[8,256]{1,0:T(8,128)S(1)}) custom-call(s32[2,1,10]{2,1,0:T(1,128)} %refs_0_.6, s32[2,4096]{1,0:T(2,128)} %refs_1_.3, s32[2,2,4096]{2,1,0:T(2,128)} %refs_2_.3, f32[16,256]{1,0:T(8,128)} %refs_8_.3), custom_call_target="tpu_custom_call" | custom-call | tf_op jit(solution)/shard_map/asks/pallas_call | solution.py:656
  1.2 2.6 %collective-permute-start = (f32[24,128]{1,0:T(8,128)S(1)}, f32[24,128]{1,0:T(8,128)S(1)}, u32[]{:S(2)}, u32[]{:S(2)}) collective-permute-start(f32[24,128]{1,0:T(8,128)S(1)} %get-tuple-element.52), channel_id=1, source_target_pairs={{0,112},{16,32},{32,16},{48,64},{64,48},{80,96},{96,80},{112,0},{1... | collective-permute-start | bytes 36872 | tf_op jit(solution)/shard_map/ppermute | solution.py:54
  3.8 1.8 %collective-permute-done.refs_0_.refs_1_ = f32[24,128]{1,0:T(8,128)S(1)} collective-permute-done((f32[24,128]{1,0:T(8,128)S(1)}, f32[24,128]{1,0:T(8,128)S(1)}, u32[]{:S(2)}, u32[]{:S(2)}) %collective-permute-start) | collective-permute-done | bytes 12320 | tf_op jit(solution)/shard_map/ppermute | solution.py:54
  5.7 6.4 %collective-permute-start.2 = (f32[24,128]{1,0:T(8,128)S(1)}, f32[24,128]{1,0:T(8,128)S(1)}, u32[]{:S(2)}, u32[]{:S(2)}) collective-permute-start(f32[24,128]{1,0:T(8,128)S(1)} %get-tuple-element.56), channel_id=1, source_target_pairs={{0,15},{1,2},{2,1},{3,4},{4,3},{5,6},{6,5},{7,8},{8,7},{9,10},{10,... | collective-permute-start | bytes 36872 | tf_op jit(solution)/shard_map/ppermute | solution.py:54
  12.0 1.9 %order.2 = (f32[2,32,128]{2,1,0:T(8,128)S(1)}, f32[24,32,128]{2,1,0:T(8,128)S(1)}, f32[8,256]{1,0:T(8,128)S(1)}, s32[8,4096]{1,0:T(8,128)S(1)}, s32[8,128]{1,0:T(8,128)S(1)}) custom-call(s32[2,1,10]{2,1,0:T(1,128)} %refs_0_.6, s32[2,1,4096]{2,1,0:T(1,128)} %refs_1_.2, s32[2,4096]{1,0:T(2,128)} %refs_1_.3, s32[2,2,4096]{2,1,0:T(2,128)} %refs_2_.3), custom_call_target="tpu_custom_call" | custom-call | tf_op jit(solution)/shard_map/order/pallas_call | solution.py:672
  13.9 1.5 %table.1.refs_0_ = bf16[1024,512]{1,0:T(8,128)(2,1)S(1)} custom-call(f32[64,16,256]{2,1,0:T(8,128)} %refs_0_.4), custom_call_target="tpu_custom_call" | custom-call | tf_op jit(solution)/shard_map/table/pallas_call | solution.py:697
  15.5 0.2 collective-permute-done.3.refs_4_.refs_5_
  15.7 1.0 %reply_y.1 = (f32[192,128]{1,0:T(8,128)S(1)}, f32[192,128]{1,0:T(8,128)S(1)}) custom-call(bf16[1024,512]{1,0:T(8,128)(2,1)S(1)} %table.1.refs_0_, f32[24,128]{1,0:T(8,128)S(1)} %collective-permute-done.refs_0_.refs_1_, f32[24,128]{1,0:T(8,128)S(1)} %collective-permute-done.1.refs_1_.refs_2_, f32[24,128]{1,0:T(8,128)S(1)} %collective-permute-done.2.refs_3_.refs_4_, ...), custom_call_target="tpu_custom_call" | custom-call | tf_op jit(solution)/shard_map/reply_y/pallas_call | solution.py:705
  16.7 3.4 %collective-permute-start.4 = (f32[192,128]{1,0:T(8,128)S(1)}, f32[192,128]{1,0:T(8,128)S(1)}, u32[]{:S(2)}, u32[]{:S(2)}) collective-permute-start(f32[192,128]{1,0:T(8,128)S(1)} %get-tuple-element.58), channel_id=1, source_target_pairs={{0,15},{1,2},{2,1},{3,4},{4,3},{5,6},{6,5},{7,8},{8,7},{9,10},{10,... | collective-permute-start | bytes 294920 | tf_op jit(solution)/shard_map/ppermute | solution.py:54
  20.1 0.4 own_faces.2.refs_5_.refs_0_
  20.6 3.1 %own.4.refs_3_.refs_0_ = f32[64,2560]{1,0:T(8,128)S(1)} custom-call(bf16[1024,512]{1,0:T(8,128)(2,1)S(1)} %table.1.refs_0_, f32[2,32,128]{2,1,0:T(8,128)S(1)} %get-tuple-element.49.refs_1_.refs_6_, f32[24,32,128]{2,1,0:T(8,128)S(1)} %get-tuple-element.50.refs_2_.refs_7_), custom_call_target="tpu_custom_call" | custom-call | tf_op jit(solution)/shard_map/own/pallas_call | solution.py:720
  23.7 0.3 scale.1
  24.0 0.5 reply_x.2.refs_2_
  24.4 0.3 collective-permute-done.4.refs_0_.refs_2_.refs_4_
  24.9 2.6 %collective-permute-start.7 = (f32[192,128]{1,0:T(8,128)S(1)}, f32[192,128]{1,0:T(8,128)S(1)}, u32[]{:S(2)}, u32[]{:S(2)}) collective-permute-start(f32[192,128]{1,0:T(8,128)S(1)} %get-tuple-element.63.refs_3_), channel_id=1, source_target_pairs={{0,112},{16,32},{32,16},{48,64},{64,48},{80,96},{96,80},{112,0},{1... | collective-permute-start | bytes 294920 | tf_op jit(solution)/shard_map/ppermute | solution.py:54
  27.4 0.2 faces_near.2
  27.7 1.0 %collective-permute-start.8 = (f32[72,128]{1,0:T(8,128)S(1)}, f32[72,128]{1,0:T(8,128)S(1)}, u32[]{:S(2)}, u32[]{:S(2)}) collective-permute-start(f32[72,128]{1,0:T(8,128)S(1)} %get-tuple-element.64), channel_id=1, source_target_pairs={{0,112},{16,32},{32,16},{48,64},{64,48},{80,96},{96,80},{112,0},{1... | collective-permute-start | bytes 110600 | tf_op jit(solution)/shard_map/ppermute | solution.py:54
  28.7 2.0 %own.5.refs_6_.refs_1_ = f32[64,1536]{1,0:T(8,128)S(1)} custom-call(bf16[1024,512]{1,0:T(8,128)(2,1)S(1)} %table.1.refs_0_, f32[2,32,128]{2,1,0:T(8,128)S(1)} %get-tuple-element.49.refs_1_.refs_6_, f32[24,32,128]{2,1,0:T(8,128)S(1)} %get-tuple-element.50.refs_2_.refs_7_, f32[64,256]{1,0:T(8,128)S(1)} %get-tuple-element.62.refs_3_.refs_2_.refs_0_), custom_call_target="tpu_custom_call" | custom-call | tf_op jit(solution)/shard_map/own/pallas_call | solution.py:730
  30.7 1.0 %order.3 = (f32[2,32,128]{2,1,0:T(8,128)S(1)}, f32[24,32,128]{2,1,0:T(8,128)S(1)}, f32[8,256]{1,0:T(8,128)S(1)}) custom-call(s32[8,4096]{1,0:T(8,128)S(1)} %get-tuple-element.65.refs_0_, s32[8,128]{1,0:T(8,128)S(1)} %get-tuple-element.66.refs_1_, f32[64,256]{1,0:T(8,128)S(1)} %get-tuple-element.62.refs_3_.refs_2_.refs_0_), custom_call_target="tpu_custom_call" | custom-call | tf_op jit(solution)/shard_map/order/pallas_call | solution.py:733
  31.7 0.7 %collective-permute-done.8.refs_2_ = f32[72,128]{1,0:T(8,128)S(1)} collective-permute-done((f32[72,128]{1,0:T(8,128)S(1)}, f32[72,128]{1,0:T(8,128)S(1)}, u32[]{:S(2)}, u32[]{:S(2)}) %collective-permute-start.8) | collective-permute-done | bytes 36896 | tf_op jit(solution)/shard_map/ppermute | solution.py:54
  32.3 0.2 faces_far.2
  32.7 1.3 %place.2.refs_0_.refs_3_ = f32[64,4096]{1,0:T(8,128)S(1)} custom-call(f32[64,2560]{1,0:T(8,128)S(1)} %own.4.refs_3_.refs_0_, f32[64,1536]{1,0:T(8,128)S(1)} %own.5.refs_6_.refs_1_, f32[192,128]{1,0:T(8,128)S(1)} %collective-permute-done.7.refs_1_.refs_2_, f32[192,128]{1,0:T(8,128)S(1)} %collective-permute-done.6.refs_1_.refs_3_, ...), custom_call_target="tpu_custom_call" | custom-call | tf_op jit(solution)/shard_map/place/pallas_call | solution.py:750
  34.0 0.1 rim.2
  34.1 1.2 %collective-permute-start.11 = (f32[64,128]{1,0:T(8,128)S(1)}, f32[64,128]{1,0:T(8,128)S(1)}, u32[]{:S(2)}, u32[]{:S(2)}) collective-permute-start(f32[64,128]{1,0:T(8,128)S(1)} %get-tuple-element.74), channel_id=1, source_target_pairs={{0,1},{1,0},{2,3},{3,2},{4,5},{5,4},{6,7},{7,6},{8,9},{9,8},{10,11... | collective-permute-start | bytes 98312 | tf_op jit(solution)/shard_map/ppermute | solution.py:58
  35.3 2.0 %collective-permute-start.10 = (f32[64,128]{1,0:T(8,128)S(1)}, f32[64,128]{1,0:T(8,128)S(1)}, u32[]{:S(2)}, u32[]{:S(2)}) collective-permute-start(f32[64,128]{1,0:T(8,128)S(1)} %get-tuple-element.73), channel_id=1, source_target_pairs={{0,15},{1,2},{2,1},{3,4},{4,3},{5,6},{6,5},{7,8},{8,7},{9,10},{10,... | collective-permute-start | bytes 98312 | tf_op jit(solution)/shard_map/ppermute | solution.py:54
  37.3 1.2 %between.1 = (f32[64,4096]{1,0:T(8,128)S(1)}, f32[6,64,128]{2,1,0:T(8,128)S(1)}, s32[8,128]{1,0:T(8,128)S(1)}, f32[4,8,128]{2,1,0:T(8,128)S(1)}) custom-call(f32[64,4096]{1,0:T(8,128)S(1)} %place.2.refs_0_.refs_3_, f32[64,128]{1,0:T(8,128)S(1)} %get-tuple-element.68.refs_9_.refs_1_, f32[64,128]{1,0:T(8,128)S(1)} %collective-permute-done.9.refs_2_, ...), custom_call_target="tpu_custom_call" | custom-call | tf_op jit(solution)/shard_map/between/pallas_call | solution.py:759
  38.5 0.3 late_far.1
  38.8 3.6 %collective-permute-start.12 = (f32[192,128]{1,0:T(8,128)S(1)}, f32[192,128]{1,0:T(8,128)S(1)}, u32[]{:S(2)}, u32[]{:S(2)}) collective-permute-start(f32[192,128]{1,0:T(8,128)S(1)} %late_far.1), channel_id=1, source_target_pairs={{0,15},{1,2},{2,1},{3,4},{4,3},{5,6},{6,5},{7,8},{8,7},{9,10},{10,... | collective-permute-start | bytes 294920 | tf_op jit(solution)/shard_map/ppermute | solution.py:54
  42.4 0.1 collective-permute-done.10.refs_1_.refs_3_
  42.5 0.3 late_near.1
  42.9 0.4 finish.1.refs_0_
  43.3 0.4 own_faces.3.refs_5_.refs_0_
  43.7 2.1 %own.6.refs_3_.refs_0_ = f32[64,1792]{1,0:T(8,128)S(1)} custom-call(bf16[1024,512]{1,0:T(8,128)(2,1)S(1)} %finish.1.refs_0_, f32[2,32,128]{2,1,0:T(8,128)S(1)} %get-tuple-element.75.refs_1_.refs_6_, f32[24,32,128]{2,1,0:T(8,128)S(1)} %get-tuple-element.76.refs_2_.refs_7_), custom_call_target="tpu_custom_call" | custom-call | tf_op jit(solution)/shard_map/own/pallas_call | solution.py:720
  45.8 0.5 reply_x.3.refs_2_
  46.3 0.9 %collective-permute-done.12.refs_0_ = f32[192,128]{1,0:T(8,128)S(1)} collective-permute-done((f32[192,128]{1,0:T(8,128)S(1)}, f32[192,128]{1,0:T(8,128)S(1)}, u32[]{:S(2)}, u32[]{:S(2)}) %collective-permute-start.12) | collective-permute-done | bytes 98336 | tf_op jit(solution)/shard_map/ppermute | solution.py:54
  47.2 0.2 fix.1.refs_0_.refs_2_.refs_4_
  47.6 1.8 %collective-permute-start.15 = (f32[192,128]{1,0:T(8,128)S(1)}, f32[192,128]{1,0:T(8,128)S(1)}, u32[]{:S(2)}, u32[]{:S(2)}) collective-permute-start(f32[192,128]{1,0:T(8,128)S(1)} %get-tuple-element.84.refs_3_), channel_id=1, source_target_pairs={{0,112},{16,32},{32,16},{48,64},{64,48},{80,96},{96,80},{112,0},{1... | collective-permute-start | bytes 294920 | tf_op jit(solution)/shard_map/ppermute | solution.py:54
  49.5 0.2 faces_near.3
  49.7 1.3 %collective-permute-start.16 = (f32[72,128]{1,0:T(8,128)S(1)}, f32[72,128]{1,0:T(8,128)S(1)}, u32[]{:S(2)}, u32[]{:S(2)}) collective-permute-start(f32[72,128]{1,0:T(8,128)S(1)} %get-tuple-element.85), channel_id=1, source_target_pairs={{0,112},{16,32},{32,16},{48,64},{64,48},{80,96},{96,80},{112,0},{1... | collective-permute-start | bytes 110600 | tf_op jit(solution)/shard_map/ppermute | solution.py:54
  51.0 3.0 %own.7.refs_6_.refs_1_ = f32[64,2304]{1,0:T(8,128)S(1)} custom-call(bf16[1024,512]{1,0:T(8,128)(2,1)S(1)} %finish.1.refs_0_, f32[2,32,128]{2,1,0:T(8,128)S(1)} %get-tuple-element.75.refs_1_.refs_6_, f32[24,32,128]{2,1,0:T(8,128)S(1)} %get-tuple-element.76.refs_2_.refs_7_, f32[64,256]{1,0:T(8,128)S(1)} %get-tuple-element.83.refs_3_.refs_0_), custom_call_target="tpu_custom_call" | custom-call | tf_op jit(solution)/shard_map/own/pallas_call | solution.py:730
  54.0 0.4 collective-permute-done.16.refs_2_
  54.4 0.2 faces_far.3
  54.7 1.2 %collective-permute-done.17.refs_2_.x_second = f32[64,128]{1,0:T(8,128)S(1)} collective-permute-done((f32[64,128]{1,0:T(8,128)S(1)}, f32[64,128]{1,0:T(8,128)S(1)}, u32[]{:S(2)}, u32[]{:S(2)}) %collective-permute-start.17) | collective-permute-done | bytes 32800 | tf_op jit(solution)/shard_map/ppermute | solution.py:58
  56.0 3.1 %collective-permute-start.18 = (f32[64,128]{1,0:T(8,128)S(1)}, f32[64,128]{1,0:T(8,128)S(1)}, u32[]{:S(2)}, u32[]{:S(2)}) collective-permute-start(f32[64,128]{1,0:T(8,128)S(1)} %get-tuple-element.91), channel_id=1, source_target_pairs={{0,15},{1,2},{2,1},{3,4},{4,3},{5,6},{6,5},{7,8},{8,7},{9,10},{10,... | collective-permute-start | bytes 98312 | tf_op jit(solution)/shard_map/ppermute | solution.py:54
  59.2 1.3 %place.3.weighted = f32[64,4096]{1,0:T(8,128)S(1)} custom-call(f32[64,1792]{1,0:T(8,128)S(1)} %own.6.refs_3_.refs_0_, f32[64,2304]{1,0:T(8,128)S(1)} %own.7.refs_6_.refs_1_, f32[192,128]{1,0:T(8,128)S(1)} %collective-permute-done.15.refs_1_.refs_2_, f32[192,128]{1,0:T(8,128)S(1)} %collective-permute-done.14.refs_1_.refs_3_, ...), custom_call_target="tpu_custom_call" | custom-call | tf_op jit(solution)/shard_map/place/pallas_call | solution.py:756
  60.4 1.1 %inner.1 = (f32[64,2048]{1,0:T(8,128)S(1)}, f32[64,16,256]{2,1,0:T(8,128)}) custom-call(f32[64,4096]{1,0:T(8,128)S(1)} %place.3.weighted, f32[64,128]{1,0:T(8,128)S(1)} %get-tuple-element.87.refs_1_.x_first, f32[64,128]{1,0:T(8,128)S(1)} %collective-permute-done.17.refs_2_.x_second, f32[16,256]{1,0:T(8,128)S(1)} %get-tuple-element.70.refs_3_.inverse), custom_call_target="tpu_custom_call" | custom-call | tf_op jit(solution)/shard_map/inner/pallas_call | solution.py:782
  61.5 1.8 %collective-permute-done.18.y_first = f32[64,128]{1,0:T(8,128)S(1)} collective-permute-done((f32[64,128]{1,0:T(8,128)S(1)}, f32[64,128]{1,0:T(8,128)S(1)}, u32[]{:S(2)}, u32[]{:S(2)}) %collective-permute-start.18) | collective-permute-done | bytes 32800 | tf_op jit(solution)/shard_map/ppermute | solution.py:54
  63.4 1.0 %last.1 = f32[64,16,256]{2,1,0:T(8,128)} custom-call(f32[64,2048]{1,0:T(8,128)S(1)} %get-tuple-element.90.part, f32[64,128]{1,0:T(8,128)S(1)} %collective-permute-done.18.y_first, f32[64,128]{1,0:T(8,128)S(1)} %collective-permute-done.19.y_second, f32[8,128]{1,0:T(8,128)S(1)} %get-tuple-element.60.refs_4_.refs_3_.refs_5_.scale, ...), custom_call_target="tpu_custom_call", output_to_operand_aliasing={{}: (4, {})} | custom-call | tf_op jit(solution)/shard_map/last/pallas_call | solution.py:791
  (26 shorter events, 0.8 us)
Async XLA Ops:
  1.2 4.4 %collective-permute-start = (f32[24,128]{1,0:T(8,128)S(1)}, f32[24,128]{1,0:T(8,128)S(1)}, u32[]{:S(2)}, u32[]{:S(2)}) collective-permute-start(f32[24,128]{1,0:T(8,128)S(1)} %get-tuple-element.52), channel_id=1, source_target_pairs={{0,112},{16,32},{32,16},{48,64},{64,48},{80,96},{96,80},{112,0},{1... | collective-permute-start | bytes 36872 | tf_op jit(solution)/shard_map/ppermute | solution.py:54
  3.8 1.8 %collective-permute-start.1 = (f32[24,128]{1,0:T(8,128)S(1)}, f32[24,128]{1,0:T(8,128)S(1)}, u32[]{:S(2)}, u32[]{:S(2)}) collective-permute-start(f32[24,128]{1,0:T(8,128)S(1)} %get-tuple-element.53), channel_id=1, source_target_pairs={{0,16},{16,0},{32,48},{48,32},{64,80},{80,64},{96,112},{112,96},{1... | collective-permute-start | bytes 36872 | tf_op jit(solution)/shard_map/ppermute | solution.py:58
  5.7 9.8 %collective-permute-start.2 = (f32[24,128]{1,0:T(8,128)S(1)}, f32[24,128]{1,0:T(8,128)S(1)}, u32[]{:S(2)}, u32[]{:S(2)}) collective-permute-start(f32[24,128]{1,0:T(8,128)S(1)} %get-tuple-element.56), channel_id=1, source_target_pairs={{0,15},{1,2},{2,1},{3,4},{4,3},{5,6},{6,5},{7,8},{8,7},{9,10},{10,... | collective-permute-start | bytes 36872 | tf_op jit(solution)/shard_map/ppermute | solution.py:54
  12.0 3.7 %collective-permute-start.3 = (f32[24,128]{1,0:T(8,128)S(1)}, f32[24,128]{1,0:T(8,128)S(1)}, u32[]{:S(2)}, u32[]{:S(2)}) collective-permute-start(f32[24,128]{1,0:T(8,128)S(1)} %get-tuple-element.57), channel_id=1, source_target_pairs={{0,1},{1,0},{2,3},{3,2},{4,5},{5,4},{6,7},{7,6},{8,9},{9,8},{10,11... | collective-permute-start | bytes 36872 | tf_op jit(solution)/shard_map/ppermute | solution.py:58
  16.7 8.0 %collective-permute-start.4 = (f32[192,128]{1,0:T(8,128)S(1)}, f32[192,128]{1,0:T(8,128)S(1)}, u32[]{:S(2)}, u32[]{:S(2)}) collective-permute-start(f32[192,128]{1,0:T(8,128)S(1)} %get-tuple-element.58), channel_id=1, source_target_pairs={{0,15},{1,2},{2,1},{3,4},{4,3},{5,6},{6,5},{7,8},{8,7},{9,10},{10,... | collective-permute-start | bytes 294920 | tf_op jit(solution)/shard_map/ppermute | solution.py:54
  20.1 4.6 %collective-permute-start.5 = (f32[192,128]{1,0:T(8,128)S(1)}, f32[192,128]{1,0:T(8,128)S(1)}, u32[]{:S(2)}, u32[]{:S(2)}) collective-permute-start(f32[192,128]{1,0:T(8,128)S(1)} %get-tuple-element.59), channel_id=1, source_target_pairs={{0,1},{1,0},{2,3},{3,2},{4,5},{5,4},{6,7},{7,6},{8,9},{9,8},{10,11... | collective-permute-start | bytes 294920 | tf_op jit(solution)/shard_map/ppermute | solution.py:58
  20.6 3.1 %copy-start = (f32[16,256]{1,0:T(8,128)S(1)}, f32[16,256]{1,0:T(8,128)}, u32[]{:S(2)}) copy-start(f32[16,256]{1,0:T(8,128)} %refs_8_.3) | copy-start | bytes 49156
  24.8 2.7 %collective-permute-start.6 = (f32[192,128]{1,0:T(8,128)S(1)}, f32[192,128]{1,0:T(8,128)S(1)}, u32[]{:S(2)}, u32[]{:S(2)}) collective-permute-start(f32[192,128]{1,0:T(8,128)S(1)} %get-tuple-element.61), channel_id=1, source_target_pairs={{0,16},{16,0},{32,48},{48,32},{64,80},{80,64},{96,112},{112,96},{1... | collective-permute-start | bytes 294920 | tf_op jit(solution)/shard_map/ppermute | solution.py:58
  24.9 6.8 %collective-permute-start.7 = (f32[192,128]{1,0:T(8,128)S(1)}, f32[192,128]{1,0:T(8,128)S(1)}, u32[]{:S(2)}, u32[]{:S(2)}) collective-permute-start(f32[192,128]{1,0:T(8,128)S(1)} %get-tuple-element.63.refs_3_), channel_id=1, source_target_pairs={{0,112},{16,32},{32,16},{48,64},{64,48},{80,96},{96,80},{112,0},{1... | collective-permute-start | bytes 294920 | tf_op jit(solution)/shard_map/ppermute | solution.py:54
  27.7 4.7 %collective-permute-start.8 = (f32[72,128]{1,0:T(8,128)S(1)}, f32[72,128]{1,0:T(8,128)S(1)}, u32[]{:S(2)}, u32[]{:S(2)}) collective-permute-start(f32[72,128]{1,0:T(8,128)S(1)} %get-tuple-element.64), channel_id=1, source_target_pairs={{0,112},{16,32},{32,16},{48,64},{64,48},{80,96},{96,80},{112,0},{1... | collective-permute-start | bytes 110600 | tf_op jit(solution)/shard_map/ppermute | solution.py:54
  32.6 1.4 %collective-permute-start.9 = (f32[64,128]{1,0:T(8,128)S(1)}, f32[64,128]{1,0:T(8,128)S(1)}, u32[]{:S(2)}, u32[]{:S(2)}) collective-permute-start(f32[64,128]{1,0:T(8,128)S(1)} %get-tuple-element.69), channel_id=1, source_target_pairs={{0,16},{16,0},{32,48},{48,32},{64,80},{80,64},{96,112},{112,96},{1... | collective-permute-start | bytes 98312 | tf_op jit(solution)/shard_map/ppermute | solution.py:58
  34.1 4.4 %collective-permute-start.11 = (f32[64,128]{1,0:T(8,128)S(1)}, f32[64,128]{1,0:T(8,128)S(1)}, u32[]{:S(2)}, u32[]{:S(2)}) collective-permute-start(f32[64,128]{1,0:T(8,128)S(1)} %get-tuple-element.74), channel_id=1, source_target_pairs={{0,1},{1,0},{2,3},{3,2},{4,5},{5,4},{6,7},{7,6},{8,9},{9,8},{10,11... | collective-permute-start | bytes 98312 | tf_op jit(solution)/shard_map/ppermute | solution.py:58
  35.3 7.2 %collective-permute-start.10 = (f32[64,128]{1,0:T(8,128)S(1)}, f32[64,128]{1,0:T(8,128)S(1)}, u32[]{:S(2)}, u32[]{:S(2)}) collective-permute-start(f32[64,128]{1,0:T(8,128)S(1)} %get-tuple-element.73), channel_id=1, source_target_pairs={{0,15},{1,2},{2,1},{3,4},{4,3},{5,6},{6,5},{7,8},{8,7},{9,10},{10,... | collective-permute-start | bytes 98312 | tf_op jit(solution)/shard_map/ppermute | solution.py:54
  38.8 8.4 %collective-permute-start.12 = (f32[192,128]{1,0:T(8,128)S(1)}, f32[192,128]{1,0:T(8,128)S(1)}, u32[]{:S(2)}, u32[]{:S(2)}) collective-permute-start(f32[192,128]{1,0:T(8,128)S(1)} %late_far.1), channel_id=1, source_target_pairs={{0,15},{1,2},{2,1},{3,4},{4,3},{5,6},{6,5},{7,8},{8,7},{9,10},{10,... | collective-permute-start | bytes 294920 | tf_op jit(solution)/shard_map/ppermute | solution.py:54
  42.8 4.7 %collective-permute-start.13 = (f32[192,128]{1,0:T(8,128)S(1)}, f32[192,128]{1,0:T(8,128)S(1)}, u32[]{:S(2)}, u32[]{:S(2)}) collective-permute-start(f32[192,128]{1,0:T(8,128)S(1)} %late_near.1), channel_id=1, source_target_pairs={{0,1},{1,0},{2,3},{3,2},{4,5},{5,4},{6,7},{7,6},{8,9},{9,8},{10,11... | collective-permute-start | bytes 294920 | tf_op jit(solution)/shard_map/ppermute | solution.py:58
  47.5 1.9 %collective-permute-start.14 = (f32[192,128]{1,0:T(8,128)S(1)}, f32[192,128]{1,0:T(8,128)S(1)}, u32[]{:S(2)}, u32[]{:S(2)}) collective-permute-start(f32[192,128]{1,0:T(8,128)S(1)} %get-tuple-element.82), channel_id=1, source_target_pairs={{0,16},{16,0},{32,48},{48,32},{64,80},{80,64},{96,112},{112,96},{1... | collective-permute-start | bytes 294920 | tf_op jit(solution)/shard_map/ppermute | solution.py:58
  47.6 6.3 %collective-permute-start.15 = (f32[192,128]{1,0:T(8,128)S(1)}, f32[192,128]{1,0:T(8,128)S(1)}, u32[]{:S(2)}, u32[]{:S(2)}) collective-permute-start(f32[192,128]{1,0:T(8,128)S(1)} %get-tuple-element.84.refs_3_), channel_id=1, source_target_pairs={{0,112},{16,32},{32,16},{48,64},{64,48},{80,96},{96,80},{112,0},{1... | collective-permute-start | bytes 294920 | tf_op jit(solution)/shard_map/ppermute | solution.py:54
  49.7 4.7 %collective-permute-start.16 = (f32[72,128]{1,0:T(8,128)S(1)}, f32[72,128]{1,0:T(8,128)S(1)}, u32[]{:S(2)}, u32[]{:S(2)}) collective-permute-start(f32[72,128]{1,0:T(8,128)S(1)} %get-tuple-element.85), channel_id=1, source_target_pairs={{0,112},{16,32},{32,16},{48,64},{64,48},{80,96},{96,80},{112,0},{1... | collective-permute-start | bytes 110600 | tf_op jit(solution)/shard_map/ppermute | solution.py:54
  54.6 1.3 %collective-permute-start.17 = (f32[64,128]{1,0:T(8,128)S(1)}, f32[64,128]{1,0:T(8,128)S(1)}, u32[]{:S(2)}, u32[]{:S(2)}) collective-permute-start(f32[64,128]{1,0:T(8,128)S(1)} %get-tuple-element.88), channel_id=1, source_target_pairs={{0,16},{16,0},{32,48},{48,32},{64,80},{80,64},{96,112},{112,96},{1... | collective-permute-start | bytes 98312 | tf_op jit(solution)/shard_map/ppermute | solution.py:58
  56.0 7.3 %collective-permute-start.18 = (f32[64,128]{1,0:T(8,128)S(1)}, f32[64,128]{1,0:T(8,128)S(1)}, u32[]{:S(2)}, u32[]{:S(2)}) collective-permute-start(f32[64,128]{1,0:T(8,128)S(1)} %get-tuple-element.91), channel_id=1, source_target_pairs={{0,15},{1,2},{2,1},{3,4},{4,3},{5,6},{6,5},{7,8},{8,7},{9,10},{10,... | collective-permute-start | bytes 98312 | tf_op jit(solution)/shard_map/ppermute | solution.py:54
  59.2 4.2 %collective-permute-start.19 = (f32[64,128]{1,0:T(8,128)S(1)}, f32[64,128]{1,0:T(8,128)S(1)}, u32[]{:S(2)}, u32[]{:S(2)}) collective-permute-start(f32[64,128]{1,0:T(8,128)S(1)} %get-tuple-element.89.refs_9_), channel_id=1, source_target_pairs={{0,1},{1,0},{2,3},{3,2},{4,5},{5,4},{6,7},{7,6},{8,9},{9,8},{10,11... | collective-permute-start | bytes 98312 | tf_op jit(solution)/shard_map/ppermute | solution.py:58

commit v6 on v5

--- a/solution.py
+++ b/solution.py
@@ -371,21 +371,20 @@
 SIDES = (1, 6)
 
 
-def side(rows, far):
-    even = lax.axis_index("fy") % 2 == 0
-    pairs = [(rows[b : b + 1], rows[a : a + 1]) for b, a in zip(BEHIND, AHEAD)]
-    if far:
-        return [jnp.where(even, behind, ahead) for behind, ahead in pairs]
-    return [jnp.where(even, ahead, behind) for behind, ahead in pairs]
-
-
-def sides_first(rows):
-    return jnp.concatenate(side(rows, True) + side(rows, False) + [rows[0:2]], axis=0)
-
-
-def reply_y_body(table, x_first, x_second, y_first, y_second, far, near):
-    rows = asked_rows(0, asked_blocks(x_first, x_second, y_first, y_second))
-    pick, cx, cy = [sides_first(block) for block in rows]
+def partner_rows(s, asked):
+    return [
+        jnp.concatenate([asked[k * 8 + 3 * s + q : k * 8 + 3 * s + q + 1, :] for k in range(3)], axis=0)
+        for q in range(3)
+    ]
+
+
+def partners_rows(s, far, near):
+    pairs = zip(partner_rows(s, far), partner_rows(s, near))
+    return [jnp.concatenate(pair, axis=0) for pair in pairs]
+
+
+def reply_y_body(table, asked_far, asked_near, far, near):
+    pick, cx, cy = partners_rows(0, asked_far, asked_near)
     values = answer(table, pick, weights_of(cx, cy), ((0, 1), (2, 3), (4, 5)))
     for k in range(3):
         far[k * F : (k + 1) * F, :] = values[k]
@@ -399,21 +398,11 @@
         own[k * F : (k + 1) * F, :] = values[d]
 
 
-def partner_rows(s, asked):
-    return [
-        jnp.concatenate([asked[k * 8 + 3 * s + q : k * 8 + 3 * s + q + 1, :] for k in range(3)], axis=0)
-        for q in range(3)
-    ]
-
-
 def between_body(
     weighted, x_first, x_second, inverse, asked_far, asked_near, summed, values, lanes, shares, table
 ):
     sum_body(weighted, x_first, x_second, inverse, summed, table)
-    pick, cx, cy = [
-        jnp.concatenate(pair, axis=0)
-        for pair in zip(partner_rows(1, asked_far), partner_rows(1, asked_near))
-    ]
+    pick, cx, cy = partners_rows(1, asked_far, asked_near)
     weights = weights_of(cx, cy)
     for d, value in answer(table, pick, weights, ((0, 1), (2, 3), (4, 5))).items():
         values[d] = value
@@ -702,8 +691,8 @@
         count=1,
         scratch=[pltpu.VMEM(tracers.shape, F32), pltpu.SemaphoreType.DMA((1,))],
     )(in_hbm(tracers))
-    far, near = call(reply_y_body, [answers] * 2, "reply_y", count=5, after=1)(
-        table, *asked, now[2]
+    far, near = call(reply_y_body, [answers] * 2, "reply_y", count=3, after=1)(
+        table, asked[2], asked[3], now[2]
     )
     answers_y = swap("fy", far, near)
     inverse, scale = call(scale_body, [shape((NODES, E)), shape((8, 128))], "scale", count=5)(

time: 64.8 us -> 64.8 us (level)
  no operation moved by 1% of the time
where the time goes in v6:
time: 64.8 us; the launch traced here: 64.5 us
  starting transfers between devices  29.4 us (45%)
  Pallas kernels  27 us (42%)
  waiting for transfers between devices  7.6 us (12%)
    ppermute x10, starting transfers between devices, swap_far(): return lax.ppermute(block, axis, pairs)  27.8 us
    ppermute x10, waiting for transfers between devices, swap_far(): return lax.ppermute(block, axis, pairs)  6.06 us
    pallas_call x2, Pallas kernels, per_device(): own_a = interpolate(s, 0)(table, picks, factors)  5.14 us
    pallas_call x2, Pallas kernels, per_device(): own_b = interpolate(s, 1, after=1)(table, picks, factors, partial)  4.96 us
    pallas_call x1, Pallas kernels, per_device(): call(order_body, requests + [shape((8, POINTS), jnp.int32), shape((8, 128...  1.91 us
    ppermute x10, starting transfers between devices, swap_near(): lax.ppermute(block, axis, [(i, i ^ 1) for i in range(lax.axis_size(axis))])  1.65 us
    ppermute x10, waiting for transfers between devices, swap_near(): lax.ppermute(block, axis, [(i, i ^ 1) for i in range(lax.axis_size(axis))])  1.54 us
    pallas_call x1, Pallas kernels, per_device(): call(table_body, table_shape, 'table', hbm=(0,), count=1, scratch=[pltpu....  1.54 us
  transfers between devices with their start and end apart: 20, of which 10 were waited for; matrix products, arithmetic and copies ran while one was open for 0% of the time, Pallas kernels for 36%

profile of v6, /device:TPU:0, one launch (start us, length us, event | category | flops | bytes accessed | tf_op | source)
XLA Modules:
  0.0 64.5 jit_solution(10007773673265345274)
XLA Ops:
  0.0 1.2 %asks.1 = (f32[24,128]{1,0:T(8,128)S(1)}, f32[24,128]{1,0:T(8,128)S(1)}, f32[24,128]{1,0:T(8,128)S(1)}, f32[8,256]{1,0:T(8,128)S(1)}) custom-call(s32[2,1,10]{2,1,0:T(1,128)} %refs_0_.6, s32[2,4096]{1,0:T(2,128)} %refs_1_.3, s32[2,2,4096]{2,1,0:T(2,128)} %refs_2_.3, f32[16,256]{1,0:T(8,128)} %refs_8_.3), custom_call_target="tpu_custom_call" | custom-call | tf_op jit(solution)/shard_map/asks/pallas_call | solution.py:645
  1.2 2.6 %collective-permute-start = (f32[24,128]{1,0:T(8,128)S(1)}, f32[24,128]{1,0:T(8,128)S(1)}, u32[]{:S(2)}, u32[]{:S(2)}) collective-permute-start(f32[24,128]{1,0:T(8,128)S(1)} %get-tuple-element.52), channel_id=1, source_target_pairs={{0,112},{16,32},{32,16},{48,64},{64,48},{80,96},{96,80},{112,0},{1... | collective-permute-start | bytes 36872 | tf_op jit(solution)/shard_map/ppermute | solution.py:54
  3.8 1.8 %collective-permute-done.refs_0_.refs_1_ = f32[24,128]{1,0:T(8,128)S(1)} collective-permute-done((f32[24,128]{1,0:T(8,128)S(1)}, f32[24,128]{1,0:T(8,128)S(1)}, u32[]{:S(2)}, u32[]{:S(2)}) %collective-permute-start) | collective-permute-done | bytes 12320 | tf_op jit(solution)/shard_map/ppermute | solution.py:54
  5.7 6.4 %collective-permute-start.2 = (f32[24,128]{1,0:T(8,128)S(1)}, f32[24,128]{1,0:T(8,128)S(1)}, u32[]{:S(2)}, u32[]{:S(2)}) collective-permute-start(f32[24,128]{1,0:T(8,128)S(1)} %get-tuple-element.56), channel_id=1, source_target_pairs={{0,15},{1,2},{2,1},{3,4},{4,3},{5,6},{6,5},{7,8},{8,7},{9,10},{10,... | collective-permute-start | bytes 36872 | tf_op jit(solution)/shard_map/ppermute | solution.py:54
  12.0 1.9 %order.2 = (f32[2,32,128]{2,1,0:T(8,128)S(1)}, f32[24,32,128]{2,1,0:T(8,128)S(1)}, f32[8,256]{1,0:T(8,128)S(1)}, s32[8,4096]{1,0:T(8,128)S(1)}, s32[8,128]{1,0:T(8,128)S(1)}) custom-call(s32[2,1,10]{2,1,0:T(1,128)} %refs_0_.6, s32[2,1,4096]{2,1,0:T(1,128)} %refs_1_.2, s32[2,4096]{1,0:T(2,128)} %refs_1_.3, s32[2,2,4096]{2,1,0:T(2,128)} %refs_2_.3), custom_call_target="tpu_custom_call" | custom-call | tf_op jit(solution)/shard_map/order/pallas_call | solution.py:661
  13.9 1.5 %table.1.refs_0_ = bf16[1024,512]{1,0:T(8,128)(2,1)S(1)} custom-call(f32[64,16,256]{2,1,0:T(8,128)} %refs_0_.4), custom_call_target="tpu_custom_call" | custom-call | tf_op jit(solution)/shard_map/table/pallas_call | solution.py:686
  15.5 0.2 collective-permute-done.3.refs_2_.refs_4_.refs_5_
  15.7 1.0 %reply_y.1 = (f32[192,128]{1,0:T(8,128)S(1)}, f32[192,128]{1,0:T(8,128)S(1)}) custom-call(bf16[1024,512]{1,0:T(8,128)(2,1)S(1)} %table.1.refs_0_, f32[24,128]{1,0:T(8,128)S(1)} %collective-permute-done.2.refs_1_.refs_3_.refs_4_, f32[24,128]{1,0:T(8,128)S(1)} %collective-permute-done.3.refs_2_.refs_4_.refs_5_, ...), custom_call_target="tpu_custom_call" | custom-call | tf_op jit(solution)/shard_map/reply_y/pallas_call | solution.py:694
  16.7 3.4 %collective-permute-start.4 = (f32[192,128]{1,0:T(8,128)S(1)}, f32[192,128]{1,0:T(8,128)S(1)}, u32[]{:S(2)}, u32[]{:S(2)}) collective-permute-start(f32[192,128]{1,0:T(8,128)S(1)} %get-tuple-element.58), channel_id=1, source_target_pairs={{0,15},{1,2},{2,1},{3,4},{4,3},{5,6},{6,5},{7,8},{8,7},{9,10},{10,... | collective-permute-start | bytes 294920 | tf_op jit(solution)/shard_map/ppermute | solution.py:54
  20.1 0.4 own_faces.2.refs_5_.refs_0_
  20.6 3.1 %own.4.refs_3_.refs_0_ = f32[64,2560]{1,0:T(8,128)S(1)} custom-call(bf16[1024,512]{1,0:T(8,128)(2,1)S(1)} %table.1.refs_0_, f32[2,32,128]{2,1,0:T(8,128)S(1)} %get-tuple-element.49.refs_1_.refs_6_, f32[24,32,128]{2,1,0:T(8,128)S(1)} %get-tuple-element.50.refs_2_.refs_7_), custom_call_target="tpu_custom_call" | custom-call | tf_op jit(solution)/shard_map/own/pallas_call | solution.py:709
  23.7 0.3 scale.1
  23.9 0.5 reply_x.2.refs_2_
  24.4 0.3 collective-permute-done.4.refs_0_.refs_2_.refs_4_
  24.9 2.5 %collective-permute-start.7 = (f32[192,128]{1,0:T(8,128)S(1)}, f32[192,128]{1,0:T(8,128)S(1)}, u32[]{:S(2)}, u32[]{:S(2)}) collective-permute-start(f32[192,128]{1,0:T(8,128)S(1)} %get-tuple-element.63.refs_3_), channel_id=1, source_target_pairs={{0,112},{16,32},{32,16},{48,64},{64,48},{80,96},{96,80},{112,0},{1... | collective-permute-start | bytes 294920 | tf_op jit(solution)/shard_map/ppermute | solution.py:54
  27.4 0.2 faces_near.2
  27.6 1.0 %collective-permute-start.8 = (f32[72,128]{1,0:T(8,128)S(1)}, f32[72,128]{1,0:T(8,128)S(1)}, u32[]{:S(2)}, u32[]{:S(2)}) collective-permute-start(f32[72,128]{1,0:T(8,128)S(1)} %get-tuple-element.64), channel_id=1, source_target_pairs={{0,112},{16,32},{32,16},{48,64},{64,48},{80,96},{96,80},{112,0},{1... | collective-permute-start | bytes 110600 | tf_op jit(solution)/shard_map/ppermute | solution.py:54
  28.7 2.0 %own.5.refs_6_.refs_1_ = f32[64,1536]{1,0:T(8,128)S(1)} custom-call(bf16[1024,512]{1,0:T(8,128)(2,1)S(1)} %table.1.refs_0_, f32[2,32,128]{2,1,0:T(8,128)S(1)} %get-tuple-element.49.refs_1_.refs_6_, f32[24,32,128]{2,1,0:T(8,128)S(1)} %get-tuple-element.50.refs_2_.refs_7_, f32[64,256]{1,0:T(8,128)S(1)} %get-tuple-element.62.refs_3_.refs_2_.refs_0_), custom_call_target="tpu_custom_call" | custom-call | tf_op jit(solution)/shard_map/own/pallas_call | solution.py:719
  30.7 1.0 %order.3 = (f32[2,32,128]{2,1,0:T(8,128)S(1)}, f32[24,32,128]{2,1,0:T(8,128)S(1)}, f32[8,256]{1,0:T(8,128)S(1)}) custom-call(s32[8,4096]{1,0:T(8,128)S(1)} %get-tuple-element.65.refs_0_, s32[8,128]{1,0:T(8,128)S(1)} %get-tuple-element.66.refs_1_, f32[64,256]{1,0:T(8,128)S(1)} %get-tuple-element.62.refs_3_.refs_2_.refs_0_), custom_call_target="tpu_custom_call" | custom-call | tf_op jit(solution)/shard_map/order/pallas_call | solution.py:722
  31.7 0.7 %collective-permute-done.8.refs_2_ = f32[72,128]{1,0:T(8,128)S(1)} collective-permute-done((f32[72,128]{1,0:T(8,128)S(1)}, f32[72,128]{1,0:T(8,128)S(1)}, u32[]{:S(2)}, u32[]{:S(2)}) %collective-permute-start.8) | collective-permute-done | bytes 36896 | tf_op jit(solution)/shard_map/ppermute | solution.py:54
  32.3 0.2 faces_far.2
  32.6 1.3 %place.2.refs_0_.refs_3_ = f32[64,4096]{1,0:T(8,128)S(1)} custom-call(f32[64,2560]{1,0:T(8,128)S(1)} %own.4.refs_3_.refs_0_, f32[64,1536]{1,0:T(8,128)S(1)} %own.5.refs_6_.refs_1_, f32[192,128]{1,0:T(8,128)S(1)} %collective-permute-done.7.refs_1_.refs_2_, f32[192,128]{1,0:T(8,128)S(1)} %collective-permute-done.6.refs_1_.refs_3_, ...), custom_call_target="tpu_custom_call" | custom-call | tf_op jit(solution)/shard_map/place/pallas_call | solution.py:739
  33.9 0.1 rim.2
  34.1 1.2 %collective-permute-start.11 = (f32[64,128]{1,0:T(8,128)S(1)}, f32[64,128]{1,0:T(8,128)S(1)}, u32[]{:S(2)}, u32[]{:S(2)}) collective-permute-start(f32[64,128]{1,0:T(8,128)S(1)} %get-tuple-element.74), channel_id=1, source_target_pairs={{0,1},{1,0},{2,3},{3,2},{4,5},{5,4},{6,7},{7,6},{8,9},{9,8},{10,11... | collective-permute-start | bytes 98312 | tf_op jit(solution)/shard_map/ppermute | solution.py:58
  35.3 2.0 %collective-permute-start.10 = (f32[64,128]{1,0:T(8,128)S(1)}, f32[64,128]{1,0:T(8,128)S(1)}, u32[]{:S(2)}, u32[]{:S(2)}) collective-permute-start(f32[64,128]{1,0:T(8,128)S(1)} %get-tuple-element.73), channel_id=1, source_target_pairs={{0,15},{1,2},{2,1},{3,4},{4,3},{5,6},{6,5},{7,8},{8,7},{9,10},{10,... | collective-permute-start | bytes 98312 | tf_op jit(solution)/shard_map/ppermute | solution.py:54
  37.3 1.2 %between.1 = (f32[64,4096]{1,0:T(8,128)S(1)}, f32[6,64,128]{2,1,0:T(8,128)S(1)}, s32[8,128]{1,0:T(8,128)S(1)}, f32[4,8,128]{2,1,0:T(8,128)S(1)}) custom-call(f32[64,4096]{1,0:T(8,128)S(1)} %place.2.refs_0_.refs_3_, f32[64,128]{1,0:T(8,128)S(1)} %get-tuple-element.68.refs_9_.refs_1_, f32[64,128]{1,0:T(8,128)S(1)} %collective-permute-done.9.refs_2_, ...), custom_call_target="tpu_custom_call" | custom-call | tf_op jit(solution)/shard_map/between/pallas_call | solution.py:748
  38.5 0.3 late_far.1
  38.7 3.6 %collective-permute-start.12 = (f32[192,128]{1,0:T(8,128)S(1)}, f32[192,128]{1,0:T(8,128)S(1)}, u32[]{:S(2)}, u32[]{:S(2)}) collective-permute-start(f32[192,128]{1,0:T(8,128)S(1)} %late_far.1), channel_id=1, source_target_pairs={{0,15},{1,2},{2,1},{3,4},{4,3},{5,6},{6,5},{7,8},{8,7},{9,10},{10,... | collective-permute-start | bytes 294920 | tf_op jit(solution)/shard_map/ppermute | solution.py:54
  42.4 0.1 collective-permute-done.10.refs_1_.refs_3_
  42.5 0.3 late_near.1
  42.9 0.4 finish.1.refs_0_
  43.3 0.4 own_faces.3.refs_5_.refs_0_
  43.7 2.1 %own.6.refs_3_.refs_0_ = f32[64,1792]{1,0:T(8,128)S(1)} custom-call(bf16[1024,512]{1,0:T(8,128)(2,1)S(1)} %finish.1.refs_0_, f32[2,32,128]{2,1,0:T(8,128)S(1)} %get-tuple-element.75.refs_1_.refs_6_, f32[24,32,128]{2,1,0:T(8,128)S(1)} %get-tuple-element.76.refs_2_.refs_7_), custom_call_target="tpu_custom_call" | custom-call | tf_op jit(solution)/shard_map/own/pallas_call | solution.py:709
  45.8 0.5 reply_x.3.refs_2_
  46.3 0.9 %collective-permute-done.12.refs_0_ = f32[192,128]{1,0:T(8,128)S(1)} collective-permute-done((f32[192,128]{1,0:T(8,128)S(1)}, f32[192,128]{1,0:T(8,128)S(1)}, u32[]{:S(2)}, u32[]{:S(2)}) %collective-permute-start.12) | collective-permute-done | bytes 98336 | tf_op jit(solution)/shard_map/ppermute | solution.py:54
  47.2 0.2 fix.1.refs_0_.refs_2_.refs_4_
  47.6 1.8 %collective-permute-start.15 = (f32[192,128]{1,0:T(8,128)S(1)}, f32[192,128]{1,0:T(8,128)S(1)}, u32[]{:S(2)}, u32[]{:S(2)}) collective-permute-start(f32[192,128]{1,0:T(8,128)S(1)} %get-tuple-element.84.refs_3_), channel_id=1, source_target_pairs={{0,112},{16,32},{32,16},{48,64},{64,48},{80,96},{96,80},{112,0},{1... | collective-permute-start | bytes 294920 | tf_op jit(solution)/shard_map/ppermute | solution.py:54
  49.5 0.2 faces_near.3
  49.7 1.3 %collective-permute-start.16 = (f32[72,128]{1,0:T(8,128)S(1)}, f32[72,128]{1,0:T(8,128)S(1)}, u32[]{:S(2)}, u32[]{:S(2)}) collective-permute-start(f32[72,128]{1,0:T(8,128)S(1)} %get-tuple-element.85), channel_id=1, source_target_pairs={{0,112},{16,32},{32,16},{48,64},{64,48},{80,96},{96,80},{112,0},{1... | collective-permute-start | bytes 110600 | tf_op jit(solution)/shard_map/ppermute | solution.py:54
  51.0 3.0 %own.7.refs_6_.refs_1_ = f32[64,2304]{1,0:T(8,128)S(1)} custom-call(bf16[1024,512]{1,0:T(8,128)(2,1)S(1)} %finish.1.refs_0_, f32[2,32,128]{2,1,0:T(8,128)S(1)} %get-tuple-element.75.refs_1_.refs_6_, f32[24,32,128]{2,1,0:T(8,128)S(1)} %get-tuple-element.76.refs_2_.refs_7_, f32[64,256]{1,0:T(8,128)S(1)} %get-tuple-element.83.refs_3_.refs_0_), custom_call_target="tpu_custom_call" | custom-call | tf_op jit(solution)/shard_map/own/pallas_call | solution.py:719
  54.0 0.4 collective-permute-done.16.refs_2_
  54.4 0.2 faces_far.3
  54.7 1.2 %collective-permute-done.17.refs_2_.x_second = f32[64,128]{1,0:T(8,128)S(1)} collective-permute-done((f32[64,128]{1,0:T(8,128)S(1)}, f32[64,128]{1,0:T(8,128)S(1)}, u32[]{:S(2)}, u32[]{:S(2)}) %collective-permute-start.17) | collective-permute-done | bytes 32800 | tf_op jit(solution)/shard_map/ppermute | solution.py:58
  56.0 3.1 %collective-permute-start.18 = (f32[64,128]{1,0:T(8,128)S(1)}, f32[64,128]{1,0:T(8,128)S(1)}, u32[]{:S(2)}, u32[]{:S(2)}) collective-permute-start(f32[64,128]{1,0:T(8,128)S(1)} %get-tuple-element.91), channel_id=1, source_target_pairs={{0,15},{1,2},{2,1},{3,4},{4,3},{5,6},{6,5},{7,8},{8,7},{9,10},{10,... | collective-permute-start | bytes 98312 | tf_op jit(solution)/shard_map/ppermute | solution.py:54
  59.2 1.3 %place.3.weighted = f32[64,4096]{1,0:T(8,128)S(1)} custom-call(f32[64,1792]{1,0:T(8,128)S(1)} %own.6.refs_3_.refs_0_, f32[64,2304]{1,0:T(8,128)S(1)} %own.7.refs_6_.refs_1_, f32[192,128]{1,0:T(8,128)S(1)} %collective-permute-done.15.refs_1_.refs_2_, f32[192,128]{1,0:T(8,128)S(1)} %collective-permute-done.14.refs_1_.refs_3_, ...), custom_call_target="tpu_custom_call" | custom-call | tf_op jit(solution)/shard_map/place/pallas_call | solution.py:745
  60.4 1.1 %inner.1 = (f32[64,2048]{1,0:T(8,128)S(1)}, f32[64,16,256]{2,1,0:T(8,128)}) custom-call(f32[64,4096]{1,0:T(8,128)S(1)} %place.3.weighted, f32[64,128]{1,0:T(8,128)S(1)} %get-tuple-element.87.refs_1_.x_first, f32[64,128]{1,0:T(8,128)S(1)} %collective-permute-done.17.refs_2_.x_second, f32[16,256]{1,0:T(8,128)S(1)} %get-tuple-element.70.refs_3_.inverse), custom_call_target="tpu_custom_call" | custom-call | tf_op jit(solution)/shard_map/inner/pallas_call | solution.py:771
  61.5 1.8 %collective-permute-done.18.y_first = f32[64,128]{1,0:T(8,128)S(1)} collective-permute-done((f32[64,128]{1,0:T(8,128)S(1)}, f32[64,128]{1,0:T(8,128)S(1)}, u32[]{:S(2)}, u32[]{:S(2)}) %collective-permute-start.18) | collective-permute-done | bytes 32800 | tf_op jit(solution)/shard_map/ppermute | solution.py:54
  63.3 1.0 %last.1 = f32[64,16,256]{2,1,0:T(8,128)} custom-call(f32[64,2048]{1,0:T(8,128)S(1)} %get-tuple-element.90.part, f32[64,128]{1,0:T(8,128)S(1)} %collective-permute-done.18.y_first, f32[64,128]{1,0:T(8,128)S(1)} %collective-permute-done.19.y_second, f32[8,128]{1,0:T(8,128)S(1)} %get-tuple-element.60.refs_4_.refs_3_.refs_5_.scale, ...), custom_call_target="tpu_custom_call", output_to_operand_aliasing={{}: (4, {})} | custom-call | tf_op jit(solution)/shard_map/last/pallas_call | solution.py:780
  (26 shorter events, 0.8 us)
Async XLA Ops:
  1.2 4.4 %collective-permute-start = (f32[24,128]{1,0:T(8,128)S(1)}, f32[24,128]{1,0:T(8,128)S(1)}, u32[]{:S(2)}, u32[]{:S(2)}) collective-permute-start(f32[24,128]{1,0:T(8,128)S(1)} %get-tuple-element.52), channel_id=1, source_target_pairs={{0,112},{16,32},{32,16},{48,64},{64,48},{80,96},{96,80},{112,0},{1... | collective-permute-start | bytes 36872 | tf_op jit(solution)/shard_map/ppermute | solution.py:54
  3.8 1.8 %collective-permute-start.1 = (f32[24,128]{1,0:T(8,128)S(1)}, f32[24,128]{1,0:T(8,128)S(1)}, u32[]{:S(2)}, u32[]{:S(2)}) collective-permute-start(f32[24,128]{1,0:T(8,128)S(1)} %get-tuple-element.53), channel_id=1, source_target_pairs={{0,16},{16,0},{32,48},{48,32},{64,80},{80,64},{96,112},{112,96},{1... | collective-permute-start | bytes 36872 | tf_op jit(solution)/shard_map/ppermute | solution.py:58
  5.7 9.8 %collective-permute-start.2 = (f32[24,128]{1,0:T(8,128)S(1)}, f32[24,128]{1,0:T(8,128)S(1)}, u32[]{:S(2)}, u32[]{:S(2)}) collective-permute-start(f32[24,128]{1,0:T(8,128)S(1)} %get-tuple-element.56), channel_id=1, source_target_pairs={{0,15},{1,2},{2,1},{3,4},{4,3},{5,6},{6,5},{7,8},{8,7},{9,10},{10,... | collective-permute-start | bytes 36872 | tf_op jit(solution)/shard_map/ppermute | solution.py:54
  12.0 3.7 %collective-permute-start.3 = (f32[24,128]{1,0:T(8,128)S(1)}, f32[24,128]{1,0:T(8,128)S(1)}, u32[]{:S(2)}, u32[]{:S(2)}) collective-permute-start(f32[24,128]{1,0:T(8,128)S(1)} %get-tuple-element.57), channel_id=1, source_target_pairs={{0,1},{1,0},{2,3},{3,2},{4,5},{5,4},{6,7},{7,6},{8,9},{9,8},{10,11... | collective-permute-start | bytes 36872 | tf_op jit(solution)/shard_map/ppermute | solution.py:58
  16.7 8.0 %collective-permute-start.4 = (f32[192,128]{1,0:T(8,128)S(1)}, f32[192,128]{1,0:T(8,128)S(1)}, u32[]{:S(2)}, u32[]{:S(2)}) collective-permute-start(f32[192,128]{1,0:T(8,128)S(1)} %get-tuple-element.58), channel_id=1, source_target_pairs={{0,15},{1,2},{2,1},{3,4},{4,3},{5,6},{6,5},{7,8},{8,7},{9,10},{10,... | collective-permute-start | bytes 294920 | tf_op jit(solution)/shard_map/ppermute | solution.py:54
  20.1 4.6 %collective-permute-start.5 = (f32[192,128]{1,0:T(8,128)S(1)}, f32[192,128]{1,0:T(8,128)S(1)}, u32[]{:S(2)}, u32[]{:S(2)}) collective-permute-start(f32[192,128]{1,0:T(8,128)S(1)} %get-tuple-element.59), channel_id=1, source_target_pairs={{0,1},{1,0},{2,3},{3,2},{4,5},{5,4},{6,7},{7,6},{8,9},{9,8},{10,11... | collective-permute-start | bytes 294920 | tf_op jit(solution)/shard_map/ppermute | solution.py:58
  20.6 3.1 %copy-start = (f32[16,256]{1,0:T(8,128)S(1)}, f32[16,256]{1,0:T(8,128)}, u32[]{:S(2)}) copy-start(f32[16,256]{1,0:T(8,128)} %refs_8_.3) | copy-start | bytes 49156
  24.8 2.6 %collective-permute-start.6 = (f32[192,128]{1,0:T(8,128)S(1)}, f32[192,128]{1,0:T(8,128)S(1)}, u32[]{:S(2)}, u32[]{:S(2)}) collective-permute-start(f32[192,128]{1,0:T(8,128)S(1)} %get-tuple-element.61), channel_id=1, source_target_pairs={{0,16},{16,0},{32,48},{48,32},{64,80},{80,64},{96,112},{112,96},{1... | collective-permute-start | bytes 294920 | tf_op jit(solution)/shard_map/ppermute | solution.py:58
  24.9 6.8 %collective-permute-start.7 = (f32[192,128]{1,0:T(8,128)S(1)}, f32[192,128]{1,0:T(8,128)S(1)}, u32[]{:S(2)}, u32[]{:S(2)}) collective-permute-start(f32[192,128]{1,0:T(8,128)S(1)} %get-tuple-element.63.refs_3_), channel_id=1, source_target_pairs={{0,112},{16,32},{32,16},{48,64},{64,48},{80,96},{96,80},{112,0},{1... | collective-permute-start | bytes 294920 | tf_op jit(solution)/shard_map/ppermute | solution.py:54
  27.6 4.7 %collective-permute-start.8 = (f32[72,128]{1,0:T(8,128)S(1)}, f32[72,128]{1,0:T(8,128)S(1)}, u32[]{:S(2)}, u32[]{:S(2)}) collective-permute-start(f32[72,128]{1,0:T(8,128)S(1)} %get-tuple-element.64), channel_id=1, source_target_pairs={{0,112},{16,32},{32,16},{48,64},{64,48},{80,96},{96,80},{112,0},{1... | collective-permute-start | bytes 110600 | tf_op jit(solution)/shard_map/ppermute | solution.py:54
  32.5 1.4 %collective-permute-start.9 = (f32[64,128]{1,0:T(8,128)S(1)}, f32[64,128]{1,0:T(8,128)S(1)}, u32[]{:S(2)}, u32[]{:S(2)}) collective-permute-start(f32[64,128]{1,0:T(8,128)S(1)} %get-tuple-element.69), channel_id=1, source_target_pairs={{0,16},{16,0},{32,48},{48,32},{64,80},{80,64},{96,112},{112,96},{1... | collective-permute-start | bytes 98312 | tf_op jit(solution)/shard_map/ppermute | solution.py:58
  34.1 4.4 %collective-permute-start.11 = (f32[64,128]{1,0:T(8,128)S(1)}, f32[64,128]{1,0:T(8,128)S(1)}, u32[]{:S(2)}, u32[]{:S(2)}) collective-permute-start(f32[64,128]{1,0:T(8,128)S(1)} %get-tuple-element.74), channel_id=1, source_target_pairs={{0,1},{1,0},{2,3},{3,2},{4,5},{5,4},{6,7},{7,6},{8,9},{9,8},{10,11... | collective-permute-start | bytes 98312 | tf_op jit(solution)/shard_map/ppermute | solution.py:58
  35.3 7.2 %collective-permute-start.10 = (f32[64,128]{1,0:T(8,128)S(1)}, f32[64,128]{1,0:T(8,128)S(1)}, u32[]{:S(2)}, u32[]{:S(2)}) collective-permute-start(f32[64,128]{1,0:T(8,128)S(1)} %get-tuple-element.73), channel_id=1, source_target_pairs={{0,15},{1,2},{2,1},{3,4},{4,3},{5,6},{6,5},{7,8},{8,7},{9,10},{10,... | collective-permute-start | bytes 98312 | tf_op jit(solution)/shard_map/ppermute | solution.py:54
  38.7 8.4 %collective-permute-start.12 = (f32[192,128]{1,0:T(8,128)S(1)}, f32[192,128]{1,0:T(8,128)S(1)}, u32[]{:S(2)}, u32[]{:S(2)}) collective-permute-start(f32[192,128]{1,0:T(8,128)S(1)} %late_far.1), channel_id=1, source_target_pairs={{0,15},{1,2},{2,1},{3,4},{4,3},{5,6},{6,5},{7,8},{8,7},{9,10},{10,... | collective-permute-start | bytes 294920 | tf_op jit(solution)/shard_map/ppermute | solution.py:54
  42.8 4.7 %collective-permute-start.13 = (f32[192,128]{1,0:T(8,128)S(1)}, f32[192,128]{1,0:T(8,128)S(1)}, u32[]{:S(2)}, u32[]{:S(2)}) collective-permute-start(f32[192,128]{1,0:T(8,128)S(1)} %late_near.1), channel_id=1, source_target_pairs={{0,1},{1,0},{2,3},{3,2},{4,5},{5,4},{6,7},{7,6},{8,9},{9,8},{10,11... | collective-permute-start | bytes 294920 | tf_op jit(solution)/shard_map/ppermute | solution.py:58
  47.5 1.9 %collective-permute-start.14 = (f32[192,128]{1,0:T(8,128)S(1)}, f32[192,128]{1,0:T(8,128)S(1)}, u32[]{:S(2)}, u32[]{:S(2)}) collective-permute-start(f32[192,128]{1,0:T(8,128)S(1)} %get-tuple-element.82), channel_id=1, source_target_pairs={{0,16},{16,0},{32,48},{48,32},{64,80},{80,64},{96,112},{112,96},{1... | collective-permute-start | bytes 294920 | tf_op jit(solution)/shard_map/ppermute | solution.py:58
  47.6 6.3 %collective-permute-start.15 = (f32[192,128]{1,0:T(8,128)S(1)}, f32[192,128]{1,0:T(8,128)S(1)}, u32[]{:S(2)}, u32[]{:S(2)}) collective-permute-start(f32[192,128]{1,0:T(8,128)S(1)} %get-tuple-element.84.refs_3_), channel_id=1, source_target_pairs={{0,112},{16,32},{32,16},{48,64},{64,48},{80,96},{96,80},{112,0},{1... | collective-permute-start | bytes 294920 | tf_op jit(solution)/shard_map/ppermute | solution.py:54
  49.7 4.7 %collective-permute-start.16 = (f32[72,128]{1,0:T(8,128)S(1)}, f32[72,128]{1,0:T(8,128)S(1)}, u32[]{:S(2)}, u32[]{:S(2)}) collective-permute-start(f32[72,128]{1,0:T(8,128)S(1)} %get-tuple-element.85), channel_id=1, source_target_pairs={{0,112},{16,32},{32,16},{48,64},{64,48},{80,96},{96,80},{112,0},{1... | collective-permute-start | bytes 110600 | tf_op jit(solution)/shard_map/ppermute | solution.py:54
  54.6 1.3 %collective-permute-start.17 = (f32[64,128]{1,0:T(8,128)S(1)}, f32[64,128]{1,0:T(8,128)S(1)}, u32[]{:S(2)}, u32[]{:S(2)}) collective-permute-start(f32[64,128]{1,0:T(8,128)S(1)} %get-tuple-element.88), channel_id=1, source_target_pairs={{0,16},{16,0},{32,48},{48,32},{64,80},{80,64},{96,112},{112,96},{1... | collective-permute-start | bytes 98312 | tf_op jit(solution)/shard_map/ppermute | solution.py:58
  56.0 7.3 %collective-permute-start.18 = (f32[64,128]{1,0:T(8,128)S(1)}, f32[64,128]{1,0:T(8,128)S(1)}, u32[]{:S(2)}, u32[]{:S(2)}) collective-permute-start(f32[64,128]{1,0:T(8,128)S(1)} %get-tuple-element.91), channel_id=1, source_target_pairs={{0,15},{1,2},{2,1},{3,4},{4,3},{5,6},{6,5},{7,8},{8,7},{9,10},{10,... | collective-permute-start | bytes 98312 | tf_op jit(solution)/shard_map/ppermute | solution.py:54
  59.2 4.2 %collective-permute-start.19 = (f32[64,128]{1,0:T(8,128)S(1)}, f32[64,128]{1,0:T(8,128)S(1)}, u32[]{:S(2)}, u32[]{:S(2)}) collective-permute-start(f32[64,128]{1,0:T(8,128)S(1)} %get-tuple-element.89.refs_9_), channel_id=1, source_target_pairs={{0,1},{1,0},{2,3},{3,2},{4,5},{5,4},{6,7},{7,6},{8,9},{9,8},{10,11... | collective-permute-start | bytes 98312 | tf_op jit(solution)/shard_map/ppermute | solution.py:58

commit v7 on v6

--- a/solution.py
+++ b/solution.py
@@ -14,7 +14,7 @@
 NODES = 16
 POINTS = 4096
 TILES = POINTS // 128
-PIECES = (((0, 10), (10, 16)), ((0, 7), (7, 16)))
+PIECES = (((0, 9), (9, 16)), ((0, 8), (8, 16)))
 GLL_NODES = (-1.0, -0.4472135954999579, 0.4472135954999579, 1.0)
 REMOTE = (0, 1, 2, 3, 5, 6, 7, 8)
 BF16 = jnp.bfloat16
@@ -469,7 +469,7 @@
         return carry
 
     count = result.shape[1] // E
-    lax.fori_loop(0, count, block, 0, unroll=5 if count == 10 else 3 if count in (6, 9) else count)
+    lax.fori_loop(0, count, block, 0, unroll=3 if count == 9 else 4 if count == 8 else count)
 
 
 def stacked(blocks):

time: 64.8 us -> 64.8 us (level)
  transfers between devices with their start and end apart: 20 -> 20, of which waited for: 10 -> 9; matrix products, arithmetic and copies ran while one was open for 0% -> 0% of each run, Pallas kernels for 36% -> 36%
where the time goes in v7:
time: 64.8 us; the launch traced here: 64.6 us
  starting transfers between devices  29 us (45%)
  Pallas kernels  27 us (42%)
  waiting for transfers between devices  8.04 us (12%)
    ppermute x10, starting transfers between devices, swap_far(): return lax.ppermute(block, axis, pairs)  27.4 us
    ppermute x10, waiting for transfers between devices, swap_far(): return lax.ppermute(block, axis, pairs)  6.57 us
    pallas_call x2, Pallas kernels, per_device(): own_a = interpolate(s, 0)(table, picks, factors)  5.51 us
    pallas_call x2, Pallas kernels, per_device(): own_b = interpolate(s, 1, after=1)(table, picks, factors, partial)  4.61 us
    pallas_call x1, Pallas kernels, per_device(): call(order_body, requests + [shape((8, POINTS), jnp.int32), shape((8, 128...  1.91 us
    ppermute x10, starting transfers between devices, swap_near(): lax.ppermute(block, axis, [(i, i ^ 1) for i in range(lax.axis_size(axis))])  1.57 us
    pallas_call x1, Pallas kernels, per_device(): call(table_body, table_shape, 'table', hbm=(0,), count=1, scratch=[pltpu....  1.54 us
    ppermute x10, waiting for transfers between devices, swap_near(): lax.ppermute(block, axis, [(i, i ^ 1) for i in range(lax.axis_size(axis))])  1.47 us
  transfers between devices with their start and end apart: 20, of which 9 were waited for; matrix products, arithmetic and copies ran while one was open for 0% of the time, Pallas kernels for 36%

profile of v7, /device:TPU:0, one launch (start us, length us, event | category | flops | bytes accessed | tf_op | source)
XLA Modules:
  0.0 64.6 jit_solution(14523853153807291959)
XLA Ops:
  0.0 1.2 %asks.1 = (f32[24,128]{1,0:T(8,128)S(1)}, f32[24,128]{1,0:T(8,128)S(1)}, f32[24,128]{1,0:T(8,128)S(1)}, f32[8,256]{1,0:T(8,128)S(1)}) custom-call(s32[2,1,10]{2,1,0:T(1,128)} %refs_0_.6, s32[2,4096]{1,0:T(2,128)} %refs_1_.3, s32[2,2,4096]{2,1,0:T(2,128)} %refs_2_.3, f32[16,256]{1,0:T(8,128)} %refs_8_.3), custom_call_target="tpu_custom_call" | custom-call | tf_op jit(solution)/shard_map/asks/pallas_call | solution.py:645
  1.2 2.6 %collective-permute-start = (f32[24,128]{1,0:T(8,128)S(1)}, f32[24,128]{1,0:T(8,128)S(1)}, u32[]{:S(2)}, u32[]{:S(2)}) collective-permute-start(f32[24,128]{1,0:T(8,128)S(1)} %get-tuple-element.52), channel_id=1, source_target_pairs={{0,112},{16,32},{32,16},{48,64},{64,48},{80,96},{96,80},{112,0},{1... | collective-permute-start | bytes 36872 | tf_op jit(solution)/shard_map/ppermute | solution.py:54
  3.8 1.8 %collective-permute-done.refs_0_.refs_1_ = f32[24,128]{1,0:T(8,128)S(1)} collective-permute-done((f32[24,128]{1,0:T(8,128)S(1)}, f32[24,128]{1,0:T(8,128)S(1)}, u32[]{:S(2)}, u32[]{:S(2)}) %collective-permute-start) | collective-permute-done | bytes 12320 | tf_op jit(solution)/shard_map/ppermute | solution.py:54
  5.7 6.4 %collective-permute-start.2 = (f32[24,128]{1,0:T(8,128)S(1)}, f32[24,128]{1,0:T(8,128)S(1)}, u32[]{:S(2)}, u32[]{:S(2)}) collective-permute-start(f32[24,128]{1,0:T(8,128)S(1)} %get-tuple-element.56), channel_id=1, source_target_pairs={{0,15},{1,2},{2,1},{3,4},{4,3},{5,6},{6,5},{7,8},{8,7},{9,10},{10,... | collective-permute-start | bytes 36872 | tf_op jit(solution)/shard_map/ppermute | solution.py:54
  12.0 1.9 %order.2 = (f32[2,32,128]{2,1,0:T(8,128)S(1)}, f32[24,32,128]{2,1,0:T(8,128)S(1)}, f32[8,256]{1,0:T(8,128)S(1)}, s32[8,4096]{1,0:T(8,128)S(1)}, s32[8,128]{1,0:T(8,128)S(1)}) custom-call(s32[2,1,10]{2,1,0:T(1,128)} %refs_0_.6, s32[2,1,4096]{2,1,0:T(1,128)} %refs_1_.2, s32[2,4096]{1,0:T(2,128)} %refs_1_.3, s32[2,2,4096]{2,1,0:T(2,128)} %refs_2_.3), custom_call_target="tpu_custom_call" | custom-call | tf_op jit(solution)/shard_map/order/pallas_call | solution.py:661
  13.9 1.5 %table.1.refs_0_ = bf16[1024,512]{1,0:T(8,128)(2,1)S(1)} custom-call(f32[64,16,256]{2,1,0:T(8,128)} %refs_0_.4), custom_call_target="tpu_custom_call" | custom-call | tf_op jit(solution)/shard_map/table/pallas_call | solution.py:686
  15.5 0.2 collective-permute-done.3.refs_2_.refs_4_.refs_5_
  15.7 1.0 %reply_y.1 = (f32[192,128]{1,0:T(8,128)S(1)}, f32[192,128]{1,0:T(8,128)S(1)}) custom-call(bf16[1024,512]{1,0:T(8,128)(2,1)S(1)} %table.1.refs_0_, f32[24,128]{1,0:T(8,128)S(1)} %collective-permute-done.2.refs_1_.refs_3_.refs_4_, f32[24,128]{1,0:T(8,128)S(1)} %collective-permute-done.3.refs_2_.refs_4_.refs_5_, ...), custom_call_target="tpu_custom_call" | custom-call | tf_op jit(solution)/shard_map/reply_y/pallas_call | solution.py:694
  16.7 3.4 %collective-permute-start.4 = (f32[192,128]{1,0:T(8,128)S(1)}, f32[192,128]{1,0:T(8,128)S(1)}, u32[]{:S(2)}, u32[]{:S(2)}) collective-permute-start(f32[192,128]{1,0:T(8,128)S(1)} %get-tuple-element.58), channel_id=1, source_target_pairs={{0,15},{1,2},{2,1},{3,4},{4,3},{5,6},{6,5},{7,8},{8,7},{9,10},{10,... | collective-permute-start | bytes 294920 | tf_op jit(solution)/shard_map/ppermute | solution.py:54
  20.1 0.4 own_faces.2.refs_5_.refs_0_
  20.6 3.0 %own.4.refs_3_.refs_0_ = f32[64,2304]{1,0:T(8,128)S(1)} custom-call(bf16[1024,512]{1,0:T(8,128)(2,1)S(1)} %table.1.refs_0_, f32[2,32,128]{2,1,0:T(8,128)S(1)} %get-tuple-element.49.refs_1_.refs_6_, f32[24,32,128]{2,1,0:T(8,128)S(1)} %get-tuple-element.50.refs_2_.refs_7_), custom_call_target="tpu_custom_call" | custom-call | tf_op jit(solution)/shard_map/own/pallas_call | solution.py:709
  23.6 0.3 scale.1
  23.9 0.5 reply_x.2.refs_2_
  24.3 0.4 collective-permute-done.4.refs_0_.refs_2_.refs_4_
  24.9 2.5 %collective-permute-start.7 = (f32[192,128]{1,0:T(8,128)S(1)}, f32[192,128]{1,0:T(8,128)S(1)}, u32[]{:S(2)}, u32[]{:S(2)}) collective-permute-start(f32[192,128]{1,0:T(8,128)S(1)} %get-tuple-element.63.refs_3_), channel_id=1, source_target_pairs={{0,112},{16,32},{32,16},{48,64},{64,48},{80,96},{96,80},{112,0},{1... | collective-permute-start | bytes 294920 | tf_op jit(solution)/shard_map/ppermute | solution.py:54
  27.4 0.2 faces_near.2
  27.6 1.0 %collective-permute-start.8 = (f32[72,128]{1,0:T(8,128)S(1)}, f32[72,128]{1,0:T(8,128)S(1)}, u32[]{:S(2)}, u32[]{:S(2)}) collective-permute-start(f32[72,128]{1,0:T(8,128)S(1)} %get-tuple-element.64), channel_id=1, source_target_pairs={{0,112},{16,32},{32,16},{48,64},{64,48},{80,96},{96,80},{112,0},{1... | collective-permute-start | bytes 110600 | tf_op jit(solution)/shard_map/ppermute | solution.py:54
  28.7 2.1 %own.5.refs_6_.refs_1_ = f32[64,1792]{1,0:T(8,128)S(1)} custom-call(bf16[1024,512]{1,0:T(8,128)(2,1)S(1)} %table.1.refs_0_, f32[2,32,128]{2,1,0:T(8,128)S(1)} %get-tuple-element.49.refs_1_.refs_6_, f32[24,32,128]{2,1,0:T(8,128)S(1)} %get-tuple-element.50.refs_2_.refs_7_, f32[64,256]{1,0:T(8,128)S(1)} %get-tuple-element.62.refs_3_.refs_2_.refs_0_), custom_call_target="tpu_custom_call" | custom-call | tf_op jit(solution)/shard_map/own/pallas_call | solution.py:719
  30.7 1.0 %order.3 = (f32[2,32,128]{2,1,0:T(8,128)S(1)}, f32[24,32,128]{2,1,0:T(8,128)S(1)}, f32[8,256]{1,0:T(8,128)S(1)}) custom-call(s32[8,4096]{1,0:T(8,128)S(1)} %get-tuple-element.65.refs_0_, s32[8,128]{1,0:T(8,128)S(1)} %get-tuple-element.66.refs_1_, f32[64,256]{1,0:T(8,128)S(1)} %get-tuple-element.62.refs_3_.refs_2_.refs_0_), custom_call_target="tpu_custom_call" | custom-call | tf_op jit(solution)/shard_map/order/pallas_call | solution.py:722
  31.8 0.6 collective-permute-done.8.refs_2_
  32.3 0.2 faces_far.2
  32.6 1.3 %place.2.refs_0_.refs_3_ = f32[64,4096]{1,0:T(8,128)S(1)} custom-call(f32[64,2304]{1,0:T(8,128)S(1)} %own.4.refs_3_.refs_0_, f32[64,1792]{1,0:T(8,128)S(1)} %own.5.refs_6_.refs_1_, f32[192,128]{1,0:T(8,128)S(1)} %collective-permute-done.7.refs_1_.refs_2_, f32[192,128]{1,0:T(8,128)S(1)} %collective-permute-done.6.refs_1_.refs_3_, ...), custom_call_target="tpu_custom_call" | custom-call | tf_op jit(solution)/shard_map/place/pallas_call | solution.py:739
  33.9 0.1 rim.2
  34.1 1.1 %collective-permute-start.11 = (f32[64,128]{1,0:T(8,128)S(1)}, f32[64,128]{1,0:T(8,128)S(1)}, u32[]{:S(2)}, u32[]{:S(2)}) collective-permute-start(f32[64,128]{1,0:T(8,128)S(1)} %get-tuple-element.74), channel_id=1, source_target_pairs={{0,1},{1,0},{2,3},{3,2},{4,5},{5,4},{6,7},{7,6},{8,9},{9,8},{10,11... | collective-permute-start | bytes 98312 | tf_op jit(solution)/shard_map/ppermute | solution.py:58
  35.2 2.2 %collective-permute-start.10 = (f32[64,128]{1,0:T(8,128)S(1)}, f32[64,128]{1,0:T(8,128)S(1)}, u32[]{:S(2)}, u32[]{:S(2)}) collective-permute-start(f32[64,128]{1,0:T(8,128)S(1)} %get-tuple-element.73), channel_id=1, source_target_pairs={{0,15},{1,2},{2,1},{3,4},{4,3},{5,6},{6,5},{7,8},{8,7},{9,10},{10,... | collective-permute-start | bytes 98312 | tf_op jit(solution)/shard_map/ppermute | solution.py:54
  37.4 1.2 %between.1 = (f32[64,4096]{1,0:T(8,128)S(1)}, f32[6,64,128]{2,1,0:T(8,128)S(1)}, s32[8,128]{1,0:T(8,128)S(1)}, f32[4,8,128]{2,1,0:T(8,128)S(1)}) custom-call(f32[64,4096]{1,0:T(8,128)S(1)} %place.2.refs_0_.refs_3_, f32[64,128]{1,0:T(8,128)S(1)} %get-tuple-element.68.refs_9_.refs_1_, f32[64,128]{1,0:T(8,128)S(1)} %collective-permute-done.9.refs_2_, ...), custom_call_target="tpu_custom_call" | custom-call | tf_op jit(solution)/shard_map/between/pallas_call | solution.py:748
  38.6 0.3 late_far.1
  38.9 3.3 %collective-permute-start.12 = (f32[192,128]{1,0:T(8,128)S(1)}, f32[192,128]{1,0:T(8,128)S(1)}, u32[]{:S(2)}, u32[]{:S(2)}) collective-permute-start(f32[192,128]{1,0:T(8,128)S(1)} %late_far.1), channel_id=1, source_target_pairs={{0,15},{1,2},{2,1},{3,4},{4,3},{5,6},{6,5},{7,8},{8,7},{9,10},{10,... | collective-permute-start | bytes 294920 | tf_op jit(solution)/shard_map/ppermute | solution.py:54
  42.1 0.3 collective-permute-done.10.refs_1_.refs_3_
  42.4 0.3 late_near.1
  42.8 0.4 finish.1.refs_0_
  43.2 0.4 own_faces.3.refs_5_.refs_0_
  43.6 2.5 %own.6.refs_3_.refs_0_ = f32[64,2048]{1,0:T(8,128)S(1)} custom-call(bf16[1024,512]{1,0:T(8,128)(2,1)S(1)} %finish.1.refs_0_, f32[2,32,128]{2,1,0:T(8,128)S(1)} %get-tuple-element.75.refs_1_.refs_6_, f32[24,32,128]{2,1,0:T(8,128)S(1)} %get-tuple-element.76.refs_2_.refs_7_), custom_call_target="tpu_custom_call" | custom-call | tf_op jit(solution)/shard_map/own/pallas_call | solution.py:709
  46.2 0.5 reply_x.3.refs_2_
  46.7 0.5 collective-permute-done.12.refs_0_
  47.2 0.2 fix.1.refs_0_.refs_2_.refs_4_
  47.6 1.9 %collective-permute-start.15 = (f32[192,128]{1,0:T(8,128)S(1)}, f32[192,128]{1,0:T(8,128)S(1)}, u32[]{:S(2)}, u32[]{:S(2)}) collective-permute-start(f32[192,128]{1,0:T(8,128)S(1)} %get-tuple-element.84.refs_3_), channel_id=1, source_target_pairs={{0,112},{16,32},{32,16},{48,64},{64,48},{80,96},{96,80},{112,0},{1... | collective-permute-start | bytes 294920 | tf_op jit(solution)/shard_map/ppermute | solution.py:54
  49.5 0.2 faces_near.3
  49.7 1.2 %collective-permute-start.16 = (f32[72,128]{1,0:T(8,128)S(1)}, f32[72,128]{1,0:T(8,128)S(1)}, u32[]{:S(2)}, u32[]{:S(2)}) collective-permute-start(f32[72,128]{1,0:T(8,128)S(1)} %get-tuple-element.85), channel_id=1, source_target_pairs={{0,112},{16,32},{32,16},{48,64},{64,48},{80,96},{96,80},{112,0},{1... | collective-permute-start | bytes 110600 | tf_op jit(solution)/shard_map/ppermute | solution.py:54
  50.9 2.5 %own.7.refs_6_.refs_1_ = f32[64,2048]{1,0:T(8,128)S(1)} custom-call(bf16[1024,512]{1,0:T(8,128)(2,1)S(1)} %finish.1.refs_0_, f32[2,32,128]{2,1,0:T(8,128)S(1)} %get-tuple-element.75.refs_1_.refs_6_, f32[24,32,128]{2,1,0:T(8,128)S(1)} %get-tuple-element.76.refs_2_.refs_7_, f32[64,256]{1,0:T(8,128)S(1)} %get-tuple-element.83.refs_3_.refs_0_), custom_call_target="tpu_custom_call" | custom-call | tf_op jit(solution)/shard_map/own/pallas_call | solution.py:719
  53.4 0.9 %collective-permute-done.16.refs_2_ = f32[72,128]{1,0:T(8,128)S(1)} collective-permute-done((f32[72,128]{1,0:T(8,128)S(1)}, f32[72,128]{1,0:T(8,128)S(1)}, u32[]{:S(2)}, u32[]{:S(2)}) %collective-permute-start.16) | collective-permute-done | bytes 36896 | tf_op jit(solution)/shard_map/ppermute | solution.py:54
  54.4 0.2 faces_far.3
  54.7 1.2 %collective-permute-done.17.refs_2_.x_second = f32[64,128]{1,0:T(8,128)S(1)} collective-permute-done((f32[64,128]{1,0:T(8,128)S(1)}, f32[64,128]{1,0:T(8,128)S(1)}, u32[]{:S(2)}, u32[]{:S(2)}) %collective-permute-start.17) | collective-permute-done | bytes 32800 | tf_op jit(solution)/shard_map/ppermute | solution.py:58
  56.0 3.0 %collective-permute-start.18 = (f32[64,128]{1,0:T(8,128)S(1)}, f32[64,128]{1,0:T(8,128)S(1)}, u32[]{:S(2)}, u32[]{:S(2)}) collective-permute-start(f32[64,128]{1,0:T(8,128)S(1)} %get-tuple-element.91), channel_id=1, source_target_pairs={{0,15},{1,2},{2,1},{3,4},{4,3},{5,6},{6,5},{7,8},{8,7},{9,10},{10,... | collective-permute-start | bytes 98312 | tf_op jit(solution)/shard_map/ppermute | solution.py:54
  59.0 1.3 %place.3.weighted = f32[64,4096]{1,0:T(8,128)S(1)} custom-call(f32[64,2048]{1,0:T(8,128)S(1)} %own.6.refs_3_.refs_0_, f32[64,2048]{1,0:T(8,128)S(1)} %own.7.refs_6_.refs_1_, f32[192,128]{1,0:T(8,128)S(1)} %collective-permute-done.15.refs_1_.refs_2_, f32[192,128]{1,0:T(8,128)S(1)} %collective-permute-done.14.refs_1_.refs_3_, ...), custom_call_target="tpu_custom_call" | custom-call | tf_op jit(solution)/shard_map/place/pallas_call | solution.py:745
  60.3 1.1 %inner.1 = (f32[64,2048]{1,0:T(8,128)S(1)}, f32[64,16,256]{2,1,0:T(8,128)}) custom-call(f32[64,4096]{1,0:T(8,128)S(1)} %place.3.weighted, f32[64,128]{1,0:T(8,128)S(1)} %get-tuple-element.87.refs_1_.x_first, f32[64,128]{1,0:T(8,128)S(1)} %collective-permute-done.17.refs_2_.x_second, f32[16,256]{1,0:T(8,128)S(1)} %get-tuple-element.70.refs_3_.inverse), custom_call_target="tpu_custom_call" | custom-call | tf_op jit(solution)/shard_map/inner/pallas_call | solution.py:771
  61.4 2.0 %collective-permute-done.18.y_first = f32[64,128]{1,0:T(8,128)S(1)} collective-permute-done((f32[64,128]{1,0:T(8,128)S(1)}, f32[64,128]{1,0:T(8,128)S(1)}, u32[]{:S(2)}, u32[]{:S(2)}) %collective-permute-start.18) | collective-permute-done | bytes 32800 | tf_op jit(solution)/shard_map/ppermute | solution.py:54
  63.4 1.0 %last.1 = f32[64,16,256]{2,1,0:T(8,128)} custom-call(f32[64,2048]{1,0:T(8,128)S(1)} %get-tuple-element.90.part, f32[64,128]{1,0:T(8,128)S(1)} %collective-permute-done.18.y_first, f32[64,128]{1,0:T(8,128)S(1)} %collective-permute-done.19.y_second, f32[8,128]{1,0:T(8,128)S(1)} %get-tuple-element.60.refs_4_.refs_3_.refs_5_.scale, ...), custom_call_target="tpu_custom_call", output_to_operand_aliasing={{}: (4, {})} | custom-call | tf_op jit(solution)/shard_map/last/pallas_call | solution.py:780
  (26 shorter events, 0.8 us)
Async XLA Ops:
  1.2 4.4 %collective-permute-start = (f32[24,128]{1,0:T(8,128)S(1)}, f32[24,128]{1,0:T(8,128)S(1)}, u32[]{:S(2)}, u32[]{:S(2)}) collective-permute-start(f32[24,128]{1,0:T(8,128)S(1)} %get-tuple-element.52), channel_id=1, source_target_pairs={{0,112},{16,32},{32,16},{48,64},{64,48},{80,96},{96,80},{112,0},{1... | collective-permute-start | bytes 36872 | tf_op jit(solution)/shard_map/ppermute | solution.py:54
  3.8 1.8 %collective-permute-start.1 = (f32[24,128]{1,0:T(8,128)S(1)}, f32[24,128]{1,0:T(8,128)S(1)}, u32[]{:S(2)}, u32[]{:S(2)}) collective-permute-start(f32[24,128]{1,0:T(8,128)S(1)} %get-tuple-element.53), channel_id=1, source_target_pairs={{0,16},{16,0},{32,48},{48,32},{64,80},{80,64},{96,112},{112,96},{1... | collective-permute-start | bytes 36872 | tf_op jit(solution)/shard_map/ppermute | solution.py:58
  5.7 9.8 %collective-permute-start.2 = (f32[24,128]{1,0:T(8,128)S(1)}, f32[24,128]{1,0:T(8,128)S(1)}, u32[]{:S(2)}, u32[]{:S(2)}) collective-permute-start(f32[24,128]{1,0:T(8,128)S(1)} %get-tuple-element.56), channel_id=1, source_target_pairs={{0,15},{1,2},{2,1},{3,4},{4,3},{5,6},{6,5},{7,8},{8,7},{9,10},{10,... | collective-permute-start | bytes 36872 | tf_op jit(solution)/shard_map/ppermute | solution.py:54
  12.0 3.7 %collective-permute-start.3 = (f32[24,128]{1,0:T(8,128)S(1)}, f32[24,128]{1,0:T(8,128)S(1)}, u32[]{:S(2)}, u32[]{:S(2)}) collective-permute-start(f32[24,128]{1,0:T(8,128)S(1)} %get-tuple-element.57), channel_id=1, source_target_pairs={{0,1},{1,0},{2,3},{3,2},{4,5},{5,4},{6,7},{7,6},{8,9},{9,8},{10,11... | collective-permute-start | bytes 36872 | tf_op jit(solution)/shard_map/ppermute | solution.py:58
  16.7 8.0 %collective-permute-start.4 = (f32[192,128]{1,0:T(8,128)S(1)}, f32[192,128]{1,0:T(8,128)S(1)}, u32[]{:S(2)}, u32[]{:S(2)}) collective-permute-start(f32[192,128]{1,0:T(8,128)S(1)} %get-tuple-element.58), channel_id=1, source_target_pairs={{0,15},{1,2},{2,1},{3,4},{4,3},{5,6},{6,5},{7,8},{8,7},{9,10},{10,... | collective-permute-start | bytes 294920 | tf_op jit(solution)/shard_map/ppermute | solution.py:54
  20.1 4.6 %collective-permute-start.5 = (f32[192,128]{1,0:T(8,128)S(1)}, f32[192,128]{1,0:T(8,128)S(1)}, u32[]{:S(2)}, u32[]{:S(2)}) collective-permute-start(f32[192,128]{1,0:T(8,128)S(1)} %get-tuple-element.59), channel_id=1, source_target_pairs={{0,1},{1,0},{2,3},{3,2},{4,5},{5,4},{6,7},{7,6},{8,9},{9,8},{10,11... | collective-permute-start | bytes 294920 | tf_op jit(solution)/shard_map/ppermute | solution.py:58
  20.6 3.0 %copy-start = (f32[16,256]{1,0:T(8,128)S(1)}, f32[16,256]{1,0:T(8,128)}, u32[]{:S(2)}) copy-start(f32[16,256]{1,0:T(8,128)} %refs_8_.3) | copy-start | bytes 49156
  24.8 2.6 %collective-permute-start.6 = (f32[192,128]{1,0:T(8,128)S(1)}, f32[192,128]{1,0:T(8,128)S(1)}, u32[]{:S(2)}, u32[]{:S(2)}) collective-permute-start(f32[192,128]{1,0:T(8,128)S(1)} %get-tuple-element.61), channel_id=1, source_target_pairs={{0,16},{16,0},{32,48},{48,32},{64,80},{80,64},{96,112},{112,96},{1... | collective-permute-start | bytes 294920 | tf_op jit(solution)/shard_map/ppermute | solution.py:58
  24.9 6.9 %collective-permute-start.7 = (f32[192,128]{1,0:T(8,128)S(1)}, f32[192,128]{1,0:T(8,128)S(1)}, u32[]{:S(2)}, u32[]{:S(2)}) collective-permute-start(f32[192,128]{1,0:T(8,128)S(1)} %get-tuple-element.63.refs_3_), channel_id=1, source_target_pairs={{0,112},{16,32},{32,16},{48,64},{64,48},{80,96},{96,80},{112,0},{1... | collective-permute-start | bytes 294920 | tf_op jit(solution)/shard_map/ppermute | solution.py:54
  27.6 4.7 %collective-permute-start.8 = (f32[72,128]{1,0:T(8,128)S(1)}, f32[72,128]{1,0:T(8,128)S(1)}, u32[]{:S(2)}, u32[]{:S(2)}) collective-permute-start(f32[72,128]{1,0:T(8,128)S(1)} %get-tuple-element.64), channel_id=1, source_target_pairs={{0,112},{16,32},{32,16},{48,64},{64,48},{80,96},{96,80},{112,0},{1... | collective-permute-start | bytes 110600 | tf_op jit(solution)/shard_map/ppermute | solution.py:54
  32.5 1.4 %collective-permute-start.9 = (f32[64,128]{1,0:T(8,128)S(1)}, f32[64,128]{1,0:T(8,128)S(1)}, u32[]{:S(2)}, u32[]{:S(2)}) collective-permute-start(f32[64,128]{1,0:T(8,128)S(1)} %get-tuple-element.69), channel_id=1, source_target_pairs={{0,16},{16,0},{32,48},{48,32},{64,80},{80,64},{96,112},{112,96},{1... | collective-permute-start | bytes 98312 | tf_op jit(solution)/shard_map/ppermute | solution.py:58
  34.1 4.5 %collective-permute-start.11 = (f32[64,128]{1,0:T(8,128)S(1)}, f32[64,128]{1,0:T(8,128)S(1)}, u32[]{:S(2)}, u32[]{:S(2)}) collective-permute-start(f32[64,128]{1,0:T(8,128)S(1)} %get-tuple-element.74), channel_id=1, source_target_pairs={{0,1},{1,0},{2,3},{3,2},{4,5},{5,4},{6,7},{7,6},{8,9},{9,8},{10,11... | collective-permute-start | bytes 98312 | tf_op jit(solution)/shard_map/ppermute | solution.py:58
  35.2 7.2 %collective-permute-start.10 = (f32[64,128]{1,0:T(8,128)S(1)}, f32[64,128]{1,0:T(8,128)S(1)}, u32[]{:S(2)}, u32[]{:S(2)}) collective-permute-start(f32[64,128]{1,0:T(8,128)S(1)} %get-tuple-element.73), channel_id=1, source_target_pairs={{0,15},{1,2},{2,1},{3,4},{4,3},{5,6},{6,5},{7,8},{8,7},{9,10},{10,... | collective-permute-start | bytes 98312 | tf_op jit(solution)/shard_map/ppermute | solution.py:54
  38.9 8.3 %collective-permute-start.12 = (f32[192,128]{1,0:T(8,128)S(1)}, f32[192,128]{1,0:T(8,128)S(1)}, u32[]{:S(2)}, u32[]{:S(2)}) collective-permute-start(f32[192,128]{1,0:T(8,128)S(1)} %late_far.1), channel_id=1, source_target_pairs={{0,15},{1,2},{2,1},{3,4},{4,3},{5,6},{6,5},{7,8},{8,7},{9,10},{10,... | collective-permute-start | bytes 294920 | tf_op jit(solution)/shard_map/ppermute | solution.py:54
  42.7 4.7 %collective-permute-start.13 = (f32[192,128]{1,0:T(8,128)S(1)}, f32[192,128]{1,0:T(8,128)S(1)}, u32[]{:S(2)}, u32[]{:S(2)}) collective-permute-start(f32[192,128]{1,0:T(8,128)S(1)} %late_near.1), channel_id=1, source_target_pairs={{0,1},{1,0},{2,3},{3,2},{4,5},{5,4},{6,7},{7,6},{8,9},{9,8},{10,11... | collective-permute-start | bytes 294920 | tf_op jit(solution)/shard_map/ppermute | solution.py:58
  47.5 2.0 %collective-permute-start.14 = (f32[192,128]{1,0:T(8,128)S(1)}, f32[192,128]{1,0:T(8,128)S(1)}, u32[]{:S(2)}, u32[]{:S(2)}) collective-permute-start(f32[192,128]{1,0:T(8,128)S(1)} %get-tuple-element.82), channel_id=1, source_target_pairs={{0,16},{16,0},{32,48},{48,32},{64,80},{80,64},{96,112},{112,96},{1... | collective-permute-start | bytes 294920 | tf_op jit(solution)/shard_map/ppermute | solution.py:58
  47.6 5.9 %collective-permute-start.15 = (f32[192,128]{1,0:T(8,128)S(1)}, f32[192,128]{1,0:T(8,128)S(1)}, u32[]{:S(2)}, u32[]{:S(2)}) collective-permute-start(f32[192,128]{1,0:T(8,128)S(1)} %get-tuple-element.84.refs_3_), channel_id=1, source_target_pairs={{0,112},{16,32},{32,16},{48,64},{64,48},{80,96},{96,80},{112,0},{1... | collective-permute-start | bytes 294920 | tf_op jit(solution)/shard_map/ppermute | solution.py:54
  49.7 4.7 %collective-permute-start.16 = (f32[72,128]{1,0:T(8,128)S(1)}, f32[72,128]{1,0:T(8,128)S(1)}, u32[]{:S(2)}, u32[]{:S(2)}) collective-permute-start(f32[72,128]{1,0:T(8,128)S(1)} %get-tuple-element.85), channel_id=1, source_target_pairs={{0,112},{16,32},{32,16},{48,64},{64,48},{80,96},{96,80},{112,0},{1... | collective-permute-start | bytes 110600 | tf_op jit(solution)/shard_map/ppermute | solution.py:54
  54.6 1.3 %collective-permute-start.17 = (f32[64,128]{1,0:T(8,128)S(1)}, f32[64,128]{1,0:T(8,128)S(1)}, u32[]{:S(2)}, u32[]{:S(2)}) collective-permute-start(f32[64,128]{1,0:T(8,128)S(1)} %get-tuple-element.88), channel_id=1, source_target_pairs={{0,16},{16,0},{32,48},{48,32},{64,80},{80,64},{96,112},{112,96},{1... | collective-permute-start | bytes 98312 | tf_op jit(solution)/shard_map/ppermute | solution.py:58
  56.0 7.3 %collective-permute-start.18 = (f32[64,128]{1,0:T(8,128)S(1)}, f32[64,128]{1,0:T(8,128)S(1)}, u32[]{:S(2)}, u32[]{:S(2)}) collective-permute-start(f32[64,128]{1,0:T(8,128)S(1)} %get-tuple-element.91), channel_id=1, source_target_pairs={{0,15},{1,2},{2,1},{3,4},{4,3},{5,6},{6,5},{7,8},{8,7},{9,10},{10,... | collective-permute-start | bytes 98312 | tf_op jit(solution)/shard_map/ppermute | solution.py:54
  59.0 4.4 %collective-permute-start.19 = (f32[64,128]{1,0:T(8,128)S(1)}, f32[64,128]{1,0:T(8,128)S(1)}, u32[]{:S(2)}, u32[]{:S(2)}) collective-permute-start(f32[64,128]{1,0:T(8,128)S(1)} %get-tuple-element.89.refs_9_), channel_id=1, source_target_pairs={{0,1},{1,0},{2,3},{3,2},{4,5},{5,4},{6,7},{7,6},{8,9},{9,8},{10,11... | collective-permute-start | bytes 98312 | tf_op jit(solution)/shard_map/ppermute | solution.py:58

commit v8 on v6

--- a/solution.py
+++ b/solution.py
@@ -14,7 +14,7 @@
 NODES = 16
 POINTS = 4096
 TILES = POINTS // 128
-PIECES = (((0, 10), (10, 16)), ((0, 7), (7, 16)))
+PIECES = (((0, 10), (10, 16)), ((0, 9), (9, 16)))
 GLL_NODES = (-1.0, -0.4472135954999579, 0.4472135954999579, 1.0)
 REMOTE = (0, 1, 2, 3, 5, 6, 7, 8)
 BF16 = jnp.bfloat16

time: 64.8 us -> 64.8 us (level)
    pallas_call x2, Pallas kernels: 4.96 us -> 4.05 us  [per_device(): own_b = interpolate(s, 1, after=1)(table, picks, factors, partial)]
    pallas_call x2, Pallas kernels: 5.14 us -> 6.04 us  [per_device(): own_a = interpolate(s, 0)(table, picks, factors)]
  transfers between devices with their start and end apart: 20 -> 20, of which waited for: 10 -> 9; matrix products, arithmetic and copies ran while one was open for 0% -> 0% of each run, Pallas kernels for 36% -> 36%
where the time goes in v8:
time: 64.8 us; the launch traced here: 64.5 us
  starting transfers between devices  29.4 us (45%)
  Pallas kernels  27 us (42%)
  waiting for transfers between devices  7.61 us (12%)
    ppermute x10, starting transfers between devices, swap_far(): return lax.ppermute(block, axis, pairs)  27.8 us
    ppermute x10, waiting for transfers between devices, swap_far(): return lax.ppermute(block, axis, pairs)  6.08 us
    pallas_call x2, Pallas kernels, per_device(): own_a = interpolate(s, 0)(table, picks, factors)  6.04 us
    pallas_call x2, Pallas kernels, per_device(): own_b = interpolate(s, 1, after=1)(table, picks, factors, partial)  4.05 us
    pallas_call x1, Pallas kernels, per_device(): call(order_body, requests + [shape((8, POINTS), jnp.int32), shape((8, 128...  1.91 us
    ppermute x10, starting transfers between devices, swap_near(): lax.ppermute(block, axis, [(i, i ^ 1) for i in range(lax.axis_size(axis))])  1.64 us
    pallas_call x1, Pallas kernels, per_device(): call(table_body, table_shape, 'table', hbm=(0,), count=1, scratch=[pltpu....  1.54 us
    ppermute x10, waiting for transfers between devices, swap_near(): lax.ppermute(block, axis, [(i, i ^ 1) for i in range(lax.axis_size(axis))])  1.52 us
  transfers between devices with their start and end apart: 20, of which 9 were waited for; matrix products, arithmetic and copies ran while one was open for 0% of the time, Pallas kernels for 36%

profile of v8, /device:TPU:0, one launch (start us, length us, event | category | flops | bytes accessed | tf_op | source)
XLA Modules:
  0.0 64.5 jit_solution(9680315990481351148)
XLA Ops:
  0.0 1.2 %asks.1 = (f32[24,128]{1,0:T(8,128)S(1)}, f32[24,128]{1,0:T(8,128)S(1)}, f32[24,128]{1,0:T(8,128)S(1)}, f32[8,256]{1,0:T(8,128)S(1)}) custom-call(s32[2,1,10]{2,1,0:T(1,128)} %refs_0_.6, s32[2,4096]{1,0:T(2,128)} %refs_1_.3, s32[2,2,4096]{2,1,0:T(2,128)} %refs_2_.3, f32[16,256]{1,0:T(8,128)} %refs_8_.3), custom_call_target="tpu_custom_call" | custom-call | tf_op jit(solution)/shard_map/asks/pallas_call | solution.py:645
  1.2 2.6 %collective-permute-start = (f32[24,128]{1,0:T(8,128)S(1)}, f32[24,128]{1,0:T(8,128)S(1)}, u32[]{:S(2)}, u32[]{:S(2)}) collective-permute-start(f32[24,128]{1,0:T(8,128)S(1)} %get-tuple-element.52), channel_id=1, source_target_pairs={{0,112},{16,32},{32,16},{48,64},{64,48},{80,96},{96,80},{112,0},{1... | collective-permute-start | bytes 36872 | tf_op jit(solution)/shard_map/ppermute | solution.py:54
  3.8 1.8 %collective-permute-done.refs_0_.refs_1_ = f32[24,128]{1,0:T(8,128)S(1)} collective-permute-done((f32[24,128]{1,0:T(8,128)S(1)}, f32[24,128]{1,0:T(8,128)S(1)}, u32[]{:S(2)}, u32[]{:S(2)}) %collective-permute-start) | collective-permute-done | bytes 12320 | tf_op jit(solution)/shard_map/ppermute | solution.py:54
  5.7 6.4 %collective-permute-start.2 = (f32[24,128]{1,0:T(8,128)S(1)}, f32[24,128]{1,0:T(8,128)S(1)}, u32[]{:S(2)}, u32[]{:S(2)}) collective-permute-start(f32[24,128]{1,0:T(8,128)S(1)} %get-tuple-element.56), channel_id=1, source_target_pairs={{0,15},{1,2},{2,1},{3,4},{4,3},{5,6},{6,5},{7,8},{8,7},{9,10},{10,... | collective-permute-start | bytes 36872 | tf_op jit(solution)/shard_map/ppermute | solution.py:54
  12.0 1.9 %order.2 = (f32[2,32,128]{2,1,0:T(8,128)S(1)}, f32[24,32,128]{2,1,0:T(8,128)S(1)}, f32[8,256]{1,0:T(8,128)S(1)}, s32[8,4096]{1,0:T(8,128)S(1)}, s32[8,128]{1,0:T(8,128)S(1)}) custom-call(s32[2,1,10]{2,1,0:T(1,128)} %refs_0_.6, s32[2,1,4096]{2,1,0:T(1,128)} %refs_1_.2, s32[2,4096]{1,0:T(2,128)} %refs_1_.3, s32[2,2,4096]{2,1,0:T(2,128)} %refs_2_.3), custom_call_target="tpu_custom_call" | custom-call | tf_op jit(solution)/shard_map/order/pallas_call | solution.py:661
  13.9 1.5 %table.1.refs_0_ = bf16[1024,512]{1,0:T(8,128)(2,1)S(1)} custom-call(f32[64,16,256]{2,1,0:T(8,128)} %refs_0_.4), custom_call_target="tpu_custom_call" | custom-call | tf_op jit(solution)/shard_map/table/pallas_call | solution.py:686
  15.5 0.2 collective-permute-done.3.refs_2_.refs_4_.refs_5_
  15.7 1.0 %reply_y.1 = (f32[192,128]{1,0:T(8,128)S(1)}, f32[192,128]{1,0:T(8,128)S(1)}) custom-call(bf16[1024,512]{1,0:T(8,128)(2,1)S(1)} %table.1.refs_0_, f32[24,128]{1,0:T(8,128)S(1)} %collective-permute-done.2.refs_1_.refs_3_.refs_4_, f32[24,128]{1,0:T(8,128)S(1)} %collective-permute-done.3.refs_2_.refs_4_.refs_5_, ...), custom_call_target="tpu_custom_call" | custom-call | tf_op jit(solution)/shard_map/reply_y/pallas_call | solution.py:694
  16.7 3.4 %collective-permute-start.4 = (f32[192,128]{1,0:T(8,128)S(1)}, f32[192,128]{1,0:T(8,128)S(1)}, u32[]{:S(2)}, u32[]{:S(2)}) collective-permute-start(f32[192,128]{1,0:T(8,128)S(1)} %get-tuple-element.58), channel_id=1, source_target_pairs={{0,15},{1,2},{2,1},{3,4},{4,3},{5,6},{6,5},{7,8},{8,7},{9,10},{10,... | collective-permute-start | bytes 294920 | tf_op jit(solution)/shard_map/ppermute | solution.py:54
  20.1 0.4 own_faces.2.refs_5_.refs_0_
  20.6 3.1 %own.4.refs_3_.refs_0_ = f32[64,2560]{1,0:T(8,128)S(1)} custom-call(bf16[1024,512]{1,0:T(8,128)(2,1)S(1)} %table.1.refs_0_, f32[2,32,128]{2,1,0:T(8,128)S(1)} %get-tuple-element.49.refs_1_.refs_6_, f32[24,32,128]{2,1,0:T(8,128)S(1)} %get-tuple-element.50.refs_2_.refs_7_), custom_call_target="tpu_custom_call" | custom-call | tf_op jit(solution)/shard_map/own/pallas_call | solution.py:709
  23.7 0.3 scale.1
  23.9 0.5 reply_x.2.refs_2_
  24.4 0.3 collective-permute-done.4.refs_0_.refs_2_.refs_4_
  24.9 2.5 %collective-permute-start.7 = (f32[192,128]{1,0:T(8,128)S(1)}, f32[192,128]{1,0:T(8,128)S(1)}, u32[]{:S(2)}, u32[]{:S(2)}) collective-permute-start(f32[192,128]{1,0:T(8,128)S(1)} %get-tuple-element.63.refs_3_), channel_id=1, source_target_pairs={{0,112},{16,32},{32,16},{48,64},{64,48},{80,96},{96,80},{112,0},{1... | collective-permute-start | bytes 294920 | tf_op jit(solution)/shard_map/ppermute | solution.py:54
  27.4 0.2 faces_near.2
  27.6 1.0 %collective-permute-start.8 = (f32[72,128]{1,0:T(8,128)S(1)}, f32[72,128]{1,0:T(8,128)S(1)}, u32[]{:S(2)}, u32[]{:S(2)}) collective-permute-start(f32[72,128]{1,0:T(8,128)S(1)} %get-tuple-element.64), channel_id=1, source_target_pairs={{0,112},{16,32},{32,16},{48,64},{64,48},{80,96},{96,80},{112,0},{1... | collective-permute-start | bytes 110600 | tf_op jit(solution)/shard_map/ppermute | solution.py:54
  28.7 2.0 %own.5.refs_6_.refs_1_ = f32[64,1536]{1,0:T(8,128)S(1)} custom-call(bf16[1024,512]{1,0:T(8,128)(2,1)S(1)} %table.1.refs_0_, f32[2,32,128]{2,1,0:T(8,128)S(1)} %get-tuple-element.49.refs_1_.refs_6_, f32[24,32,128]{2,1,0:T(8,128)S(1)} %get-tuple-element.50.refs_2_.refs_7_, f32[64,256]{1,0:T(8,128)S(1)} %get-tuple-element.62.refs_3_.refs_2_.refs_0_), custom_call_target="tpu_custom_call" | custom-call | tf_op jit(solution)/shard_map/own/pallas_call | solution.py:719
  30.6 1.0 %order.3 = (f32[2,32,128]{2,1,0:T(8,128)S(1)}, f32[24,32,128]{2,1,0:T(8,128)S(1)}, f32[8,256]{1,0:T(8,128)S(1)}) custom-call(s32[8,4096]{1,0:T(8,128)S(1)} %get-tuple-element.65.refs_0_, s32[8,128]{1,0:T(8,128)S(1)} %get-tuple-element.66.refs_1_, f32[64,256]{1,0:T(8,128)S(1)} %get-tuple-element.62.refs_3_.refs_2_.refs_0_), custom_call_target="tpu_custom_call" | custom-call | tf_op jit(solution)/shard_map/order/pallas_call | solution.py:722
  31.7 0.7 %collective-permute-done.8.refs_2_ = f32[72,128]{1,0:T(8,128)S(1)} collective-permute-done((f32[72,128]{1,0:T(8,128)S(1)}, f32[72,128]{1,0:T(8,128)S(1)}, u32[]{:S(2)}, u32[]{:S(2)}) %collective-permute-start.8) | collective-permute-done | bytes 36896 | tf_op jit(solution)/shard_map/ppermute | solution.py:54
  32.3 0.2 faces_far.2
  32.6 1.3 %place.2.refs_0_.refs_3_ = f32[64,4096]{1,0:T(8,128)S(1)} custom-call(f32[64,2560]{1,0:T(8,128)S(1)} %own.4.refs_3_.refs_0_, f32[64,1536]{1,0:T(8,128)S(1)} %own.5.refs_6_.refs_1_, f32[192,128]{1,0:T(8,128)S(1)} %collective-permute-done.7.refs_1_.refs_2_, f32[192,128]{1,0:T(8,128)S(1)} %collective-permute-done.6.refs_1_.refs_3_, ...), custom_call_target="tpu_custom_call" | custom-call | tf_op jit(solution)/shard_map/place/pallas_call | solution.py:739
  33.9 0.1 rim.2
  34.1 1.2 %collective-permute-start.11 = (f32[64,128]{1,0:T(8,128)S(1)}, f32[64,128]{1,0:T(8,128)S(1)}, u32[]{:S(2)}, u32[]{:S(2)}) collective-permute-start(f32[64,128]{1,0:T(8,128)S(1)} %get-tuple-element.74), channel_id=1, source_target_pairs={{0,1},{1,0},{2,3},{3,2},{4,5},{5,4},{6,7},{7,6},{8,9},{9,8},{10,11... | collective-permute-start | bytes 98312 | tf_op jit(solution)/shard_map/ppermute | solution.py:58
  35.3 2.0 %collective-permute-start.10 = (f32[64,128]{1,0:T(8,128)S(1)}, f32[64,128]{1,0:T(8,128)S(1)}, u32[]{:S(2)}, u32[]{:S(2)}) collective-permute-start(f32[64,128]{1,0:T(8,128)S(1)} %get-tuple-element.73), channel_id=1, source_target_pairs={{0,15},{1,2},{2,1},{3,4},{4,3},{5,6},{6,5},{7,8},{8,7},{9,10},{10,... | collective-permute-start | bytes 98312 | tf_op jit(solution)/shard_map/ppermute | solution.py:54
  37.3 1.2 %between.1 = (f32[64,4096]{1,0:T(8,128)S(1)}, f32[6,64,128]{2,1,0:T(8,128)S(1)}, s32[8,128]{1,0:T(8,128)S(1)}, f32[4,8,128]{2,1,0:T(8,128)S(1)}) custom-call(f32[64,4096]{1,0:T(8,128)S(1)} %place.2.refs_0_.refs_3_, f32[64,128]{1,0:T(8,128)S(1)} %get-tuple-element.68.refs_9_.refs_1_, f32[64,128]{1,0:T(8,128)S(1)} %collective-permute-done.9.refs_2_, ...), custom_call_target="tpu_custom_call" | custom-call | tf_op jit(solution)/shard_map/between/pallas_call | solution.py:748
  38.5 0.3 late_far.1
  38.7 3.6 %collective-permute-start.12 = (f32[192,128]{1,0:T(8,128)S(1)}, f32[192,128]{1,0:T(8,128)S(1)}, u32[]{:S(2)}, u32[]{:S(2)}) collective-permute-start(f32[192,128]{1,0:T(8,128)S(1)} %late_far.1), channel_id=1, source_target_pairs={{0,15},{1,2},{2,1},{3,4},{4,3},{5,6},{6,5},{7,8},{8,7},{9,10},{10,... | collective-permute-start | bytes 294920 | tf_op jit(solution)/shard_map/ppermute | solution.py:54
  42.4 0.1 collective-permute-done.10.refs_1_.refs_3_
  42.5 0.3 late_near.1
  42.9 0.4 finish.1.refs_0_
  43.3 0.4 own_faces.3.refs_5_.refs_0_
  43.7 3.0 %own.6.refs_3_.refs_0_ = f32[64,2304]{1,0:T(8,128)S(1)} custom-call(bf16[1024,512]{1,0:T(8,128)(2,1)S(1)} %finish.1.refs_0_, f32[2,32,128]{2,1,0:T(8,128)S(1)} %get-tuple-element.75.refs_1_.refs_6_, f32[24,32,128]{2,1,0:T(8,128)S(1)} %get-tuple-element.76.refs_2_.refs_7_), custom_call_target="tpu_custom_call" | custom-call | tf_op jit(solution)/shard_map/own/pallas_call | solution.py:709
  46.7 0.5 reply_x.3.refs_2_
  47.2 0.2 fix.1.refs_0_.refs_2_.refs_4_
  47.6 1.8 %collective-permute-start.15 = (f32[192,128]{1,0:T(8,128)S(1)}, f32[192,128]{1,0:T(8,128)S(1)}, u32[]{:S(2)}, u32[]{:S(2)}) collective-permute-start(f32[192,128]{1,0:T(8,128)S(1)} %get-tuple-element.84.refs_3_), channel_id=1, source_target_pairs={{0,112},{16,32},{32,16},{48,64},{64,48},{80,96},{96,80},{112,0},{1... | collective-permute-start | bytes 294920 | tf_op jit(solution)/shard_map/ppermute | solution.py:54
  49.5 0.2 faces_near.3
  49.7 1.3 %collective-permute-start.16 = (f32[72,128]{1,0:T(8,128)S(1)}, f32[72,128]{1,0:T(8,128)S(1)}, u32[]{:S(2)}, u32[]{:S(2)}) collective-permute-start(f32[72,128]{1,0:T(8,128)S(1)} %get-tuple-element.85), channel_id=1, source_target_pairs={{0,112},{16,32},{32,16},{48,64},{64,48},{80,96},{96,80},{112,0},{1... | collective-permute-start | bytes 110600 | tf_op jit(solution)/shard_map/ppermute | solution.py:54
  51.0 2.1 %own.7.refs_6_.refs_1_ = f32[64,1792]{1,0:T(8,128)S(1)} custom-call(bf16[1024,512]{1,0:T(8,128)(2,1)S(1)} %finish.1.refs_0_, f32[2,32,128]{2,1,0:T(8,128)S(1)} %get-tuple-element.75.refs_1_.refs_6_, f32[24,32,128]{2,1,0:T(8,128)S(1)} %get-tuple-element.76.refs_2_.refs_7_, f32[64,256]{1,0:T(8,128)S(1)} %get-tuple-element.83.refs_3_.refs_0_), custom_call_target="tpu_custom_call" | custom-call | tf_op jit(solution)/shard_map/own/pallas_call | solution.py:719
  53.1 1.3 %collective-permute-done.16.refs_2_ = f32[72,128]{1,0:T(8,128)S(1)} collective-permute-done((f32[72,128]{1,0:T(8,128)S(1)}, f32[72,128]{1,0:T(8,128)S(1)}, u32[]{:S(2)}, u32[]{:S(2)}) %collective-permute-start.16) | collective-permute-done | bytes 36896 | tf_op jit(solution)/shard_map/ppermute | solution.py:54
  54.4 0.2 faces_far.3
  54.7 1.2 %collective-permute-done.17.refs_2_.x_second = f32[64,128]{1,0:T(8,128)S(1)} collective-permute-done((f32[64,128]{1,0:T(8,128)S(1)}, f32[64,128]{1,0:T(8,128)S(1)}, u32[]{:S(2)}, u32[]{:S(2)}) %collective-permute-start.17) | collective-permute-done | bytes 32800 | tf_op jit(solution)/shard_map/ppermute | solution.py:58
  55.9 0.1 rim.3
  56.0 3.1 %collective-permute-start.18 = (f32[64,128]{1,0:T(8,128)S(1)}, f32[64,128]{1,0:T(8,128)S(1)}, u32[]{:S(2)}, u32[]{:S(2)}) collective-permute-start(f32[64,128]{1,0:T(8,128)S(1)} %get-tuple-element.91), channel_id=1, source_target_pairs={{0,15},{1,2},{2,1},{3,4},{4,3},{5,6},{6,5},{7,8},{8,7},{9,10},{10,... | collective-permute-start | bytes 98312 | tf_op jit(solution)/shard_map/ppermute | solution.py:54
  59.2 1.3 %place.3.weighted = f32[64,4096]{1,0:T(8,128)S(1)} custom-call(f32[64,2304]{1,0:T(8,128)S(1)} %own.6.refs_3_.refs_0_, f32[64,1792]{1,0:T(8,128)S(1)} %own.7.refs_6_.refs_1_, f32[192,128]{1,0:T(8,128)S(1)} %collective-permute-done.15.refs_1_.refs_2_, f32[192,128]{1,0:T(8,128)S(1)} %collective-permute-done.14.refs_1_.refs_3_, ...), custom_call_target="tpu_custom_call" | custom-call | tf_op jit(solution)/shard_map/place/pallas_call | solution.py:745
  60.5 1.1 %inner.1 = (f32[64,2048]{1,0:T(8,128)S(1)}, f32[64,16,256]{2,1,0:T(8,128)}) custom-call(f32[64,4096]{1,0:T(8,128)S(1)} %place.3.weighted, f32[64,128]{1,0:T(8,128)S(1)} %get-tuple-element.87.refs_1_.x_first, f32[64,128]{1,0:T(8,128)S(1)} %collective-permute-done.17.refs_2_.x_second, f32[16,256]{1,0:T(8,128)S(1)} %get-tuple-element.70.refs_3_.inverse), custom_call_target="tpu_custom_call" | custom-call | tf_op jit(solution)/shard_map/inner/pallas_call | solution.py:771
  61.5 1.8 %collective-permute-done.18.y_first = f32[64,128]{1,0:T(8,128)S(1)} collective-permute-done((f32[64,128]{1,0:T(8,128)S(1)}, f32[64,128]{1,0:T(8,128)S(1)}, u32[]{:S(2)}, u32[]{:S(2)}) %collective-permute-start.18) | collective-permute-done | bytes 32800 | tf_op jit(solution)/shard_map/ppermute | solution.py:54
  63.3 1.0 %last.1 = f32[64,16,256]{2,1,0:T(8,128)} custom-call(f32[64,2048]{1,0:T(8,128)S(1)} %get-tuple-element.90.part, f32[64,128]{1,0:T(8,128)S(1)} %collective-permute-done.18.y_first, f32[64,128]{1,0:T(8,128)S(1)} %collective-permute-done.19.y_second, f32[8,128]{1,0:T(8,128)S(1)} %get-tuple-element.60.refs_4_.refs_3_.refs_5_.scale, ...), custom_call_target="tpu_custom_call", output_to_operand_aliasing={{}: (4, {})} | custom-call | tf_op jit(solution)/shard_map/last/pallas_call | solution.py:780
  (26 shorter events, 0.7 us)
Async XLA Ops:
  1.2 4.4 %collective-permute-start = (f32[24,128]{1,0:T(8,128)S(1)}, f32[24,128]{1,0:T(8,128)S(1)}, u32[]{:S(2)}, u32[]{:S(2)}) collective-permute-start(f32[24,128]{1,0:T(8,128)S(1)} %get-tuple-element.52), channel_id=1, source_target_pairs={{0,112},{16,32},{32,16},{48,64},{64,48},{80,96},{96,80},{112,0},{1... | collective-permute-start | bytes 36872 | tf_op jit(solution)/shard_map/ppermute | solution.py:54
  3.8 1.8 %collective-permute-start.1 = (f32[24,128]{1,0:T(8,128)S(1)}, f32[24,128]{1,0:T(8,128)S(1)}, u32[]{:S(2)}, u32[]{:S(2)}) collective-permute-start(f32[24,128]{1,0:T(8,128)S(1)} %get-tuple-element.53), channel_id=1, source_target_pairs={{0,16},{16,0},{32,48},{48,32},{64,80},{80,64},{96,112},{112,96},{1... | collective-permute-start | bytes 36872 | tf_op jit(solution)/shard_map/ppermute | solution.py:58
  5.7 9.8 %collective-permute-start.2 = (f32[24,128]{1,0:T(8,128)S(1)}, f32[24,128]{1,0:T(8,128)S(1)}, u32[]{:S(2)}, u32[]{:S(2)}) collective-permute-start(f32[24,128]{1,0:T(8,128)S(1)} %get-tuple-element.56), channel_id=1, source_target_pairs={{0,15},{1,2},{2,1},{3,4},{4,3},{5,6},{6,5},{7,8},{8,7},{9,10},{10,... | collective-permute-start | bytes 36872 | tf_op jit(solution)/shard_map/ppermute | solution.py:54
  12.0 3.7 %collective-permute-start.3 = (f32[24,128]{1,0:T(8,128)S(1)}, f32[24,128]{1,0:T(8,128)S(1)}, u32[]{:S(2)}, u32[]{:S(2)}) collective-permute-start(f32[24,128]{1,0:T(8,128)S(1)} %get-tuple-element.57), channel_id=1, source_target_pairs={{0,1},{1,0},{2,3},{3,2},{4,5},{5,4},{6,7},{7,6},{8,9},{9,8},{10,11... | collective-permute-start | bytes 36872 | tf_op jit(solution)/shard_map/ppermute | solution.py:58
  16.7 8.0 %collective-permute-start.4 = (f32[192,128]{1,0:T(8,128)S(1)}, f32[192,128]{1,0:T(8,128)S(1)}, u32[]{:S(2)}, u32[]{:S(2)}) collective-permute-start(f32[192,128]{1,0:T(8,128)S(1)} %get-tuple-element.58), channel_id=1, source_target_pairs={{0,15},{1,2},{2,1},{3,4},{4,3},{5,6},{6,5},{7,8},{8,7},{9,10},{10,... | collective-permute-start | bytes 294920 | tf_op jit(solution)/shard_map/ppermute | solution.py:54
  20.1 4.6 %collective-permute-start.5 = (f32[192,128]{1,0:T(8,128)S(1)}, f32[192,128]{1,0:T(8,128)S(1)}, u32[]{:S(2)}, u32[]{:S(2)}) collective-permute-start(f32[192,128]{1,0:T(8,128)S(1)} %get-tuple-element.59), channel_id=1, source_target_pairs={{0,1},{1,0},{2,3},{3,2},{4,5},{5,4},{6,7},{7,6},{8,9},{9,8},{10,11... | collective-permute-start | bytes 294920 | tf_op jit(solution)/shard_map/ppermute | solution.py:58
  20.6 3.1 %copy-start = (f32[16,256]{1,0:T(8,128)S(1)}, f32[16,256]{1,0:T(8,128)}, u32[]{:S(2)}) copy-start(f32[16,256]{1,0:T(8,128)} %refs_8_.3) | copy-start | bytes 49156
  24.8 2.6 %collective-permute-start.6 = (f32[192,128]{1,0:T(8,128)S(1)}, f32[192,128]{1,0:T(8,128)S(1)}, u32[]{:S(2)}, u32[]{:S(2)}) collective-permute-start(f32[192,128]{1,0:T(8,128)S(1)} %get-tuple-element.61), channel_id=1, source_target_pairs={{0,16},{16,0},{32,48},{48,32},{64,80},{80,64},{96,112},{112,96},{1... | collective-permute-start | bytes 294920 | tf_op jit(solution)/shard_map/ppermute | solution.py:58
  24.9 6.8 %collective-permute-start.7 = (f32[192,128]{1,0:T(8,128)S(1)}, f32[192,128]{1,0:T(8,128)S(1)}, u32[]{:S(2)}, u32[]{:S(2)}) collective-permute-start(f32[192,128]{1,0:T(8,128)S(1)} %get-tuple-element.63.refs_3_), channel_id=1, source_target_pairs={{0,112},{16,32},{32,16},{48,64},{64,48},{80,96},{96,80},{112,0},{1... | collective-permute-start | bytes 294920 | tf_op jit(solution)/shard_map/ppermute | solution.py:54
  27.6 4.7 %collective-permute-start.8 = (f32[72,128]{1,0:T(8,128)S(1)}, f32[72,128]{1,0:T(8,128)S(1)}, u32[]{:S(2)}, u32[]{:S(2)}) collective-permute-start(f32[72,128]{1,0:T(8,128)S(1)} %get-tuple-element.64), channel_id=1, source_target_pairs={{0,112},{16,32},{32,16},{48,64},{64,48},{80,96},{96,80},{112,0},{1... | collective-permute-start | bytes 110600 | tf_op jit(solution)/shard_map/ppermute | solution.py:54
  32.5 1.4 %collective-permute-start.9 = (f32[64,128]{1,0:T(8,128)S(1)}, f32[64,128]{1,0:T(8,128)S(1)}, u32[]{:S(2)}, u32[]{:S(2)}) collective-permute-start(f32[64,128]{1,0:T(8,128)S(1)} %get-tuple-element.69), channel_id=1, source_target_pairs={{0,16},{16,0},{32,48},{48,32},{64,80},{80,64},{96,112},{112,96},{1... | collective-permute-start | bytes 98312 | tf_op jit(solution)/shard_map/ppermute | solution.py:58
  34.1 4.4 %collective-permute-start.11 = (f32[64,128]{1,0:T(8,128)S(1)}, f32[64,128]{1,0:T(8,128)S(1)}, u32[]{:S(2)}, u32[]{:S(2)}) collective-permute-start(f32[64,128]{1,0:T(8,128)S(1)} %get-tuple-element.74), channel_id=1, source_target_pairs={{0,1},{1,0},{2,3},{3,2},{4,5},{5,4},{6,7},{7,6},{8,9},{9,8},{10,11... | collective-permute-start | bytes 98312 | tf_op jit(solution)/shard_map/ppermute | solution.py:58
  35.3 7.2 %collective-permute-start.10 = (f32[64,128]{1,0:T(8,128)S(1)}, f32[64,128]{1,0:T(8,128)S(1)}, u32[]{:S(2)}, u32[]{:S(2)}) collective-permute-start(f32[64,128]{1,0:T(8,128)S(1)} %get-tuple-element.73), channel_id=1, source_target_pairs={{0,15},{1,2},{2,1},{3,4},{4,3},{5,6},{6,5},{7,8},{8,7},{9,10},{10,... | collective-permute-start | bytes 98312 | tf_op jit(solution)/shard_map/ppermute | solution.py:54
  38.7 8.4 %collective-permute-start.12 = (f32[192,128]{1,0:T(8,128)S(1)}, f32[192,128]{1,0:T(8,128)S(1)}, u32[]{:S(2)}, u32[]{:S(2)}) collective-permute-start(f32[192,128]{1,0:T(8,128)S(1)} %late_far.1), channel_id=1, source_target_pairs={{0,15},{1,2},{2,1},{3,4},{4,3},{5,6},{6,5},{7,8},{8,7},{9,10},{10,... | collective-permute-start | bytes 294920 | tf_op jit(solution)/shard_map/ppermute | solution.py:54
  42.8 4.7 %collective-permute-start.13 = (f32[192,128]{1,0:T(8,128)S(1)}, f32[192,128]{1,0:T(8,128)S(1)}, u32[]{:S(2)}, u32[]{:S(2)}) collective-permute-start(f32[192,128]{1,0:T(8,128)S(1)} %late_near.1), channel_id=1, source_target_pairs={{0,1},{1,0},{2,3},{3,2},{4,5},{5,4},{6,7},{7,6},{8,9},{9,8},{10,11... | collective-permute-start | bytes 294920 | tf_op jit(solution)/shard_map/ppermute | solution.py:58
  47.5 1.9 %collective-permute-start.14 = (f32[192,128]{1,0:T(8,128)S(1)}, f32[192,128]{1,0:T(8,128)S(1)}, u32[]{:S(2)}, u32[]{:S(2)}) collective-permute-start(f32[192,128]{1,0:T(8,128)S(1)} %get-tuple-element.82), channel_id=1, source_target_pairs={{0,16},{16,0},{32,48},{48,32},{64,80},{80,64},{96,112},{112,96},{1... | collective-permute-start | bytes 294920 | tf_op jit(solution)/shard_map/ppermute | solution.py:58
  47.6 5.4 %collective-permute-start.15 = (f32[192,128]{1,0:T(8,128)S(1)}, f32[192,128]{1,0:T(8,128)S(1)}, u32[]{:S(2)}, u32[]{:S(2)}) collective-permute-start(f32[192,128]{1,0:T(8,128)S(1)} %get-tuple-element.84.refs_3_), channel_id=1, source_target_pairs={{0,112},{16,32},{32,16},{48,64},{64,48},{80,96},{96,80},{112,0},{1... | collective-permute-start | bytes 294920 | tf_op jit(solution)/shard_map/ppermute | solution.py:54
  49.7 4.7 %collective-permute-start.16 = (f32[72,128]{1,0:T(8,128)S(1)}, f32[72,128]{1,0:T(8,128)S(1)}, u32[]{:S(2)}, u32[]{:S(2)}) collective-permute-start(f32[72,128]{1,0:T(8,128)S(1)} %get-tuple-element.85), channel_id=1, source_target_pairs={{0,112},{16,32},{32,16},{48,64},{64,48},{80,96},{96,80},{112,0},{1... | collective-permute-start | bytes 110600 | tf_op jit(solution)/shard_map/ppermute | solution.py:54
  54.6 1.3 %collective-permute-start.17 = (f32[64,128]{1,0:T(8,128)S(1)}, f32[64,128]{1,0:T(8,128)S(1)}, u32[]{:S(2)}, u32[]{:S(2)}) collective-permute-start(f32[64,128]{1,0:T(8,128)S(1)} %get-tuple-element.88), channel_id=1, source_target_pairs={{0,16},{16,0},{32,48},{48,32},{64,80},{80,64},{96,112},{112,96},{1... | collective-permute-start | bytes 98312 | tf_op jit(solution)/shard_map/ppermute | solution.py:58
  56.0 7.3 %collective-permute-start.18 = (f32[64,128]{1,0:T(8,128)S(1)}, f32[64,128]{1,0:T(8,128)S(1)}, u32[]{:S(2)}, u32[]{:S(2)}) collective-permute-start(f32[64,128]{1,0:T(8,128)S(1)} %get-tuple-element.91), channel_id=1, source_target_pairs={{0,15},{1,2},{2,1},{3,4},{4,3},{5,6},{6,5},{7,8},{8,7},{9,10},{10,... | collective-permute-start | bytes 98312 | tf_op jit(solution)/shard_map/ppermute | solution.py:54
  59.2 4.2 %collective-permute-start.19 = (f32[64,128]{1,0:T(8,128)S(1)}, f32[64,128]{1,0:T(8,128)S(1)}, u32[]{:S(2)}, u32[]{:S(2)}) collective-permute-start(f32[64,128]{1,0:T(8,128)S(1)} %get-tuple-element.89.refs_9_), channel_id=1, source_target_pairs={{0,1},{1,0},{2,3},{3,2},{4,5},{5,4},{6,7},{7,6},{8,9},{9,8},{10,11... | collective-permute-start | bytes 98312 | tf_op jit(solution)/shard_map/ppermute | solution.py:58
